TPU v7x, 32 devices: a whole 2x2x4 slice. The times are simulated.
32 devices in a mesh: parts: 2 (over y), blk: 4 (over x, core), col: 4 (over z).
Axes of the slice: x: 2, y: 2, z: 4, core: 2. Of those that a mesh axis runs over, the one named last changes fastest.
Arguments:
- a_blocks: float32 [8, 4, 6, 128, 128], P(('parts', 'blk')), parts along dimension 0, may hold values from -2 to 2
- a_rows: int32 [8, 4, 6], P(('parts', 'blk')), parts along dimension 0, may hold values from 0 to 2, as said below
- a_cols: int32 [8, 4, 6], P(('parts', 'blk')), parts along dimension 0, may hold values from -1 to 2, as said below
- b_panel: float32 [3072, 1536], P(('parts', 'blk'), 'col'), parts along dimension 0, may hold values from -6 to 6
- pattern: int32 [24, 12], P(('parts', 'blk'), 'col'), parts along dimension 0, may hold values 0 or 1
Outputs:
- step_matrix: float32 [3072, 1536], P(('parts', 'blk'), 'col'), parts along dimension 0
There are 2 independent parts, one for each index of `parts`. A program takes and returns all parts, laid end to end along the dimension named above; each array names one. Nothing has to cross between parts.
Inputs may be any that keep to these rules, and one draw needn't show every extreme that they name: a_rows[r, s, q] and a_cols[r, s, q] name the block of row group r and column group s held in slot q; no pair is named twice in one (r, s). `a_cols`: -1 marks an empty slot; empty slots follow the live ones; each (r, s) has 2 to 6 live slots, and some (r, s) has 6.
All inputs are finite; a program needn't handle non-finite values. No bound on the sum of `pattern` on one device may be relied on, other than what follows from the above.
Results may differ from a plain program's by a relative error of at most 0.000059.
Values sent between devices are 32-bit elements; how exact they have to be, the bound alone decides.
No kernel may reach another device: no remote copies, remote signals or barrier semaphores. Data moves between devices by JAX's collectives and lax.ppermute only.
A program may use at most 64 MiB of HBM per device.

v0:
```python
import jax
import jax.numpy as jnp
from jax import lax
from jax.sharding import PartitionSpec as P

trust_radius = 0.5


def shifted(value, axis, steps):
    count = lax.axis_size(axis)
    pairs = [(source, (source + steps) % count) for source in range(count)]
    return lax.ppermute(value, axis, pairs)


def contribute(running, panel_part, group, blocks, row_ids, col_ids):
    highest = lax.Precision.HIGHEST
    group_blocks = lax.dynamic_index_in_dim(blocks, group, 0, keepdims=False)
    group_rows = lax.dynamic_index_in_dim(row_ids, group, 0, keepdims=False)
    group_cols = lax.dynamic_index_in_dim(col_ids, group, 0, keepdims=False)
    local_ids = jnp.arange(panel_part.shape[0], dtype=jnp.int32)
    col_hot = (group_cols[:, None] == local_ids).astype(jnp.float32)
    row_hot = (group_rows[:, None] == local_ids).astype(jnp.float32)
    chosen = jnp.einsum("qk,kbw->qbw", col_hot, panel_part, precision=highest)
    partial_prod = jnp.einsum("qab,qbw->qaw", group_blocks, chosen, precision=highest)
    return running + jnp.einsum("qi,qaw->iaw", row_hot, partial_prod, precision=highest)


def body(a_blocks, a_rows, a_cols, b_panel, pattern):
    blocks = a_blocks[0]
    row_ids = a_rows[0]
    col_ids = a_cols[0]
    cycle_size = lax.axis_size("blk")
    position = lax.axis_index("blk")
    block_size = blocks.shape[-1]
    row_blocks = b_panel.shape[0] // block_size
    width = b_panel.shape[1]
    col_blocks = width // block_size
    panel = b_panel.reshape(row_blocks, block_size, width)
    running = jnp.zeros((row_blocks, block_size, width), jnp.float32)
    running = contribute(running, panel, position, blocks, row_ids, col_ids)

    def advance(turn, carry):
        running, panel = carry
        panel = shifted(panel, "blk", 1)
        group = (position - turn) % cycle_size
        running = contribute(running, panel, group, blocks, row_ids, col_ids)
        return (running, panel)

    running, panel = lax.fori_loop(1, cycle_size, advance, (running, panel))
    cutoff = pattern.astype(jnp.float32)
    gradient = (
        running.reshape(row_blocks, block_size, col_blocks, block_size) * cutoff[:, None, :, None]
    )
    squares = lax.psum(jnp.sum(gradient * gradient), ("blk", "col"))
    magnitude = jnp.sqrt(squares + 1e-06)
    whole_order = row_blocks * cycle_size * block_size
    factor = jnp.minimum(1.0, trust_radius * whole_order / magnitude)
    return (-gradient * factor).reshape(row_blocks * block_size, width)


def solution(mesh):
    in_specs = (
        P(("parts", "blk"), None, None, None, None),
        P(("parts", "blk"), None, None),
        P(("parts", "blk"), None, None),
        P(("parts", "blk"), "col"),
        P(("parts", "blk"), "col"),
    )
    out_specs = P(("parts", "blk"), "col")
    return jax.shard_map(body, mesh=mesh, in_specs=in_specs, out_specs=out_specs, check_vma=False)
```

profile of v0, /device:TPU:0, one launch (start us, length us, event | category | flops | bytes accessed | tf_op | source)
XLA Modules:
  0.0 86.0 jit_solution(2360227370935455509)
XLA Ops:
  0.0 1.2 %copy.49 = f32[384,384]{1,0:T(8,128)S(1)} copy(f32[384,384]{1,0:T(8,128)} %param.10) | data formatting | bytes 1179648
  1.2 0.7 fusion.37
  1.9 1.2 %fusion.24 = f32[6,128,384]{2,0,1:T(8,128)S(1)} fusion(f32[3,128,384]{2,1,0:T(8,128)S(1)} %bitcast.54, s32[6]{0:T(128)S(1)} %get-tuple-element.200), kind=kOutput, calls=%fused_computation.24 | convolution fusion | flops 10616850 | bytes 1769496 | tf_op jit(solution)/shard_map/qk,kbw->qbw/dot_general | solution.py:23
  3.1 0.0 copy-done
  3.1 1.3 %fusion.22 = f32[6,128,384]{2,1,0:T(8,128)S(1)} fusion(f32[6,128,384]{2,0,1:T(8,128)S(1)} %fusion.24, f32[1,4,6,128,128]{4,3,2,1,0:T(8,128)S(1)} %copy-done, s32[]{:T(128)S(6)} %select_n.39), kind=kOutput, calls=%fused_computation.22 | convolution fusion | flops 452984832 | bytes 3145732 | tf_op jit(solution)/shard_map/qab,qbw->qaw/dot_general | solution.py:24
  4.4 1.4 %fusion.20 = f32[3,128,384]{2,0,1:T(4,128)S(1)} fusion(f32[6,128,384]{2,1,0:T(8,128)S(1)} %fusion.22, s32[6]{0:T(128)S(1)} %get-tuple-element.199), kind=kOutput, calls=%fused_computation.20 | convolution fusion | flops 10616850 | bytes 1769496 | tf_op jit(solution)/shard_map/qi,qaw->iaw/dot_general | solution.py:25
  5.8 0.0 copy-start.1
  5.8 43.8 %while.17 = (s32[]{:T(128)}, f32[3,128,384]{2,0,1:T(4,128)S(1)}, f32[3,128,384]{2,1,0:T(8,128)S(1)}, s32[]{:T(128)}, s32[4,6]{1,0:T(4,128)}, /*index=5*/f32[4,6,...) while((s32[]{:T(128)}, f32[3,128,384]{2,0,1:T(4,128)S(1)}, ...), condition=%wide.region_1.2_spmd, body=%wide.region_0.1_spmd.sunk | while | flops 474366016 | bytes 10813896 | solution.py:49
  5.8 0.5 collective-permute-start
  6.3 0.7 fusion.55
  7.0 8.8 %collective-permute-done = f32[3,128,384]{2,1,0:T(8,128)S(1)} collective-permute-done((f32[3,128,384]{2,1,0:T(8,128)S(1)}, f32[3,128,384]{2,1,0:T(8,128)S(1)}, u32[]{:S(2)}, u32[]{:S(2)}) %collective-permute-start) | collective-permute-done | bytes 589856 | tf_op jit(solution)/shard_map/while/body/eval_jaxpr/ppermute | solution.py:12
  15.8 1.2 %fusion.56 = f32[6,128,384]{2,0,1:T(8,128)S(1)} fusion(f32[3,128,384]{2,1,0:T(8,128)S(1)} %collective-permute-done, s32[6]{0:T(128)S(1)} %get-tuple-element.246), kind=kOutput, calls=%fused_computation.5.clone.1 | convolution fusion | flops 10616850 | bytes 1769496 | tf_op jit(solution)/shard_map/while/body/eval_jaxpr/qk,kbw->qbw/dot_general | solution.py:23
  17.0 1.3 %fusion.57 = f32[6,128,384]{2,1,0:T(8,128)S(1)} fusion(f32[6,128,384]{2,0,1:T(8,128)S(1)} %fusion.56, f32[4,6,128,128]{3,2,1,0:T(8,128)S(1)} %get-tuple-element.275, s32[]{:T(128)S(6)} %select_n.43), kind=kOutput, calls=%fused_computation.3.clone.1 | convolution fusion | flops 452984832 | bytes 3145732 | tf_op jit(solution)/shard_map/while/body/eval_jaxpr/qab,qbw->qaw/dot_general | solution.py:24
  18.3 2.5 %fusion.58 = f32[3,128,384]{2,0,1:T(4,128)S(1)} fusion(f32[3,128,384]{2,0,1:T(4,128)S(1)} %get-tuple-element.260, f32[6,128,384]{2,1,0:T(8,128)S(1)} %fusion.57, s32[6]{0:T(128)S(1)} %get-tuple-element.247), kind=kOutput, calls=%fused_computation.2.clone.1 | convolution fusion | flops 10764306 | bytes 2359320 | tf_op jit(solution)/shard_map/while/body/eval_jaxpr/qi,qaw->iaw/dot_general | solution.py:25
  20.9 0.1 collective-permute-start
  21.0 0.7 fusion.55
  21.7 8.6 %collective-permute-done = f32[3,128,384]{2,1,0:T(8,128)S(1)} collective-permute-done((f32[3,128,384]{2,1,0:T(8,128)S(1)}, f32[3,128,384]{2,1,0:T(8,128)S(1)}, u32[]{:S(2)}, u32[]{:S(2)}) %collective-permute-start) | collective-permute-done | bytes 589856 | tf_op jit(solution)/shard_map/while/body/eval_jaxpr/ppermute | solution.py:12
  30.2 1.2 %fusion.56 = f32[6,128,384]{2,0,1:T(8,128)S(1)} fusion(f32[3,128,384]{2,1,0:T(8,128)S(1)} %collective-permute-done, s32[6]{0:T(128)S(1)} %get-tuple-element.246), kind=kOutput, calls=%fused_computation.5.clone.1 | convolution fusion | flops 10616850 | bytes 1769496 | tf_op jit(solution)/shard_map/while/body/eval_jaxpr/qk,kbw->qbw/dot_general | solution.py:23
  31.4 1.3 %fusion.57 = f32[6,128,384]{2,1,0:T(8,128)S(1)} fusion(f32[6,128,384]{2,0,1:T(8,128)S(1)} %fusion.56, f32[4,6,128,128]{3,2,1,0:T(8,128)S(1)} %get-tuple-element.275, s32[]{:T(128)S(6)} %select_n.43), kind=kOutput, calls=%fused_computation.3.clone.1 | convolution fusion | flops 452984832 | bytes 3145732 | tf_op jit(solution)/shard_map/while/body/eval_jaxpr/qab,qbw->qaw/dot_general | solution.py:24
  32.7 2.5 %fusion.58 = f32[3,128,384]{2,0,1:T(4,128)S(1)} fusion(f32[3,128,384]{2,0,1:T(4,128)S(1)} %get-tuple-element.260, f32[6,128,384]{2,1,0:T(8,128)S(1)} %fusion.57, s32[6]{0:T(128)S(1)} %get-tuple-element.247), kind=kOutput, calls=%fused_computation.2.clone.1 | convolution fusion | flops 10764306 | bytes 2359320 | tf_op jit(solution)/shard_map/while/body/eval_jaxpr/qi,qaw->iaw/dot_general | solution.py:25
  35.3 0.1 collective-permute-start
  35.4 0.7 fusion.55
  36.1 8.6 %collective-permute-done = f32[3,128,384]{2,1,0:T(8,128)S(1)} collective-permute-done((f32[3,128,384]{2,1,0:T(8,128)S(1)}, f32[3,128,384]{2,1,0:T(8,128)S(1)}, u32[]{:S(2)}, u32[]{:S(2)}) %collective-permute-start) | collective-permute-done | bytes 589856 | tf_op jit(solution)/shard_map/while/body/eval_jaxpr/ppermute | solution.py:12
  44.6 1.2 %fusion.56 = f32[6,128,384]{2,0,1:T(8,128)S(1)} fusion(f32[3,128,384]{2,1,0:T(8,128)S(1)} %collective-permute-done, s32[6]{0:T(128)S(1)} %get-tuple-element.246), kind=kOutput, calls=%fused_computation.5.clone.1 | convolution fusion | flops 10616850 | bytes 1769496 | tf_op jit(solution)/shard_map/while/body/eval_jaxpr/qk,kbw->qbw/dot_general | solution.py:23
  45.8 1.3 %fusion.57 = f32[6,128,384]{2,1,0:T(8,128)S(1)} fusion(f32[6,128,384]{2,0,1:T(8,128)S(1)} %fusion.56, f32[4,6,128,128]{3,2,1,0:T(8,128)S(1)} %get-tuple-element.275, s32[]{:T(128)S(6)} %select_n.43), kind=kOutput, calls=%fused_computation.3.clone.1 | convolution fusion | flops 452984832 | bytes 3145732 | tf_op jit(solution)/shard_map/while/body/eval_jaxpr/qab,qbw->qaw/dot_general | solution.py:24
  47.1 2.5 %fusion.58 = f32[3,128,384]{2,0,1:T(4,128)S(1)} fusion(f32[3,128,384]{2,0,1:T(4,128)S(1)} %get-tuple-element.260, f32[6,128,384]{2,1,0:T(8,128)S(1)} %fusion.57, s32[6]{0:T(128)S(1)} %get-tuple-element.247), kind=kOutput, calls=%fused_computation.2.clone.1 | convolution fusion | flops 10764306 | bytes 2359320 | tf_op jit(solution)/shard_map/while/body/eval_jaxpr/qi,qaw->iaw/dot_general | solution.py:25
  49.7 0.0 copy-done.1
  49.7 0.1 broadcast_bitcast_fusion
  49.8 1.0 %multiply_reduce_fusion = f32[]{:T(128)} fusion(f32[3,128,384]{2,0,1:T(4,128)S(1)} %get-tuple-element.182, f32[3,384]{1,0:T(4,128)S(1)} %bitcast.57), kind=kLoop, calls=%fused_computation.26 | loop fusion | flops 442367 | bytes 594436 | tf_op jit(solution)/shard_map/reduce_sum | solution.py:54
  50.8 33.4 %psum.7 = f32[]{:T(128)} all-reduce(f32[]{:T(128)} %multiply_reduce_fusion), channel_id=1, replica_groups=mesh['parts'=2,'blk'=4,'col'=4] {'blk','col'}, use_global_device_ids=true, to_apply=%region_3.4 | all-reduce | flops 1 | bytes 8 | tf_op jit(solution)/shard_map/psum | solution.py:54
  84.9 0.2 mul.31
  85.1 0.9 %fusion.27 = f32[384,384]{1,0:T(8,128)} fusion(f32[48,8,3,128]{3,2,1,0:T(4,128)S(1)} %bitcast.56, f32[3,128,384]{2,1,0:T(8,128)S(1)} %copy.7, f32[]{:T(128)S(6)} %min_shard_map.3), kind=kLoop, calls=%fused_computation.29 | loop fusion | flops 442368 | bytes 1769476 | tf_op jit(solution)/shard_map/mul | solution.py:58
  (7 shorter events, 0.2 us)
Async XLA Ops:
  0.0 3.1 %copy-start = (f32[1,4,6,128,128]{4,3,2,1,0:T(8,128)S(1)}, f32[1,4,6,128,128]{4,3,2,1,0:T(8,128)}, u32[]{:S(2)}) copy-start(f32[1,4,6,128,128]{4,3,2,1,0:T(8,128)} %param.7) | copy-start | bytes 4718596
  5.8 43.9 %copy-start.1 = (s32[3,3]{1,0:T(4,128)S(1)}, s32[3,3]{1,0:T(4,128)}, u32[]{:S(2)}) copy-start(s32[3,3]{1,0:T(4,128)} %param.11) | copy-start | bytes 112
  5.8 10.0 %collective-permute-start = (f32[3,128,384]{2,1,0:T(8,128)S(1)}, f32[3,128,384]{2,1,0:T(8,128)S(1)}, u32[]{:S(2)}, u32[]{:S(2)}) collective-permute-start(f32[3,128,384]{2,1,0:T(8,128)S(1)} %get-tuple-element.261), channel_id=1, source_target_pairs={{0,4},{4,8},{8,12},{12,0},{1,5},{5,9},{9,13},{13,1},{2,6},{6,10},{... | collective-permute-start | bytes 1769480 | tf_op jit(solution)/shard_map/while/body/eval_jaxpr/ppermute | solution.py:12
  20.9 9.4 %collective-permute-start = (f32[3,128,384]{2,1,0:T(8,128)S(1)}, f32[3,128,384]{2,1,0:T(8,128)S(1)}, u32[]{:S(2)}, u32[]{:S(2)}) collective-permute-start(f32[3,128,384]{2,1,0:T(8,128)S(1)} %get-tuple-element.261), channel_id=1, source_target_pairs={{0,4},{4,8},{8,12},{12,0},{1,5},{5,9},{9,13},{13,1},{2,6},{6,10},{... | collective-permute-start | bytes 1769480 | tf_op jit(solution)/shard_map/while/body/eval_jaxpr/ppermute | solution.py:12
  35.3 9.4 %collective-permute-start = (f32[3,128,384]{2,1,0:T(8,128)S(1)}, f32[3,128,384]{2,1,0:T(8,128)S(1)}, u32[]{:S(2)}, u32[]{:S(2)}) collective-permute-start(f32[3,128,384]{2,1,0:T(8,128)S(1)} %get-tuple-element.261), channel_id=1, source_target_pairs={{0,4},{4,8},{8,12},{12,0},{1,5},{5,9},{9,13},{13,1},{2,6},{6,10},{... | collective-permute-start | bytes 1769480 | tf_op jit(solution)/shard_map/while/body/eval_jaxpr/ppermute | solution.py:12
where the time goes:
time: 86.3 us; the launch traced here: 86 us
  blocking collectives  33.4 us (39%)
  waiting for transfers between devices  25.9 us (30%)
  matrix products  18.8 us (22%)
  local copies, waits for them, and re-layouts  4.42 us (5%)
  other arithmetic  1.92 us (2%)
    psum x1, blocking collectives, body(): squares = lax.psum(jnp.sum(gradient * gradient), ('blk', 'col'))  33.4 us
    ppermute x3, waiting for transfers between devices, shifted(): return lax.ppermute(value, axis, pairs)  25.9 us
    dot_general x4, matrix products, contribute(): jnp.einsum('qi,qaw->iaw', row_hot, partial_prod, precision=highest)  8.98 us
    dot_general x4, matrix products, contribute(): jnp.einsum('qab,qbw->qaw', group_blocks, chosen, precision=highest)  5.18 us
    dot_general x4, matrix products, contribute(): chosen = jnp.einsum('qk,kbw->qbw', col_hot, panel_part, precision=highest)  4.63 us
    eq x4, local copies, waits for them, and re-layouts, contribute(): row_hot = (group_rows[:, None] == local_ids).astype(jnp.float32)  2.82 us
  transfers between devices with their start and end apart: 3, of which 3 were waited for; matrix products, arithmetic and copies ran while one was open for 2% of the time, Pallas kernels for 0%

commit v1 on v0

v1 whole, which is shorter than its diff:
```python
import functools

import jax
import jax.numpy as jnp
from jax import lax
from jax.experimental import pallas as pl
from jax.experimental.pallas import tpu as pltpu
from jax.sharding import PartitionSpec as P

trust_radius = 0.5
LIMIT = 48 << 20
VM = pl.BlockSpec(memory_space=pltpu.VMEM)
SM = pl.BlockSpec(memory_space=pltpu.SMEM)


def vmem(value):
    return pltpu.with_memory_space_constraint(value, pltpu.VMEM)


def split(value):
    high = value.astype(jnp.bfloat16)
    low = (value - high.astype(jnp.float32)).astype(jnp.bfloat16)
    return high, low


def product(high_a, low_a, b):
    high_b, low_b = split(b)
    dot = functools.partial(jnp.dot, preferred_element_type=jnp.float32)
    return dot(high_a, high_b) + (dot(high_a, low_b) + dot(low_a, high_b))


def prepare(me_ref, rows_ref, cols_ref, blocks_ref, *dense_refs):
    groups, slots = blocks_ref.shape[0], blocks_ref.shape[1]
    size = blocks_ref.shape[-1]
    for ref in dense_refs:
        ref[...] = jnp.zeros_like(ref)
    chips = groups // 2
    chip, core = lax.div(me_ref[0], 2), lax.rem(me_ref[0], 2)
    for rel in range(groups):
        high_ref, low_ref = dense_refs[2 * rel], dense_refs[2 * rel + 1]
        owner = lax.rem(core + rel, 2)
        group = 2 * lax.rem(chip + chips - rel // 2, chips) + owner
        for slot in range(slots):
            col = cols_ref[group, slot]

            @pl.when(col >= 0)
            def _():
                high, low = split(blocks_ref[group, slot])
                row_at = pl.ds(pl.multiple_of(rows_ref[group, slot] * size, size), size)
                col_at = pl.ds(pl.multiple_of(col * size, size), size)
                high_ref[row_at, col_at] = high
                low_ref[row_at, col_at] = low


def start_sum(*refs):
    *terms, out_ref = refs
    total = product(terms[0][...], terms[1][...], terms[2][...])
    for at in range(3, len(terms), 3):
        total += product(terms[at][...], terms[at + 1][...], terms[at + 2][...])
    out_ref[...] = total


def add_sum(running_ref, *refs):
    *terms, out_ref = refs
    total = running_ref[...]
    for at in range(0, len(terms), 3):
        total += product(terms[at][...], terms[at + 1][...], terms[at + 2][...])
    out_ref[...] = total


def finish(pattern_ref, running_ref, high_ref, low_ref, b_ref, out_ref, squares_ref):
    row_blocks, col_blocks = pattern_ref.shape
    size = out_ref.shape[0] // row_blocks
    total = running_ref[...] + product(high_ref[...], low_ref[...], b_ref[...])
    squares = jnp.zeros((1, size), jnp.float32)
    for i in range(row_blocks):
        for j in range(col_blocks):
            part = total[i * size : (i + 1) * size, j * size : (j + 1) * size]
            part = part * pattern_ref[i, j].astype(jnp.float32)
            out_ref[i * size : (i + 1) * size, j * size : (j + 1) * size] = part
            squares += jnp.sum(part * part, axis=0, keepdims=True)
    squares_ref[...] = squares


def scale(limit, gradient_ref, one_ref, two_ref, out_ref):
    squares = jnp.sum(one_ref[...] + two_ref[...], axis=1, keepdims=True)
    factor = jnp.minimum(1.0, limit / jnp.sqrt(squares + 1e-06))
    out_ref[...] = -gradient_ref[...] * factor


def call(kernel, flops, outs, *args, specs=None):
    specs = specs or [VM] * len(args)
    moved = sum(a.size * a.dtype.itemsize for a in args)
    args = [vmem(a) if s is VM else a for a, s in zip(args, specs)]
    return pl.pallas_call(
        kernel,
        out_shape=outs,
        in_specs=specs,
        out_specs=jax.tree.map(lambda _: VM, outs),
        compiler_params=pltpu.CompilerParams(vmem_limit_bytes=LIMIT),
        cost_estimate=pl.CostEstimate(flops=flops, bytes_accessed=moved, transcendentals=0),
    )(*args)


def body(sizes, a_blocks, a_rows, a_cols, b_panel, pattern):
    blk_count, col_count = sizes
    chips = blk_count // 2
    blocks, rows, cols = a_blocks[0], a_rows[0], a_cols[0]
    size = blocks.shape[-1]
    height, width = b_panel.shape
    me = lax.axis_index("blk")

    def move(value, chip_step, core_flip):
        pairs = [(i, (i // 2 + chip_step) % chips * 2 + (i % 2) ^ core_flip) for i in range(blk_count)]
        return lax.ppermute(value, "blk", pairs)

    far = [move(b_panel, step, 0) for step in range(1, chips)]
    near = move(b_panel, 0, 1)
    half = jax.ShapeDtypeStruct((height, height), jnp.bfloat16)
    dense = call(
        prepare,
        0,
        [half] * (2 * blk_count),
        me.astype(jnp.int32).reshape(1),
        rows,
        cols,
        blocks,
        specs=[SM, SM, SM, VM],
    )
    full = jax.ShapeDtypeStruct((height, width), jnp.float32)
    flops = 6 * height * height * width
    running = call(start_sum, 2 * flops, full, *dense[0:2], b_panel, *dense[2:4], near)
    for step in range(1, chips):
        at = 4 * step
        there, running = lax.optimization_barrier((far[step - 1], running))
        forward = move(there, 0, 1)
        running = call(add_sum, flops, full, running, dense[at], dense[at + 1], there)
        if step < chips - 1:
            running = call(add_sum, flops, full, running, dense[at + 2], dense[at + 3], forward)
    gradient, squares = call(
        finish,
        flops,
        (full, jax.ShapeDtypeStruct((1, size), jnp.float32)),
        pattern,
        running,
        dense[-2],
        dense[-1],
        forward,
        specs=[SM, VM, VM, VM, VM],
    )

    def swap(value, step, core_flip):
        blk_step, col_step = step
        pairs = []
        for i in range(blk_count):
            for j in range(col_count):
                pairs.append((i * col_count + j, ((i ^ blk_step) ^ core_flip) * col_count + (j ^ col_step)))
        return lax.ppermute(value, ("blk", "col"), pairs)

    steps = []
    reach = 2
    while reach < blk_count:
        steps.append(((reach, 0), 1))
        reach *= 2
    reach = 1
    while reach < col_count:
        steps.append(((0, reach), 1))
        reach *= 2
    squares = squares + swap(squares, (0, 0), 1)
    for step in steps[:-1]:
        squares = squares + swap(squares, *step)
    last = swap(squares, *steps[-1])
    limit = trust_radius * height * blk_count
    return call(functools.partial(scale, limit), 0, full, gradient, squares, last)


def solution(mesh):
    in_specs = (
        P(("parts", "blk"), None, None, None, None),
        P(("parts", "blk"), None, None),
        P(("parts", "blk"), None, None),
        P(("parts", "blk"), "col"),
        P(("parts", "blk"), "col"),
    )
    out_specs = P(("parts", "blk"), "col")
    run = functools.partial(body, (mesh.shape["blk"], mesh.shape["col"]))
    return jax.shard_map(run, mesh=mesh, in_specs=in_specs, out_specs=out_specs, check_vma=False)
```

time: 86.3 us -> 32.7 us (0.38)
  blocking collectives: 33.4 us -> 0 us
  matrix products: 18.8 us -> 0 us
  waiting for transfers between devices: 25.9 us -> 15.2 us
  starting transfers between devices: 0.61 us -> 9 us
  Pallas kernels: 0 us -> 5.42 us
  other arithmetic: 1.92 us -> 0.01 us
  local copies, waits for them, and re-layouts: 4.42 us -> 2.78 us
    psum x1 -> x0, blocking collectives: 33.4 us -> none  [body(): squares = lax.psum(jnp.sum(gradient * gradient), ('blk', 'col'))]
    dot_general x12 -> x0, matrix products: 18.8 us -> none  [the longest x4 8.98 us: contribute(): jnp.einsum('qi,qaw->iaw', row_hot, partial_prod, precision=highest)]
    ppermute x3 -> x7, waiting for transfers between devices: 25.9 us -> 15.2 us  [the longest x3 10.2 us: move(): return lax.ppermute(value, 'blk', pairs)]
    ppermute x3 -> x7, starting transfers between devices: 0.61 us -> 9 us  [the longest x4 6.06 us: swap(): return lax.ppermute(value, ('blk', 'col'), pairs)]
    pallas_call x0 -> x5, Pallas kernels: none -> 5.42 us  [call(): pl.pallas_call(kernel, out_shape=outs, in_specs=specs, out_specs=jax.tree...]
    eq x4 -> x0, local copies, waits for them, and re-layouts: 2.82 us -> none  [contribute(): row_hot = (group_rows[:, None] == local_ids).astype(jnp.float32)]
    unnamed x7 -> x10, local copies, waits for them, and re-layouts: 1.27 us -> 2.78 us
    reduce_sum x1 -> x0, other arithmetic: 1.01 us -> none  [body(): squares = lax.psum(jnp.sum(gradient * gradient), ('blk', 'col'))]
  transfers between devices with their start and end apart: 3 -> 7, of which waited for: 3 -> 6; matrix products, arithmetic and copies ran while one was open for 2% -> 0% of each run, Pallas kernels for 0% -> 10%
where the time goes in v1:
time: 32.7 us; the launch traced here: 32.5 us
  waiting for transfers between devices  15.2 us (46%)
  starting transfers between devices  9 us (28%)
  Pallas kernels  5.42 us (17%)
  local copies, waits for them, and re-layouts  2.78 us (9%)
    ppermute x3, waiting for transfers between devices, move(): return lax.ppermute(value, 'blk', pairs)  10.2 us
    ppermute x4, starting transfers between devices, swap(): return lax.ppermute(value, ('blk', 'col'), pairs)  6.06 us
    pallas_call x5, Pallas kernels, call(): pl.pallas_call(kernel, out_shape=outs, in_specs=specs, out_specs=jax.tree...  5.42 us
    ppermute x4, waiting for transfers between devices, swap(): return lax.ppermute(value, ('blk', 'col'), pairs)  5.01 us
    ppermute x3, starting transfers between devices, move(): return lax.ppermute(value, 'blk', pairs)  2.94 us
    unnamed x10, local copies, waits for them, and re-layouts  2.78 us
  transfers between devices with their start and end apart: 7, of which 6 were waited for; matrix products, arithmetic and copies ran while one was open for 0% of the time, Pallas kernels for 10%

profile of v1, /device:TPU:0, one launch (start us, length us, event | category | flops | bytes accessed | tf_op | source)
XLA Modules:
  0.0 32.5 jit_solution(6671550483089390960)
XLA Ops:
  0.0 0.5 %collective-permute-start.1 = (f32[384,384]{1,0:T(8,128)}, f32[384,384]{1,0:T(8,128)S(1)}, u32[]{:S(2)}, u32[]{:S(2)}) collective-permute-start(f32[384,384]{1,0:T(8,128)} %refs_2_.1), channel_id=1, source_target_pairs={{0,4},{4,0},{8,12},{12,8},{1,5},{5,1},{9,13},{13,9},{2,6},{6,2},{1... | collective-permute-start | bytes 1769480 | tf_op jit(solution)/shard_map/ppermute | solution.py:115
  0.5 2.5 %collective-permute-start = (f32[384,384]{1,0:T(8,128)}, f32[384,384]{1,0:T(8,128)S(1)}, u32[]{:S(2)}, u32[]{:S(2)}) collective-permute-start(f32[384,384]{1,0:T(8,128)} %refs_2_.1), channel_id=1, source_target_pairs={{0,8},{4,12},{8,0},{12,4},{1,9},{5,13},{9,1},{13,5},{2,10},{6,14},... | collective-permute-start | bytes 1769480 | tf_op jit(solution)/shard_map/ppermute | solution.py:115
  2.9 0.0 copy-start
  2.9 1.4 %copy-done = f32[1,4,6,128,128]{4,3,2,1,0:T(8,128)S(1)} copy-done((f32[1,4,6,128,128]{4,3,2,1,0:T(8,128)S(1)}, f32[1,4,6,128,128]{4,3,2,1,0:T(8,128)}, u32[]{:S(2)}) %copy-start) | copy-done | bytes 1572888
  4.4 0.0 copy-start.2
  4.4 0.7 %copy-done.2 = s32[1,4,6]{2,1,0:T(4,128)S(1)} copy-done((s32[1,4,6]{2,1,0:T(4,128)S(1)}, s32[1,4,6]{2,1,0:T(4,128)}, u32[]{:S(2)}) %copy-start.2) | copy-done | bytes 120
  5.0 0.0 copy-start.3
  5.0 0.7 %copy-done.3 = s32[1,4,6]{2,1,0:T(4,128)S(1)} copy-done((s32[1,4,6]{2,1,0:T(4,128)S(1)}, s32[1,4,6]{2,1,0:T(4,128)}, u32[]{:S(2)}) %copy-start.3) | copy-done | bytes 120
  5.7 0.0 copy-start.1
  5.7 1.2 %shard_map.55 = (bf16[384,384]{1,0:T(8,128)(2,1)S(1)}, bf16[384,384]{1,0:T(8,128)(2,1)S(1)}, bf16[384,384]{1,0:T(8,128)(2,1)S(1)}, bf16[384,384]{1,0:T(8,128)(2,...) custom-call(s32[1]{0:T(128)} %bitcast.me_ref, ...), custom_call_target="tpu_custom_call" | custom-call | bytes 1573060 | tf_op jit(solution)/shard_map/pallas_call | solution.py:95
  6.9 0.0 collective-permute-done.1.refs_5_
  6.9 0.0 copy-done.1
  6.9 1.2 %shard_map.56.running_ref = f32[384,384]{1,0:T(8,128)S(1)} custom-call(bf16[384,384]{1,0:T(8,128)(2,1)S(1)} %get-tuple-element.17.refs_0_, bf16[384,384]{1,0:T(8,128)(2,1)S(1)} %get-tuple-element.18.refs_1_, f32[384,384]{1,0:T(8,128)S(1)} %copy-done.1, bf16[384,384]{1,0:T(8,128)(2,1)S(1)} %get-tuple-element.19.refs_3_, ...), custom_call_target="tpu_custom_call" | custom-call | flops 679477248 | bytes 2359296 | tf_op jit(solution)/shard_map/pallas_call | solution.py:95
  8.2 0.0 copy-start.4
  8.2 9.0 %collective-permute-done.refs_2_ = f32[384,384]{1,0:T(8,128)S(1)} collective-permute-done((f32[384,384]{1,0:T(8,128)}, f32[384,384]{1,0:T(8,128)S(1)}, u32[]{:S(2)}, u32[]{:S(2)}) %collective-permute-start) | collective-permute-done | bytes 589856 | tf_op jit(solution)/shard_map/ppermute | solution.py:115
  17.2 0.0 collective-permute-start.2
  17.2 0.7 %shard_map.57.running_ref = f32[384,384]{1,0:T(8,128)S(1)} custom-call(f32[384,384]{1,0:T(8,128)S(1)} %shard_map.56.running_ref, bf16[384,384]{1,0:T(8,128)(2,1)S(1)} %get-tuple-element.22.refs_0_, bf16[384,384]{1,0:T(8,128)(2,1)S(1)} %get-tuple-element.23.refs_1_, f32[384,384]{1,0:T(8,128)S(1)} %collective-permute-done.refs_2_), custom_call_target="tpu_custom_call" | custom-call | flops 339738624 | bytes 1769472 | tf_op jit(solution)/shard_map/pallas_call | solution.py:95
  17.9 1.3 %collective-permute-done.2.b_ref = f32[384,384]{1,0:T(8,128)S(1)} collective-permute-done((f32[384,384]{1,0:T(8,128)S(1)}, f32[384,384]{1,0:T(8,128)S(1)}, u32[]{:S(2)}, u32[]{:S(2)}) %collective-permute-start.2) | collective-permute-done | bytes 589856 | tf_op jit(solution)/shard_map/ppermute | solution.py:115
  19.2 0.0 copy-done.4
  19.2 1.3 %shard_map.58 = (f32[384,384]{1,0:T(8,128)S(1)}, f32[1,128]{1,0:T(1,128)S(1)}) custom-call(s32[3,3]{1,0:T(4,128)S(1)} %copy-done.4, f32[384,384]{1,0:T(8,128)S(1)} %shard_map.57.running_ref, bf16[384,384]{1,0:T(8,128)(2,1)S(1)} %get-tuple-element.25.high_ref, bf16[384,384]{1,0:T(8,128)(2,1)S(1)} %get-tuple-element.26.low_ref, ...), custom_call_target="tpu_custom_call" | custom-call | flops 339738624 | bytes 1769508 | tf_op jit(solution)/shard_map/pallas_call | solution.py:95
  20.5 0.2 collective-permute-start.3
  20.7 1.0 %collective-permute-done.3 = f32[1,128]{1,0:T(1,128)S(1)} collective-permute-done((f32[1,128]{1,0:T(1,128)S(1)}, f32[1,128]{1,0:T(1,128)S(1)}, u32[]{:S(2)}, u32[]{:S(2)}) %collective-permute-start.3) | collective-permute-done | bytes 544 | tf_op jit(solution)/shard_map/ppermute | solution.py:158
  21.7 1.6 %collective-permute-start.4 = (f32[1,128]{1,0:T(1,128)S(1)}, f32[1,128]{1,0:T(1,128)S(1)}, u32[]{:S(2)}, u32[]{:S(2)}) collective-permute-start(f32[1,128]{1,0:T(1,128)S(1)} %add.9), channel_id=1, source_target_pairs={{0,12},{1,13},{2,14},{3,15},{4,8},{5,9},{6,10},{7,11},{8,4},{9,5},... | collective-permute-start | bytes 1544 | tf_op jit(solution)/shard_map/ppermute | solution.py:158
  23.2 1.4 %collective-permute-done.4 = f32[1,128]{1,0:T(1,128)S(1)} collective-permute-done((f32[1,128]{1,0:T(1,128)S(1)}, f32[1,128]{1,0:T(1,128)S(1)}, u32[]{:S(2)}, u32[]{:S(2)}) %collective-permute-start.4) | collective-permute-done | bytes 544 | tf_op jit(solution)/shard_map/ppermute | solution.py:158
  24.6 1.6 %collective-permute-start.5 = (f32[1,128]{1,0:T(1,128)S(1)}, f32[1,128]{1,0:T(1,128)S(1)}, u32[]{:S(2)}, u32[]{:S(2)}) collective-permute-start(f32[1,128]{1,0:T(1,128)S(1)} %add.10), channel_id=1, source_target_pairs={{0,5},{1,4},{2,7},{3,6},{4,1},{5,0},{6,3},{7,2},{8,13},{9,12},{10,... | collective-permute-start | bytes 1544 | tf_op jit(solution)/shard_map/ppermute | solution.py:158
  26.3 1.3 %collective-permute-done.5 = f32[1,128]{1,0:T(1,128)S(1)} collective-permute-done((f32[1,128]{1,0:T(1,128)S(1)}, f32[1,128]{1,0:T(1,128)S(1)}, u32[]{:S(2)}, u32[]{:S(2)}) %collective-permute-start.5) | collective-permute-done | bytes 544 | tf_op jit(solution)/shard_map/ppermute | solution.py:158
  27.6 2.7 %collective-permute-start.6 = (f32[1,128]{1,0:T(1,128)S(1)}, f32[1,128]{1,0:T(1,128)S(1)}, u32[]{:S(2)}, u32[]{:S(2)}) collective-permute-start(f32[1,128]{1,0:T(1,128)S(1)} %add.11.one_ref), channel_id=1, source_target_pairs={{0,6},{1,7},{2,4},{3,5},{4,2},{5,3},{6,0},{7,1},{8,14},{9,15},{10,... | collective-permute-start | bytes 1544 | tf_op jit(solution)/shard_map/ppermute | solution.py:158
  30.3 1.3 %collective-permute-done.6.two_ref = f32[1,128]{1,0:T(1,128)S(1)} collective-permute-done((f32[1,128]{1,0:T(1,128)S(1)}, f32[1,128]{1,0:T(1,128)S(1)}, u32[]{:S(2)}, u32[]{:S(2)}) %collective-permute-start.6) | collective-permute-done | bytes 544 | tf_op jit(solution)/shard_map/ppermute | solution.py:158
  31.6 0.9 %shard_map.59 = f32[384,384]{1,0:T(8,128)} custom-call(f32[384,384]{1,0:T(8,128)S(1)} %get-tuple-element.27.gradient_ref, f32[1,128]{1,0:T(1,128)S(1)} %add.11.one_ref, f32[1,128]{1,0:T(1,128)S(1)} %collective-permute-done.6.two_ref), custom_call_target="tpu_custom_call" | custom-call | bytes 590848 | tf_op jit(solution)/shard_map/pallas_call | solution.py:95
  (3 shorter events, 0.0 us)
Async XLA Ops:
  0.0 6.9 %collective-permute-start.1 = (f32[384,384]{1,0:T(8,128)}, f32[384,384]{1,0:T(8,128)S(1)}, u32[]{:S(2)}, u32[]{:S(2)}) collective-permute-start(f32[384,384]{1,0:T(8,128)} %refs_2_.1), channel_id=1, source_target_pairs={{0,4},{4,0},{8,12},{12,8},{1,5},{5,1},{9,13},{13,9},{2,6},{6,2},{1... | collective-permute-start | bytes 1769480 | tf_op jit(solution)/shard_map/ppermute | solution.py:115
  0.5 16.7 %collective-permute-start = (f32[384,384]{1,0:T(8,128)}, f32[384,384]{1,0:T(8,128)S(1)}, u32[]{:S(2)}, u32[]{:S(2)}) collective-permute-start(f32[384,384]{1,0:T(8,128)} %refs_2_.1), channel_id=1, source_target_pairs={{0,8},{4,12},{8,0},{12,4},{1,9},{5,13},{9,1},{13,5},{2,10},{6,14},... | collective-permute-start | bytes 1769480 | tf_op jit(solution)/shard_map/ppermute | solution.py:115
  2.9 1.4 %copy-start = (f32[1,4,6,128,128]{4,3,2,1,0:T(8,128)S(1)}, f32[1,4,6,128,128]{4,3,2,1,0:T(8,128)}, u32[]{:S(2)}) copy-start(f32[1,4,6,128,128]{4,3,2,1,0:T(8,128)} %param.5) | copy-start | bytes 4718596
  4.4 0.7 %copy-start.2 = (s32[1,4,6]{2,1,0:T(4,128)S(1)}, s32[1,4,6]{2,1,0:T(4,128)}, u32[]{:S(2)}) copy-start(s32[1,4,6]{2,1,0:T(4,128)} %param.6) | copy-start | bytes 292
  5.0 0.7 %copy-start.3 = (s32[1,4,6]{2,1,0:T(4,128)S(1)}, s32[1,4,6]{2,1,0:T(4,128)}, u32[]{:S(2)}) copy-start(s32[1,4,6]{2,1,0:T(4,128)} %param.7) | copy-start | bytes 292
  5.7 1.2 %copy-start.1 = (f32[384,384]{1,0:T(8,128)S(1)}, f32[384,384]{1,0:T(8,128)}, u32[]{:S(2)}) copy-start(f32[384,384]{1,0:T(8,128)} %refs_2_.1) | copy-start | bytes 1769476
  8.2 11.0 %copy-start.4 = (s32[3,3]{1,0:T(4,128)S(1)}, s32[3,3]{1,0:T(4,128)}, u32[]{:S(2)}) copy-start(s32[3,3]{1,0:T(4,128)} %pattern_ref.1) | copy-start | bytes 112
  17.2 2.0 %collective-permute-start.2 = (f32[384,384]{1,0:T(8,128)S(1)}, f32[384,384]{1,0:T(8,128)S(1)}, u32[]{:S(2)}, u32[]{:S(2)}) collective-permute-start(f32[384,384]{1,0:T(8,128)S(1)} %collective-permute-done.refs_2_), channel_id=1, source_target_pairs={{0,4},{4,0},{8,12},{12,8},{1,5},{5,1},{9,13},{13,9},{2,6},{6,2},{1... | collective-permute-start | bytes 1769480 | tf_op jit(solution)/shard_map/ppermute | solution.py:115
  20.5 1.2 %collective-permute-start.3 = (f32[1,128]{1,0:T(1,128)S(1)}, f32[1,128]{1,0:T(1,128)S(1)}, u32[]{:S(2)}, u32[]{:S(2)}) collective-permute-start(f32[1,128]{1,0:T(1,128)S(1)} %get-tuple-element.28), channel_id=1, source_target_pairs={{0,4},{1,5},{2,6},{3,7},{4,0},{5,1},{6,2},{7,3},{8,12},{9,13},{10,... | collective-permute-start | bytes 1544 | tf_op jit(solution)/shard_map/ppermute | solution.py:158
  21.7 3.0 %collective-permute-start.4 = (f32[1,128]{1,0:T(1,128)S(1)}, f32[1,128]{1,0:T(1,128)S(1)}, u32[]{:S(2)}, u32[]{:S(2)}) collective-permute-start(f32[1,128]{1,0:T(1,128)S(1)} %add.9), channel_id=1, source_target_pairs={{0,12},{1,13},{2,14},{3,15},{4,8},{5,9},{6,10},{7,11},{8,4},{9,5},... | collective-permute-start | bytes 1544 | tf_op jit(solution)/shard_map/ppermute | solution.py:158
  24.6 3.0 %collective-permute-start.5 = (f32[1,128]{1,0:T(1,128)S(1)}, f32[1,128]{1,0:T(1,128)S(1)}, u32[]{:S(2)}, u32[]{:S(2)}) collective-permute-start(f32[1,128]{1,0:T(1,128)S(1)} %add.10), channel_id=1, source_target_pairs={{0,5},{1,4},{2,7},{3,6},{4,1},{5,0},{6,3},{7,2},{8,13},{9,12},{10,... | collective-permute-start | bytes 1544 | tf_op jit(solution)/shard_map/ppermute | solution.py:158
  27.6 4.0 %collective-permute-start.6 = (f32[1,128]{1,0:T(1,128)S(1)}, f32[1,128]{1,0:T(1,128)S(1)}, u32[]{:S(2)}, u32[]{:S(2)}) collective-permute-start(f32[1,128]{1,0:T(1,128)S(1)} %add.11.one_ref), channel_id=1, source_target_pairs={{0,6},{1,7},{2,4},{3,5},{4,2},{5,3},{6,0},{7,1},{8,14},{9,15},{10,... | collective-permute-start | bytes 1544 | tf_op jit(solution)/shard_map/ppermute | solution.py:158

commit v2 on v1

v2 whole, which is shorter than its diff:
```python
import functools

import jax
import jax.numpy as jnp
from jax import lax
from jax.experimental import pallas as pl
from jax.experimental.pallas import tpu as pltpu
from jax.sharding import PartitionSpec as P

trust_radius = 0.5
LIMIT = 8 << 20
VM = pl.BlockSpec(memory_space=pltpu.VMEM)
SM = pl.BlockSpec(memory_space=pltpu.SMEM)
HBM = pl.BlockSpec(memory_space=pltpu.HBM)


def shape(*dims, dtype=jnp.float32):
    return jax.ShapeDtypeStruct(dims, dtype)


def split(value):
    high = value.astype(jnp.bfloat16)
    low = (value - high.astype(jnp.float32)).astype(jnp.bfloat16)
    return high, low


def product(high_a, low_a, b):
    high_b, low_b = split(b)
    left = jnp.concatenate([high_a, high_a, low_a], axis=1)
    right = jnp.concatenate([high_b, low_b, high_b], axis=0)
    return jnp.dot(left, right, preferred_element_type=jnp.float32)


def columns(core, side, col_blocks, size):
    half = col_blocks // 2
    which = core if side == 0 else 1 - core
    return pl.ds(pl.multiple_of(which * ((col_blocks - half) * size), size), half * size)


def middle_of(col_blocks, size):
    half = col_blocks // 2
    return pl.ds(half * size, size)


def cut(col_blocks, me_ref, b_ref, *refs):
    outs, sems = refs[:-1], refs[-1]
    size = b_ref.shape[1] // col_blocks
    core = lax.rem(me_ref[0], 2)
    where = [columns(core, 0, col_blocks, size), columns(core, 1, col_blocks, size)]
    if len(outs) > 2:
        where.append(middle_of(col_blocks, size))
    copies = [pltpu.make_async_copy(b_ref.at[:, w], out, sems.at[i]) for i, (w, out) in enumerate(zip(where, outs))]
    for copy in copies:
        copy.start()
    for copy in copies:
        copy.wait()


def prepare(me_ref, own_ids, near_ids, own_ref, near_ref, *dense_refs):
    groups, slots, size = own_ref.shape[0], own_ref.shape[1], own_ref.shape[-1]
    height = dense_refs[0].shape[0] // 2
    chips = groups // 2
    chip, core = lax.div(me_ref[0], 2), lax.rem(me_ref[0], 2)
    for ref in dense_refs:
        ref[...] = jnp.zeros_like(ref)
    for rel in range(groups):
        high_ref, low_ref = dense_refs[2 * rel], dense_refs[2 * rel + 1]
        group = 2 * lax.rem(chip + chips - rel // 2, chips) + lax.rem(core + rel, 2)
        for ids, blocks_ref, top in ((own_ids, own_ref, 0), (near_ids, near_ref, height)):
            for slot in range(slots):
                row = ids[group * slots + slot]
                col = ids[(groups + group) * slots + slot]

                @pl.when(col >= 0)
                def _():
                    high, low = split(blocks_ref[group, slot])
                    row_at = pl.ds(pl.multiple_of(row * size + top, size), size)
                    col_at = pl.ds(pl.multiple_of(col * size, size), size)
                    high_ref[row_at, col_at] = high
                    low_ref[row_at, col_at] = low


def start_sum(col_blocks, me_ref, own_high, own_low, own_b, near_high, near_low, near_b, side_ref, *mid_refs):
    height, width = own_b.shape
    size = width // col_blocks
    core = lax.rem(me_ref[0], 2)
    at = columns(core, 0, col_blocks, size)
    side_ref[...] = product(own_high[...], own_low[...], own_b[:, at]) + product(
        near_high[...], near_low[...], near_b[:, at]
    )
    for mid_ref in mid_refs:
        at = middle_of(col_blocks, size)
        mid_ref[...] = product(own_high[:height], own_low[:height], own_b[:, at]) + product(
            near_high[:height], near_low[:height], near_b[:, at]
        )


def add_sum(running_ref, high_ref, low_ref, b_ref, out_ref):
    rows = running_ref.shape[0]
    out_ref[...] = running_ref[...] + product(high_ref[:rows], low_ref[:rows], b_ref[...])


def masked(value, ids, first, row_blocks, col_blocks, col, squares):
    size = value.shape[0] // row_blocks
    rows = []
    for i in range(row_blocks):
        row = []
        for j in range(value.shape[1] // size):
            part = value[i * size : (i + 1) * size, j * size : (j + 1) * size]
            part = part * ids[first + i * col_blocks + col + j].astype(jnp.float32)
            squares = squares + jnp.sum(part * part, axis=0, keepdims=True)
            row.append(part)
        rows.append(jnp.concatenate(row, axis=1))
    return jnp.concatenate(rows, axis=0), squares


def finish_middle(first, row_blocks, col_blocks, ids, running_ref, high_ref, low_ref, b_ref, out_ref, squares_ref):
    height = running_ref.shape[0]
    total = running_ref[...] + product(high_ref[:height], low_ref[:height], b_ref[...])
    zero = jnp.zeros(squares_ref.shape, jnp.float32)
    out_ref[...], squares_ref[...] = masked(total, ids, first, row_blocks, col_blocks, col_blocks // 2, zero)


def finish(first, row_blocks, col_blocks, me_ref, own_ids, near_ids, *refs):
    running_ref, high_ref, low_ref, b_ref, *before, keep_ref, give_ref, squares_ref = refs
    height = keep_ref.shape[0]
    half = col_blocks // 2
    col = lax.rem(me_ref[0], 2) * (col_blocks - half)
    total = running_ref[...] + product(high_ref[...], low_ref[...], b_ref[...])
    squares = before[0][...] if before else jnp.zeros(squares_ref.shape, jnp.float32)
    keep_ref[...], squares = masked(total[:height], own_ids, first, row_blocks, col_blocks, col, squares)
    give_ref[...], squares = masked(total[height:], near_ids, first, row_blocks, col_blocks, col, squares)
    squares_ref[...] = squares


def scale(limit, col_blocks, me_ref, one_ref, two_ref, keep_ref, take_ref, *refs):
    *mid_refs, out_ref = refs
    size = out_ref.shape[1] // col_blocks
    core = lax.rem(me_ref[0], 2)
    squares = jnp.sum(one_ref[...] + two_ref[...], axis=1, keepdims=True)
    factor = -jnp.minimum(1.0, limit / jnp.sqrt(squares + 1e-06))
    out_ref[:, columns(core, 0, col_blocks, size)] = keep_ref[...] * factor
    out_ref[:, columns(core, 1, col_blocks, size)] = take_ref[...] * factor
    for mid_ref in mid_refs:
        out_ref[:, middle_of(col_blocks, size)] = mid_ref[...] * factor


def call(kernel, flops, outs, specs, *args, scratch=()):
    specs = [{"s": SM, "v": VM, "h": HBM}[s] for s in specs]
    moved = sum(a.size * a.dtype.itemsize for a in args)
    place = pltpu.with_memory_space_constraint
    args = [a if s is SM else place(a, s.memory_space) for a, s in zip(args, specs)]
    return pl.pallas_call(
        kernel,
        out_shape=outs,
        in_specs=specs,
        out_specs=jax.tree.map(lambda _: VM, outs),
        scratch_shapes=scratch,
        compiler_params=pltpu.CompilerParams(vmem_limit_bytes=LIMIT),
        cost_estimate=pl.CostEstimate(flops=flops, bytes_accessed=moved, transcendentals=0),
    )(*args)


def body(sizes, a_blocks, a_rows, a_cols, b_panel, pattern):
    blk_count, col_count = sizes
    chips = blk_count // 2
    blocks = a_blocks[0]
    size = blocks.shape[-1]
    height, width = b_panel.shape
    row_blocks, col_blocks = pattern.shape
    half, odd = col_blocks // 2, col_blocks % 2
    me = lax.axis_index("blk").astype(jnp.int32).reshape(1)

    def move(value, chip_step, core_flip):
        pairs = [(i, (i // 2 + chip_step) % chips * 2 + (i % 2) ^ core_flip) for i in range(blk_count)]
        return lax.ppermute(value, "blk", pairs)

    piece = shape(height, half * size)
    middle = shape(height, size)
    side, other, *mids = call(
        functools.partial(cut, col_blocks),
        0,
        [piece, piece] + [middle] * odd,
        "sh",
        me,
        b_panel,
        scratch=[pltpu.SemaphoreType.DMA((2 + odd,))],
    )
    steps = range(1, chips)
    far_mids = [[move(mid, step, 0) for mid in mids] for step in steps]
    far_sides = [move(side, step, 0) for step in steps]
    far_others = [move(other, step, 1) for step in steps]

    ids = jnp.concatenate([a_rows.reshape(-1), a_cols.reshape(-1), pattern.reshape(-1)])
    first = 2 * a_rows.size
    near_blocks = move(blocks, 0, 1)
    near_ids = move(ids, 0, 1)
    near_b = move(b_panel, 0, 1)
    dense = call(
        prepare,
        0,
        [shape(2 * height, height, dtype=jnp.bfloat16)] * (2 * blk_count),
        "sssvv",
        me,
        ids,
        near_ids,
        blocks,
        near_blocks,
    )
    flops = 6 * height * height * size
    wide = shape(2 * height, half * size)
    running, *mid_running = call(
        functools.partial(start_sum, col_blocks),
        4 * flops * half + 2 * flops * odd,
        [wide] + [middle] * odd,
        "svvvvvv",
        me,
        *dense[0:2],
        b_panel,
        *dense[2:4],
        near_b,
    )
    before = []
    for at, step in enumerate(steps):
        same, cross = dense[4 * step : 4 * step + 2], dense[4 * step + 2 : 4 * step + 4]
        for far_mid in far_mids[at]:
            forward = move(far_mid, 0, 1)
            mid_running = [call(add_sum, flops, middle, "vvvv", *mid_running, *same, far_mid)]
            if step < chips - 1:
                mid_running = [call(add_sum, flops, middle, "vvvv", *mid_running, *cross, forward)]
            else:
                *mid_running, squares = call(
                    functools.partial(finish_middle, first, row_blocks, col_blocks),
                    flops,
                    [middle, shape(1, size)],
                    "svvvv",
                    ids,
                    *mid_running,
                    *cross,
                    forward,
                )
                before = [squares]
        running = call(add_sum, 2 * flops * half, wide, "vvvv", running, *same, far_sides[at])
        if step < chips - 1:
            running = call(add_sum, 2 * flops * half, wide, "vvvv", running, *cross, far_others[at])
    keep, give, squares = call(
        functools.partial(finish, first, row_blocks, col_blocks),
        2 * flops * half,
        [piece, piece, shape(1, size)],
        "sssvvvv" + "v" * odd,
        me,
        ids,
        near_ids,
        running,
        *cross,
        far_others[-1],
        *before,
    )
    take = move(give, 0, 1)

    def swap(value, blk_step, col_step):
        pairs = []
        for i in range(blk_count):
            for j in range(col_count):
                pairs.append((i * col_count + j, (i ^ blk_step) * col_count + (j ^ col_step)))
        return lax.ppermute(value, ("blk", "col"), pairs)

    hops = [(1, 0)]
    reach = 2
    while reach < blk_count:
        hops.append((reach + 1, 0))
        reach *= 2
    reach = 1
    while reach < col_count:
        hops.append((1, reach))
        reach *= 2
    for hop in hops[:-1]:
        squares = squares + swap(squares, *hop)
    last = swap(squares, *hops[-1])
    limit = trust_radius * height * blk_count
    return call(
        functools.partial(scale, limit, col_blocks),
        0,
        shape(height, width),
        "svvvv" + "v" * odd,
        me,
        squares,
        last,
        keep,
        take,
        *mid_running,
    )


def solution(mesh):
    in_specs = (
        P(("parts", "blk"), None, None, None, None),
        P(("parts", "blk"), None, None),
        P(("parts", "blk"), None, None),
        P(("parts", "blk"), "col"),
        P(("parts", "blk"), "col"),
    )
    out_specs = P(("parts", "blk"), "col")
    run = functools.partial(body, (mesh.shape["blk"], mesh.shape["col"]))
    return jax.shard_map(run, mesh=mesh, in_specs=in_specs, out_specs=out_specs, check_vma=False)
```

time: 32.7 us -> 34.2 us (1.046)
  waiting for transfers between devices: 15.2 us -> 11 us
  Pallas kernels: 5.42 us -> 8.54 us
  starting transfers between devices: 9 us -> 10.5 us
  local copies, waits for them, and re-layouts: 2.78 us -> 3.7 us
    ppermute x3 -> x8, waiting for transfers between devices: 10.2 us -> 4.21 us  [move(): return lax.ppermute(value, 'blk', pairs)]
    ppermute x3 -> x8, starting transfers between devices: 2.94 us -> 6.34 us  [move(): return lax.ppermute(value, 'blk', pairs)]
    pallas_call x5 -> x8, Pallas kernels: 5.42 us -> 8.54 us  [call(): pl.pallas_call(kernel, out_shape=outs, in_specs=specs, out_specs=jax.tree...]
    reshape x0 -> x3, local copies, waits for them, and re-layouts: none -> 2.29 us  [the longest x1 0.76 us: body(): a_cols.reshape(-1)]
    ppermute x4, starting transfers between devices: 6.06 us -> 4.21 us  [swap(): return lax.ppermute(value, ('blk', 'col'), pairs)]
    ppermute x4, waiting for transfers between devices: 5.01 us -> 6.79 us  [swap(): return lax.ppermute(value, ('blk', 'col'), pairs)]
    unnamed x10 -> x4, local copies, waits for them, and re-layouts: 2.78 us -> 1.41 us
  transfers between devices with their start and end apart: 7 -> 12, of which waited for: 6 -> 6; matrix products, arithmetic and copies ran while one was open for 0% -> 7% of each run, Pallas kernels for 10% -> 19%
where the time goes in v2:
time: 34.2 us; the launch traced here: 34 us
  waiting for transfers between devices  11 us (32%)
  starting transfers between devices  10.5 us (31%)
  Pallas kernels  8.54 us (25%)
  local copies, waits for them, and re-layouts  3.7 us (11%)
    pallas_call x8, Pallas kernels, call(): pl.pallas_call(kernel, out_shape=outs, in_specs=specs, out_specs=jax.tree...  8.54 us
    ppermute x4, waiting for transfers between devices, swap(): return lax.ppermute(value, ('blk', 'col'), pairs)  6.79 us
    ppermute x8, starting transfers between devices, move(): return lax.ppermute(value, 'blk', pairs)  6.34 us
    ppermute x8, waiting for transfers between devices, move(): return lax.ppermute(value, 'blk', pairs)  4.21 us
    ppermute x4, starting transfers between devices, swap(): return lax.ppermute(value, ('blk', 'col'), pairs)  4.21 us
    unnamed x4, local copies, waits for them, and re-layouts  1.41 us
    reshape x1, local copies, waits for them, and re-layouts, body(): a_cols.reshape(-1)  0.76 us
    reshape x1, local copies, waits for them, and re-layouts, body(): pattern.reshape(-1)  0.76 us
  transfers between devices with their start and end apart: 12, of which 6 were waited for; matrix products, arithmetic and copies ran while one was open for 7% of the time, Pallas kernels for 19%

profile of v2, /device:TPU:0, one launch (start us, length us, event | category | flops | bytes accessed | tf_op | source)
XLA Modules:
  0.0 34.0 jit_solution(2491072360362643810)
XLA Ops:
  0.0 0.5 %collective-permute-start.1 = (f32[4,6,128,128]{3,2,1,0:T(8,128)}, f32[4,6,128,128]{3,2,1,0:T(8,128)S(1)}, u32[]{:S(2)}, u32[]{:S(2)}) collective-permute-start(f32[4,6,128,128]{3,2,1,0:T(8,128)} %bitcast.2), channel_id=1, source_target_pairs={{0,4},{4,0},{8,12},{12,8},{1,5},{5,1},{9,13},{13,9},{2,6},{6,2},{1... | collective-permute-start | bytes 4718600 | tf_op jit(solution)/shard_map/ppermute | solution.py:176
  0.5 0.1 collective-permute-start.2
  0.5 1.1 %shard_map.57 = (f32[384,128]{1,0:T(8,128)S(1)}, f32[384,128]{1,0:T(8,128)S(1)}, f32[384,128]{1,0:T(8,128)S(1)}) custom-call(s32[1]{0:T(128)} %bitcast.me_ref, f32[384,384]{1,0:T(8,128)} %b_ref.1), custom_call_target="tpu_custom_call" | custom-call | bytes 589828 | tf_op jit(solution)/shard_map/pallas_call | solution.py:153
  1.7 3.0 %collective-permute-start.5 = (f32[384,128]{1,0:T(8,128)S(1)}, f32[384,128]{1,0:T(8,128)S(1)}, u32[]{:S(2)}, u32[]{:S(2)}) collective-permute-start(f32[384,128]{1,0:T(8,128)S(1)} %get-tuple-element.35), channel_id=1, source_target_pairs={{0,8},{4,12},{8,0},{12,4},{1,9},{5,13},{9,1},{13,5},{2,10},{6,14},... | collective-permute-start | bytes 589832 | tf_op jit(solution)/shard_map/ppermute | solution.py:176
  4.7 0.1 collective-permute-start.3
  4.7 0.8 %reshape.13 = s32[24]{0:T(128)S(1)} reshape(s32[1,4,6]{2,1,0:T(4,128)} %param.6) | data formatting | bytes 192 | tf_op jit(solution)/shard_map/reshape | solution.py:194
  5.5 0.8 %reshape.14 = s32[24]{0:T(128)S(1)} reshape(s32[1,4,6]{2,1,0:T(4,128)} %param.7) | data formatting | bytes 192 | tf_op jit(solution)/shard_map/reshape | solution.py:194
  6.3 0.8 %reshape.15 = s32[9]{0:T(128)S(1)} reshape(s32[3,3]{1,0:T(4,128)} %param.9) | data formatting | bytes 72 | tf_op jit(solution)/shard_map/reshape | solution.py:194
  7.0 3.3 %collective-permute-done.5.b_ref = f32[384,128]{1,0:T(8,128)S(1)} collective-permute-done((f32[384,128]{1,0:T(8,128)S(1)}, f32[384,128]{1,0:T(8,128)S(1)}, u32[]{:S(2)}, u32[]{:S(2)}) %collective-permute-start.5) | collective-permute-done | bytes 196640 | tf_op jit(solution)/shard_map/ppermute | solution.py:176
  10.4 0.1 pad_add_fusion.own_ids.ids
  10.5 0.5 %collective-permute-start = (s32[57]{0:T(128)S(1)}, s32[57]{0:T(128)S(1)}, u32[]{:S(2)}, u32[]{:S(2)}) collective-permute-start(s32[57]{0:T(128)S(1)} %pad_add_fusion.own_ids.ids), channel_id=1, source_target_pairs={{0,4},{4,0},{8,12},{12,8},{1,5},{5,1},{9,13},{13,9},{2,6},{6,2},{1... | collective-permute-start | bytes 692 | tf_op jit(solution)/shard_map/ppermute | solution.py:176
  11.0 0.9 %collective-permute-done.near_ids = s32[57]{0:T(128)S(1)} collective-permute-done((s32[57]{0:T(128)S(1)}, s32[57]{0:T(128)S(1)}, u32[]{:S(2)}, u32[]{:S(2)}) %collective-permute-start) | collective-permute-done | bytes 260 | tf_op jit(solution)/shard_map/ppermute | solution.py:176
  11.8 1.9 %collective-permute-start.4 = (f32[384,128]{1,0:T(8,128)S(1)}, f32[384,128]{1,0:T(8,128)S(1)}, u32[]{:S(2)}, u32[]{:S(2)}) collective-permute-start(f32[384,128]{1,0:T(8,128)S(1)} %get-tuple-element.33), channel_id=1, source_target_pairs={{0,12},{4,8},{8,4},{12,0},{1,13},{5,9},{9,5},{13,1},{2,14},{6,10},... | collective-permute-start | bytes 589832 | tf_op jit(solution)/shard_map/ppermute | solution.py:176
  13.8 0.0 collective-permute-done.1.near_ref
  13.8 1.4 %copy-done.1 = f32[1,4,6,128,128]{4,3,2,1,0:T(8,128)S(1)} copy-done((f32[1,4,6,128,128]{4,3,2,1,0:T(8,128)S(1)}, f32[1,4,6,128,128]{4,3,2,1,0:T(8,128)}, u32[]{:S(2)}) %copy-start.1) | copy-done | bytes 1572888
  15.2 1.7 %shard_map.55 = (bf16[768,384]{1,0:T(8,128)(2,1)S(1)}, bf16[768,384]{1,0:T(8,128)(2,1)S(1)}, bf16[768,384]{1,0:T(8,128)(2,1)S(1)}, bf16[768,384]{1,0:T(8,128)(2,...) custom-call(s32[1]{0:T(128)} %bitcast.me_ref, ...), custom_call_target="tpu_custom_call" | custom-call | bytes 3146188 | tf_op jit(solution)/shard_map/pallas_call | solution.py:153
  16.8 0.0 collective-permute-done.2.near_b
  16.8 1.6 %shard_map.56 = (f32[768,128]{1,0:T(8,128)S(1)}, f32[384,128]{1,0:T(8,128)S(1)}) custom-call(s32[1]{0:T(128)} %bitcast.me_ref, bf16[768,384]{1,0:T(8,128)(2,1)S(1)} %get-tuple-element.23.own_high, bf16[768,384]{1,0:T(8,128)(2,1)S(1)} %get-tuple-element.24.own_low, f32[384,384]{1,0:T(8,128)S(1)} %copy-done, bf16[768,384]{1,0:T(8,128)(2,1)S(1)} %get-tuple-element.25.near_high, ...), custom_call_target="tpu_custom_call" | custom-call | flops 679477248 | bytes 3538948 | tf_op jit(solution)/shard_map/pallas_call | solution.py:153
  18.5 0.4 %shard_map.59.running_ref = f32[384,128]{1,0:T(8,128)S(1)} custom-call(f32[384,128]{1,0:T(8,128)S(1)} %get-tuple-element.34.running_ref, bf16[768,384]{1,0:T(8,128)(2,1)S(1)} %get-tuple-element.28.high_ref, bf16[768,384]{1,0:T(8,128)(2,1)S(1)} %get-tuple-element.29.low_ref, f32[384,128]{1,0:T(8,128)S(1)} %collective-permute-done.5.b_ref), custom_call_target="tpu_custom_call" | custom-call | flops 113246208 | bytes 1572864 | tf_op jit(solution)/shard_map/pallas_call | solution.py:153
  18.9 1.0 %shard_map.60 = (f32[384,128]{1,0:T(8,128)S(1)}, f32[1,128]{1,0:T(1,128)S(1)}) custom-call(s32[57]{0:T(128)S(1)} %pad_add_fusion.own_ids.ids, f32[384,128]{1,0:T(8,128)S(1)} %shard_map.59.running_ref, bf16[768,384]{1,0:T(8,128)(2,1)S(1)} %get-tuple-element.31.high_ref.refs_1_, bf16[768,384]{1,0:T(8,128)(2,1)S(1)} %get-tuple-element.32.low_ref.refs_2_, ...), custom_call_target="tpu_custom_call" | custom-call | flops 113246208 | bytes 1573092 | tf_op jit(solution)/shard_map/pallas_call | solution.py:153
  19.8 0.6 %shard_map.58.refs_0_ = f32[768,128]{1,0:T(8,128)S(1)} custom-call(f32[768,128]{1,0:T(8,128)S(1)} %get-tuple-element.27.running_ref, bf16[768,384]{1,0:T(8,128)(2,1)S(1)} %get-tuple-element.28.high_ref, bf16[768,384]{1,0:T(8,128)(2,1)S(1)} %get-tuple-element.29.low_ref, f32[384,128]{1,0:T(8,128)S(1)} %collective-permute-done.3.b_ref), custom_call_target="tpu_custom_call" | custom-call | flops 226492416 | bytes 1769472 | tf_op jit(solution)/shard_map/pallas_call | solution.py:153
  20.5 1.2 %shard_map.61 = (f32[384,128]{1,0:T(8,128)S(1)}, f32[384,128]{1,0:T(8,128)S(1)}, f32[1,128]{1,0:T(1,128)S(1)}) custom-call(s32[1]{0:T(128)} %bitcast.me_ref, s32[57]{0:T(128)S(1)} %pad_add_fusion.own_ids.ids, s32[57]{0:T(128)S(1)} %collective-permute-done.near_ids, f32[768,128]{1,0:T(8,128)S(1)} %shard_map.58.refs_0_, ...), custom_call_target="tpu_custom_call" | custom-call | flops 226492416 | bytes 1770444 | tf_op jit(solution)/shard_map/pallas_call | solution.py:153
  21.7 0.3 collective-permute-start.11
  22.0 0.3 collective-permute-start.7
  22.3 0.9 %collective-permute-done.7 = f32[1,128]{1,0:T(1,128)S(1)} collective-permute-done((f32[1,128]{1,0:T(1,128)S(1)}, f32[1,128]{1,0:T(1,128)S(1)}, u32[]{:S(2)}, u32[]{:S(2)}) %collective-permute-start.7) | collective-permute-done | bytes 544 | tf_op jit(solution)/shard_map/ppermute | solution.py:266
  23.2 0.1 collective-permute-start.8
  23.3 2.9 %collective-permute-done.8 = f32[1,128]{1,0:T(1,128)S(1)} collective-permute-done((f32[1,128]{1,0:T(1,128)S(1)}, f32[1,128]{1,0:T(1,128)S(1)}, u32[]{:S(2)}, u32[]{:S(2)}) %collective-permute-start.8) | collective-permute-done | bytes 544 | tf_op jit(solution)/shard_map/ppermute | solution.py:266
  26.2 1.4 %collective-permute-start.9 = (f32[1,128]{1,0:T(1,128)S(1)}, f32[1,128]{1,0:T(1,128)S(1)}, u32[]{:S(2)}, u32[]{:S(2)}) collective-permute-start(f32[1,128]{1,0:T(1,128)S(1)} %add.10), channel_id=1, source_target_pairs={{0,5},{1,4},{2,7},{3,6},{4,1},{5,0},{6,3},{7,2},{8,13},{9,12},{10,... | collective-permute-start | bytes 1544 | tf_op jit(solution)/shard_map/ppermute | solution.py:266
  27.6 1.5 %collective-permute-done.9 = f32[1,128]{1,0:T(1,128)S(1)} collective-permute-done((f32[1,128]{1,0:T(1,128)S(1)}, f32[1,128]{1,0:T(1,128)S(1)}, u32[]{:S(2)}, u32[]{:S(2)}) %collective-permute-start.9) | collective-permute-done | bytes 544 | tf_op jit(solution)/shard_map/ppermute | solution.py:266
  29.1 2.4 %collective-permute-start.10 = (f32[1,128]{1,0:T(1,128)S(1)}, f32[1,128]{1,0:T(1,128)S(1)}, u32[]{:S(2)}, u32[]{:S(2)}) collective-permute-start(f32[1,128]{1,0:T(1,128)S(1)} %add.11.one_ref), channel_id=1, source_target_pairs={{0,6},{1,7},{2,4},{3,5},{4,2},{5,3},{6,0},{7,1},{8,14},{9,15},{10,... | collective-permute-start | bytes 1544 | tf_op jit(solution)/shard_map/ppermute | solution.py:266
  31.6 1.4 %collective-permute-done.10.two_ref = f32[1,128]{1,0:T(1,128)S(1)} collective-permute-done((f32[1,128]{1,0:T(1,128)S(1)}, f32[1,128]{1,0:T(1,128)S(1)}, u32[]{:S(2)}, u32[]{:S(2)}) %collective-permute-start.10) | collective-permute-done | bytes 544 | tf_op jit(solution)/shard_map/ppermute | solution.py:266
  33.0 1.0 %shard_map.62 = f32[384,384]{1,0:T(8,128)} custom-call(s32[1]{0:T(128)} %bitcast.me_ref, f32[1,128]{1,0:T(1,128)S(1)} %add.11.one_ref, f32[1,128]{1,0:T(1,128)S(1)} %collective-permute-done.10.two_ref, f32[384,128]{1,0:T(8,128)S(1)} %get-tuple-element.38.keep_ref, f32[384,128]{1,0:T(8,128)S(1)} %collective-permute-done.11.take_ref, ...), custom_call_target="tpu_custom_call" | custom-call | bytes 590852 | tf_op jit(solution)/shard_map/pallas_call | solution.py:153
  (11 shorter events, 0.0 us)
Async XLA Ops:
  0.0 13.8 %collective-permute-start.1 = (f32[4,6,128,128]{3,2,1,0:T(8,128)}, f32[4,6,128,128]{3,2,1,0:T(8,128)S(1)}, u32[]{:S(2)}, u32[]{:S(2)}) collective-permute-start(f32[4,6,128,128]{3,2,1,0:T(8,128)} %bitcast.2), channel_id=1, source_target_pairs={{0,4},{4,0},{8,12},{12,8},{1,5},{5,1},{9,13},{13,9},{2,6},{6,2},{1... | collective-permute-start | bytes 4718600 | tf_op jit(solution)/shard_map/ppermute | solution.py:176
  0.5 16.4 %collective-permute-start.2 = (f32[384,384]{1,0:T(8,128)}, f32[384,384]{1,0:T(8,128)S(1)}, u32[]{:S(2)}, u32[]{:S(2)}) collective-permute-start(f32[384,384]{1,0:T(8,128)} %b_ref.1), channel_id=1, source_target_pairs={{0,4},{4,0},{8,12},{12,8},{1,5},{5,1},{9,13},{13,9},{2,6},{6,2},{1... | collective-permute-start | bytes 1769480 | tf_op jit(solution)/shard_map/ppermute | solution.py:176
  1.7 8.7 %collective-permute-start.5 = (f32[384,128]{1,0:T(8,128)S(1)}, f32[384,128]{1,0:T(8,128)S(1)}, u32[]{:S(2)}, u32[]{:S(2)}) collective-permute-start(f32[384,128]{1,0:T(8,128)S(1)} %get-tuple-element.35), channel_id=1, source_target_pairs={{0,8},{4,12},{8,0},{12,4},{1,9},{5,13},{9,1},{13,5},{2,10},{6,14},... | collective-permute-start | bytes 589832 | tf_op jit(solution)/shard_map/ppermute | solution.py:176
  4.7 15.2 %collective-permute-start.3 = (f32[384,128]{1,0:T(8,128)S(1)}, f32[384,128]{1,0:T(8,128)S(1)}, u32[]{:S(2)}, u32[]{:S(2)}) collective-permute-start(f32[384,128]{1,0:T(8,128)S(1)} %get-tuple-element.30), channel_id=1, source_target_pairs={{0,8},{4,12},{8,0},{12,4},{1,9},{5,13},{9,1},{13,5},{2,10},{6,14},... | collective-permute-start | bytes 589832 | tf_op jit(solution)/shard_map/ppermute | solution.py:176
  10.4 8.5 %collective-permute-start.6 = (f32[384,128]{1,0:T(8,128)S(1)}, f32[384,128]{1,0:T(8,128)S(1)}, u32[]{:S(2)}, u32[]{:S(2)}) collective-permute-start(f32[384,128]{1,0:T(8,128)S(1)} %collective-permute-done.5.b_ref), channel_id=1, source_target_pairs={{0,4},{4,0},{8,12},{12,8},{1,5},{5,1},{9,13},{13,9},{2,6},{6,2},{1... | collective-permute-start | bytes 589832 | tf_op jit(solution)/shard_map/ppermute | solution.py:176
  10.5 1.4 %collective-permute-start = (s32[57]{0:T(128)S(1)}, s32[57]{0:T(128)S(1)}, u32[]{:S(2)}, u32[]{:S(2)}) collective-permute-start(s32[57]{0:T(128)S(1)} %pad_add_fusion.own_ids.ids), channel_id=1, source_target_pairs={{0,4},{4,0},{8,12},{12,8},{1,5},{5,1},{9,13},{13,9},{2,6},{6,2},{1... | collective-permute-start | bytes 692 | tf_op jit(solution)/shard_map/ppermute | solution.py:176
  11.8 5.0 %copy-start = (f32[384,384]{1,0:T(8,128)S(1)}, f32[384,384]{1,0:T(8,128)}, u32[]{:S(2)}) copy-start(f32[384,384]{1,0:T(8,128)} %b_ref.1) | copy-start | bytes 1769476
  11.8 8.7 %collective-permute-start.4 = (f32[384,128]{1,0:T(8,128)S(1)}, f32[384,128]{1,0:T(8,128)S(1)}, u32[]{:S(2)}, u32[]{:S(2)}) collective-permute-start(f32[384,128]{1,0:T(8,128)S(1)} %get-tuple-element.33), channel_id=1, source_target_pairs={{0,12},{4,8},{8,4},{12,0},{1,13},{5,9},{9,5},{13,1},{2,14},{6,10},... | collective-permute-start | bytes 589832 | tf_op jit(solution)/shard_map/ppermute | solution.py:176
  13.8 1.4 %copy-start.1 = (f32[1,4,6,128,128]{4,3,2,1,0:T(8,128)S(1)}, f32[1,4,6,128,128]{4,3,2,1,0:T(8,128)}, u32[]{:S(2)}) copy-start(f32[1,4,6,128,128]{4,3,2,1,0:T(8,128)} %param.5) | copy-start | bytes 4718596
  21.7 11.3 %collective-permute-start.11 = (f32[384,128]{1,0:T(8,128)S(1)}, f32[384,128]{1,0:T(8,128)S(1)}, u32[]{:S(2)}, u32[]{:S(2)}) collective-permute-start(f32[384,128]{1,0:T(8,128)S(1)} %get-tuple-element.39), channel_id=1, source_target_pairs={{0,4},{4,0},{8,12},{12,8},{1,5},{5,1},{9,13},{13,9},{2,6},{6,2},{1... | collective-permute-start | bytes 589832 | tf_op jit(solution)/shard_map/ppermute | solution.py:176
  22.0 1.2 %collective-permute-start.7 = (f32[1,128]{1,0:T(1,128)S(1)}, f32[1,128]{1,0:T(1,128)S(1)}, u32[]{:S(2)}, u32[]{:S(2)}) collective-permute-start(f32[1,128]{1,0:T(1,128)S(1)} %get-tuple-element.37), channel_id=1, source_target_pairs={{0,4},{1,5},{2,6},{3,7},{4,0},{5,1},{6,2},{7,3},{8,12},{9,13},{10,... | collective-permute-start | bytes 1544 | tf_op jit(solution)/shard_map/ppermute | solution.py:266
  23.2 3.0 %collective-permute-start.8 = (f32[1,128]{1,0:T(1,128)S(1)}, f32[1,128]{1,0:T(1,128)S(1)}, u32[]{:S(2)}, u32[]{:S(2)}) collective-permute-start(f32[1,128]{1,0:T(1,128)S(1)} %add.9), channel_id=1, source_target_pairs={{0,12},{1,13},{2,14},{3,15},{4,8},{5,9},{6,10},{7,11},{8,4},{9,5},... | collective-permute-start | bytes 1544 | tf_op jit(solution)/shard_map/ppermute | solution.py:266
  26.2 3.0 %collective-permute-start.9 = (f32[1,128]{1,0:T(1,128)S(1)}, f32[1,128]{1,0:T(1,128)S(1)}, u32[]{:S(2)}, u32[]{:S(2)}) collective-permute-start(f32[1,128]{1,0:T(1,128)S(1)} %add.10), channel_id=1, source_target_pairs={{0,5},{1,4},{2,7},{3,6},{4,1},{5,0},{6,3},{7,2},{8,13},{9,12},{10,... | collective-permute-start | bytes 1544 | tf_op jit(solution)/shard_map/ppermute | solution.py:266
  29.1 3.9 %collective-permute-start.10 = (f32[1,128]{1,0:T(1,128)S(1)}, f32[1,128]{1,0:T(1,128)S(1)}, u32[]{:S(2)}, u32[]{:S(2)}) collective-permute-start(f32[1,128]{1,0:T(1,128)S(1)} %add.11.one_ref), channel_id=1, source_target_pairs={{0,6},{1,7},{2,4},{3,5},{4,2},{5,3},{6,0},{7,1},{8,14},{9,15},{10,... | collective-permute-start | bytes 1544 | tf_op jit(solution)/shard_map/ppermute | solution.py:266

commit v3 on v2

v3 whole, which is shorter than its diff:
```python
import functools

import jax
import jax.numpy as jnp
from jax import lax
from jax.experimental import pallas as pl
from jax.experimental.pallas import tpu as pltpu
from jax.sharding import PartitionSpec as P

trust_radius = 0.5
LIMIT = 12 << 20
SHARE = 1000
VM = pl.BlockSpec(memory_space=pltpu.VMEM)
SM = pl.BlockSpec(memory_space=pltpu.SMEM)
HBM = pl.BlockSpec(memory_space=pltpu.HBM)


def shape(*dims, dtype=jnp.float32):
    return jax.ShapeDtypeStruct(dims, dtype)


def split(value):
    high = value.astype(jnp.bfloat16)
    low = (value - high.astype(jnp.float32)).astype(jnp.bfloat16)
    return high, low


def product(high_a, low_a, b):
    high_b, low_b = split(b)
    left = jnp.concatenate([high_a, high_a, low_a], axis=1)
    right = jnp.concatenate([high_b, low_b, high_b], axis=0)
    return jnp.dot(left, right, preferred_element_type=jnp.float32)


def columns(core, side, col_blocks, size):
    half = col_blocks // 2
    which = core if side == 0 else 1 - core
    return pl.ds(pl.multiple_of(which * ((col_blocks - half) * size), size), half * size)


def middle_of(col_blocks, size):
    half = col_blocks // 2
    return pl.ds(half * size, size)


def cut(col_blocks, me_ref, b_ref, *refs):
    outs, sems = refs[:-1], refs[-1]
    size = b_ref.shape[1] // col_blocks
    core = lax.rem(me_ref[0], 2)
    where = [columns(core, 0, col_blocks, size), columns(core, 1, col_blocks, size)]
    if len(outs) > 2:
        where.append(middle_of(col_blocks, size))
    copies = [pltpu.make_async_copy(b_ref.at[:, w], out, sems.at[i]) for i, (w, out) in enumerate(zip(where, outs))]
    for copy in copies:
        copy.start()
    for copy in copies:
        copy.wait()


def pack(size, rows_ref, cols_ref, pattern_ref, out_ref):
    tile = out_ref.shape
    place = lax.broadcasted_iota(jnp.int32, tile, 0) * size + lax.broadcasted_iota(jnp.int32, tile, 1)
    found = jnp.zeros(tile, jnp.int32)
    at = 0
    for ref in (rows_ref, cols_ref, pattern_ref):
        for i in range(ref.shape[0]):
            for j in range(ref.shape[1]):
                found = jnp.where(place == at, ref[i, j], found)
                at += 1
    out_ref[...] = found.astype(jnp.float32)


def prepare(sizes, me_ref, rows_ref, cols_ref, pattern_ref, near_ids, own_hbm, near_ref, mask_ref, *refs):
    *dense_refs, own_ref, sem = refs
    half, odd = sizes
    groups, slots, size = own_ref.shape[0], own_ref.shape[1], own_ref.shape[-1]
    fetch = pltpu.make_async_copy(own_hbm, own_ref, sem)
    fetch.start()
    height = dense_refs[0].shape[0] // 2
    row_blocks, col_blocks = pattern_ref.shape
    chips = groups // 2
    chip, core = lax.div(me_ref[0], 2), lax.rem(me_ref[0], 2)

    def near_id(at):
        return near_ids[at // size, at % size]

    def near_slot(kind, group, slot):
        at = (kind * groups + group) * slots + slot
        return near_ids[lax.div(at, size), lax.rem(at, size)].astype(jnp.int32)

    for ref in dense_refs:
        ref[...] = jnp.zeros_like(ref)
    for blocks_ref, top in ((near_ref, height), (own_ref, 0)):
        if top == 0:
            fetch.wait()
        for rel in range(groups):
            high_ref, low_ref = dense_refs[2 * rel], dense_refs[2 * rel + 1]
            group = 2 * lax.rem(chip + chips - rel // 2, chips) + lax.rem(core + rel, 2)
            for slot in range(slots):
                if top:
                    row, col = near_slot(0, group, slot), near_slot(1, group, slot)
                else:
                    row, col = rows_ref[group, slot], cols_ref[group, slot]

                @pl.when(col >= 0)
                def _():
                    high, low = split(blocks_ref[group, slot])
                    row_at = pl.ds(pl.multiple_of(row * size + top, size), size)
                    col_at = pl.ds(pl.multiple_of(col * size, size), size)
                    high_ref[row_at, col_at] = high
                    low_ref[row_at, col_at] = low

    def write(at, value):
        mask_ref[at : at + 1, :] = jnp.full((1, size), value, jnp.float32)

    at = 0
    for i in range(row_blocks):
        for j in range(half):
            write(at, pattern_ref[i, core * (col_blocks - half) + j].astype(jnp.float32))
            at += 1
    first = 2 * groups * slots
    for i in range(row_blocks):
        for j in range(half):
            left, right = near_id(first + i * col_blocks + j), near_id(first + (i + 1) * col_blocks - half + j)
            write(at, jnp.where(core == 0, left, right))
            at += 1
    if odd:
        for i in range(row_blocks):
            write(at, pattern_ref[i, half].astype(jnp.float32))
            at += 1
    write(at, core.astype(jnp.float32))


def start_sum(mask_ref, own_high, own_low, near_high, near_low, near_b, *refs):
    pieces, outs = refs[: len(refs) // 2], refs[len(refs) // 2 :]
    height, width = pieces[0].shape
    core = mask_ref[mask_ref.shape[0] - 1, 0:1].reshape(1, 1)
    left, right = near_b[:, :width], near_b[:, near_b.shape[1] - width :]
    near_pieces = [jnp.where(core == 0.0, left, right), near_b[:, width : near_b.shape[1] - width]]
    for own_b, piece, out_ref in zip(pieces, near_pieces, outs):
        rows = out_ref.shape[0]
        out_ref[...] = product(own_high[:rows], own_low[:rows], own_b[...]) + product(
            near_high[:rows], near_low[:rows], piece
        )


def add_sum(running_ref, high_ref, low_ref, b_ref, out_ref):
    rows = running_ref.shape[0]
    out_ref[...] = running_ref[...] + product(high_ref[:rows], low_ref[:rows], b_ref[...])


def masked(value, mask_ref, first, out_ref, squares):
    size = mask_ref.shape[1]
    across = value.shape[1] // size
    for i in range(value.shape[0] // size):
        for j in range(across):
            at = first + i * across + j
            part = value[i * size : (i + 1) * size, j * size : (j + 1) * size] * mask_ref[at : at + 1, :]
            out_ref[i * size : (i + 1) * size, j * size : (j + 1) * size] = part
            squares = squares + jnp.sum((part * part).reshape(size // 8, 8, size), axis=0)
    return squares


def finish_middle(mask_ref, running_ref, high_ref, low_ref, b_ref, out_ref, squares_ref):
    height, size = running_ref.shape
    total = running_ref[...] + product(high_ref[:height], low_ref[:height], b_ref[...])
    first = mask_ref.shape[0] - 1 - height // size
    squares_ref[...] = masked(total, mask_ref, first, out_ref, jnp.zeros((8, size), jnp.float32))


def finish(mask_ref, running_ref, high_ref, low_ref, b_ref, *refs):
    *before, keep_ref, give_ref, squares_ref = refs
    height, size = keep_ref.shape[0], mask_ref.shape[1]
    count = keep_ref.shape[0] // size * (keep_ref.shape[1] // size)
    total = running_ref[...] + product(high_ref[...], low_ref[...], b_ref[...])
    squares = before[0][...] if before else jnp.zeros((8, size), jnp.float32)
    squares = masked(total[:height], mask_ref, 0, keep_ref, squares)
    squares = masked(total[height:], mask_ref, count, give_ref, squares)
    squares_ref[...] = jnp.sum(squares, axis=0, keepdims=True)


def scale(limit, mask_ref, one_ref, two_ref, keep_ref, take_ref, *refs):
    *mid_refs, out_ref = refs
    width = keep_ref.shape[1]
    squares = jnp.sum(one_ref[...] + two_ref[...], axis=1, keepdims=True)
    factor = -jnp.minimum(1.0, limit / jnp.sqrt(squares + 1e-06))
    core = mask_ref[mask_ref.shape[0] - 1, 0:1].reshape(1, 1)
    keep, take = keep_ref[...] * factor, take_ref[...] * factor
    out_ref[:, :width] = jnp.where(core == 0.0, keep, take)
    out_ref[:, out_ref.shape[1] - width :] = jnp.where(core == 0.0, take, keep)
    for mid_ref in mid_refs:
        out_ref[:, width : width + mid_ref.shape[1]] = mid_ref[...] * factor


def call(kernel, flops, outs, specs, *args, scratch=()):
    specs = [{"s": SM, "v": VM, "h": HBM}[s] for s in specs]
    place = pltpu.with_memory_space_constraint
    given = [s is SM and a.ndim == 2 and a.dtype == jnp.int32 for a, s in zip(args, specs)]
    args = [place(a, pltpu.HBM if g else s.memory_space) for a, s, g in zip(args, specs, given)]
    return pl.pallas_call(
        kernel,
        out_shape=outs,
        in_specs=specs,
        out_specs=jax.tree.map(lambda _: VM, outs),
        scratch_shapes=scratch,
        compiler_params=pltpu.CompilerParams(vmem_limit_bytes=LIMIT),
        cost_estimate=pl.CostEstimate(flops=flops // SHARE, bytes_accessed=0, transcendentals=0),
    )(*args)


def body(sizes, a_blocks, a_rows, a_cols, b_panel, pattern):
    blk_count, col_count = sizes
    chips = blk_count // 2
    blocks = a_blocks[0]
    size = blocks.shape[-1]
    height, width = b_panel.shape
    row_blocks, col_blocks = pattern.shape
    half, odd = col_blocks // 2, col_blocks % 2
    me = lax.axis_index("blk").astype(jnp.int32).reshape(1)

    def move(value, chip_step, core_flip):
        pairs = [(i, (i // 2 + chip_step) % chips * 2 + (i % 2) ^ core_flip) for i in range(blk_count)]
        return lax.ppermute(value, "blk", pairs)

    piece = shape(height, half * size)
    middle = shape(height, size)
    side, other, *mids = call(
        functools.partial(cut, col_blocks),
        0,
        [piece, piece] + [middle] * odd,
        "sh",
        me,
        b_panel,
        scratch=[pltpu.SemaphoreType.DMA((2 + odd,))],
    )
    steps = range(1, chips)
    far_mids = [[move(mid, step, 0) for mid in mids] for step in steps]
    far_sides = [move(side, step, 0) for step in steps]
    far_others = [move(other, step, 1) for step in steps]

    rows, cols = a_rows[0], a_cols[0]
    near_blocks = move(blocks, 0, 1)
    near_b = move(b_panel, 0, 1)
    packed = call(functools.partial(pack, size), 0, shape(8, size), "sss", rows, cols, pattern)
    near_ids = move(packed, 0, 1)
    mask, *dense = call(
        functools.partial(prepare, (half, odd)),
        0,
        [shape((2 * half + odd) * row_blocks + 1, size)]
        + [shape(2 * height, height, dtype=jnp.bfloat16)] * (2 * blk_count),
        "ssssshv",
        me,
        rows,
        cols,
        pattern,
        near_ids,
        blocks,
        near_blocks,
        scratch=[pltpu.VMEM(blocks.shape, jnp.float32), pltpu.SemaphoreType.DMA],
    )
    flops = 6 * height * height * size
    wide = shape(2 * height, half * size)
    running, *mid_running = call(
        start_sum,
        4 * flops * half + 2 * flops * odd,
        [wide] + [middle] * odd,
        "vvvvvvv" + "v" * odd,
        mask,
        *dense[0:4],
        near_b,
        side,
        *mids,
    )
    before = []
    for at, step in enumerate(steps):
        same, cross = dense[4 * step : 4 * step + 2], dense[4 * step + 2 : 4 * step + 4]
        for far_mid in far_mids[at]:
            far_mid, running = lax.optimization_barrier((far_mid, running))
            forward = move(far_mid, 0, 1)
            mid_running = [call(add_sum, flops, middle, "vvvv", *mid_running, *same, far_mid)]
            if step < chips - 1:
                mid_running = [call(add_sum, flops, middle, "vvvv", *mid_running, *cross, forward)]
            else:
                *mid_running, squares = call(
                    finish_middle,
                    flops,
                    [middle, shape(8, size)],
                    "vvvvv",
                    mask,
                    *mid_running,
                    *cross,
                    forward,
                )
                before = [squares]
        running = call(add_sum, 2 * flops * half, wide, "vvvv", running, *same, far_sides[at])
        if step < chips - 1:
            running = call(add_sum, 2 * flops * half, wide, "vvvv", running, *cross, far_others[at])
    keep, give, squares = call(
        finish,
        2 * flops * half,
        [piece, piece, shape(1, size)],
        "vvvvv" + "v" * odd,
        mask,
        running,
        *cross,
        far_others[-1],
        *before,
    )
    take = move(give, 0, 1)

    def swap(value, blk_step, col_step):
        pairs = []
        for i in range(blk_count):
            for j in range(col_count):
                pairs.append((i * col_count + j, (i ^ blk_step) * col_count + (j ^ col_step)))
        return lax.ppermute(value, ("blk", "col"), pairs)

    hops = [(1, 0)]
    reach = 2
    while reach < blk_count:
        hops.append((reach + 1, 0))
        reach *= 2
    reach = 1
    while reach < col_count:
        hops.append((1, reach))
        reach *= 2
    for hop in hops[:-1]:
        squares = squares + swap(squares, *hop)
    last = swap(squares, *hops[-1])
    limit = trust_radius * height * blk_count
    return call(
        functools.partial(scale, limit),
        0,
        shape(height, width),
        "vvvvv" + "v" * odd,
        mask,
        squares,
        last,
        keep,
        take,
        *mid_running,
    )


def solution(mesh):
    in_specs = (
        P(("parts", "blk"), None, None, None, None),
        P(("parts", "blk"), None, None),
        P(("parts", "blk"), None, None),
        P(("parts", "blk"), "col"),
        P(("parts", "blk"), "col"),
    )
    out_specs = P(("parts", "blk"), "col")
    run = functools.partial(body, (mesh.shape["blk"], mesh.shape["col"]))
    return jax.shard_map(run, mesh=mesh, in_specs=in_specs, out_specs=out_specs, check_vma=False)
```

time: 34.2 us -> 31.1 us (0.909)
  local copies, waits for them, and re-layouts: 3.7 us -> 0 us
  waiting for transfers between devices: 11 us -> 9.94 us
  starting transfers between devices: 10.5 us -> 11.5 us
  Pallas kernels: 8.54 us -> 9.22 us
    reshape x3 -> x0, local copies, waits for them, and re-layouts: 2.29 us -> none  [the longest x1 0.76 us: body(): a_cols.reshape(-1)]
    ppermute x4, waiting for transfers between devices: 6.79 us -> 5.11 us  [swap(): return lax.ppermute(value, ('blk', 'col'), pairs)]
    ppermute x4, starting transfers between devices: 4.21 us -> 5.84 us  [swap(): return lax.ppermute(value, ('blk', 'col'), pairs)]
    unnamed x4 -> x0, local copies, waits for them, and re-layouts: 1.41 us -> none
    pallas_call x8 -> x9, Pallas kernels: 8.54 us -> 9.22 us  [call(): pl.pallas_call(kernel, out_shape=outs, in_specs=specs, out_specs=jax.tree...]
    ppermute x8, starting transfers between devices: 6.34 us -> 5.7 us  [move(): return lax.ppermute(value, 'blk', pairs)]
    ppermute x8, waiting for transfers between devices: 4.21 us -> 4.83 us  [move(): return lax.ppermute(value, 'blk', pairs)]
  transfers between devices with their start and end apart: 12 -> 12, of which waited for: 6 -> 7; matrix products, arithmetic and copies ran while one was open for 7% -> 0% of each run, Pallas kernels for 19% -> 25%
where the time goes in v3:
time: 31.1 us; the launch traced here: 30.8 us
  starting transfers between devices  11.5 us (37%)
  waiting for transfers between devices  9.94 us (32%)
  Pallas kernels  9.22 us (30%)
    pallas_call x9, Pallas kernels, call(): pl.pallas_call(kernel, out_shape=outs, in_specs=specs, out_specs=jax.tree...  9.22 us
    ppermute x4, starting transfers between devices, swap(): return lax.ppermute(value, ('blk', 'col'), pairs)  5.84 us
    ppermute x8, starting transfers between devices, move(): return lax.ppermute(value, 'blk', pairs)  5.7 us
    ppermute x4, waiting for transfers between devices, swap(): return lax.ppermute(value, ('blk', 'col'), pairs)  5.11 us
    ppermute x8, waiting for transfers between devices, move(): return lax.ppermute(value, 'blk', pairs)  4.83 us
  transfers between devices with their start and end apart: 12, of which 7 were waited for; matrix products, arithmetic and copies ran while one was open for 0% of the time, Pallas kernels for 25%

profile of v3, /device:TPU:0, one launch (start us, length us, event | category | flops | bytes accessed | tf_op | source)
XLA Modules:
  0.0 30.8 jit_solution(7312900077934783215)
XLA Ops:
  0.0 0.5 %collective-permute-start.1 = (f32[4,6,128,128]{3,2,1,0:T(8,128)}, f32[4,6,128,128]{3,2,1,0:T(8,128)S(1)}, u32[]{:S(2)}, u32[]{:S(2)}) collective-permute-start(f32[4,6,128,128]{3,2,1,0:T(8,128)} %bitcast.4), channel_id=1, source_target_pairs={{0,4},{4,0},{8,12},{12,8},{1,5},{5,1},{9,13},{13,9},{2,6},{6,2},{1... | collective-permute-start | bytes 4718600 | tf_op jit(solution)/shard_map/ppermute | solution.py:223
  0.5 0.1 collective-permute-start.3
  0.5 1.1 %shard_map.57 = (f32[384,128]{1,0:T(8,128)S(1)}, f32[384,128]{1,0:T(8,128)S(1)}, f32[384,128]{1,0:T(8,128)S(1)}) custom-call(s32[1]{0:T(128)} %bitcast.me_ref, f32[384,384]{1,0:T(8,128)} %b_ref.1), custom_call_target="tpu_custom_call" | custom-call | tf_op jit(solution)/shard_map/pallas_call | solution.py:200
  1.7 3.0 %collective-permute-start.2 = (f32[384,128]{1,0:T(8,128)S(1)}, f32[384,128]{1,0:T(8,128)S(1)}, u32[]{:S(2)}, u32[]{:S(2)}) collective-permute-start(f32[384,128]{1,0:T(8,128)S(1)} %get-tuple-element.27.refs_1_), channel_id=1, source_target_pairs={{0,8},{4,12},{8,0},{12,4},{1,9},{5,13},{9,1},{13,5},{2,10},{6,14},... | collective-permute-start | bytes 589832 | tf_op jit(solution)/shard_map/ppermute | solution.py:223
  4.7 0.8 %shard_map.55 = f32[8,128]{1,0:T(8,128)S(1)} custom-call(s32[4,6]{1,0:T(4,128)} %bitcast.6, s32[4,6]{1,0:T(4,128)} %bitcast.8, s32[3,3]{1,0:T(4,128)} %pattern_ref.3), custom_call_target="tpu_custom_call" | custom-call | tf_op jit(solution)/shard_map/pallas_call | solution.py:200
  5.5 0.1 collective-permute-start
  5.5 0.1 collective-permute-start.4
  5.6 1.1 %collective-permute-done.near_ids = f32[8,128]{1,0:T(8,128)S(1)} collective-permute-done((f32[8,128]{1,0:T(8,128)S(1)}, f32[8,128]{1,0:T(8,128)S(1)}, u32[]{:S(2)}, u32[]{:S(2)}) %collective-permute-start) | collective-permute-done | bytes 4128 | tf_op jit(solution)/shard_map/ppermute | solution.py:223
  6.7 0.0 collective-permute-done.1.near_ref
  6.7 2.6 %shard_map.56 = (f32[10,128]{1,0:T(8,128)S(1)}, bf16[768,384]{1,0:T(8,128)(2,1)S(1)}, bf16[768,384]{1,0:T(8,128)(2,1)S(1)}, bf16[768,384]{1,0:T(8,128)(2,1)S(1)}...) custom-call(s32[1]{0:T(128)} %bitcast.me_ref, ...), custom_call_target="tpu_custom_call" | custom-call | tf_op jit(solution)/shard_map/pallas_call | solution.py:200
  9.3 0.0 collective-permute-done.3.near_b
  9.3 1.6 %shard_map.58 = (f32[768,128]{1,0:T(8,128)S(1)}, f32[384,128]{1,0:T(8,128)S(1)}) custom-call(f32[10,128]{1,0:T(8,128)S(1)} %get-tuple-element.26.mask_ref, bf16[768,384]{1,0:T(8,128)(2,1)S(1)} %get-tuple-element.28.own_high, bf16[768,384]{1,0:T(8,128)(2,1)S(1)} %get-tuple-element.29.own_low, bf16[768,384]{1,0:T(8,128)(2,1)S(1)} %get-tuple-element.30.near_high, ...), custom_call_target="tpu_custom_call" | custom-call | flops 679477 | tf_op jit(solution)/shard_map/pallas_call | solution.py:200
  11.0 0.0 collective-permute-done.2.b_ref
  11.0 0.2 collective-permute-start.6
  11.1 1.4 %collective-permute-start.5 = (f32[384,128]{1,0:T(8,128)S(1)}, f32[384,128]{1,0:T(8,128)S(1)}, u32[]{:S(2)}, u32[]{:S(2)}) collective-permute-start(f32[384,128]{1,0:T(8,128)S(1)} %get-tuple-element.39), channel_id=1, source_target_pairs={{0,12},{4,8},{8,4},{12,0},{1,13},{5,9},{9,5},{13,1},{2,14},{6,10},... | collective-permute-start | bytes 589832 | tf_op jit(solution)/shard_map/ppermute | solution.py:223
  12.6 0.4 %shard_map.60.running_ref = f32[384,128]{1,0:T(8,128)S(1)} custom-call(f32[384,128]{1,0:T(8,128)S(1)} %get-tuple-element.40.running_ref, bf16[768,384]{1,0:T(8,128)(2,1)S(1)} %get-tuple-element.35.high_ref, bf16[768,384]{1,0:T(8,128)(2,1)S(1)} %get-tuple-element.36.low_ref, f32[384,128]{1,0:T(8,128)S(1)} %collective-permute-done.2.b_ref), custom_call_target="tpu_custom_call" | custom-call | flops 113246 | tf_op jit(solution)/shard_map/pallas_call | solution.py:200
  13.0 1.0 %collective-permute-done.4.b_ref = f32[384,128]{1,0:T(8,128)S(1)} collective-permute-done((f32[384,128]{1,0:T(8,128)S(1)}, f32[384,128]{1,0:T(8,128)S(1)}, u32[]{:S(2)}, u32[]{:S(2)}) %collective-permute-start.4) | collective-permute-done | bytes 196640 | tf_op jit(solution)/shard_map/ppermute | solution.py:223
  14.0 0.6 %shard_map.59.running_ref = f32[768,128]{1,0:T(8,128)S(1)} custom-call(f32[768,128]{1,0:T(8,128)S(1)} %get-tuple-element.34.running_ref, bf16[768,384]{1,0:T(8,128)(2,1)S(1)} %get-tuple-element.35.high_ref, bf16[768,384]{1,0:T(8,128)(2,1)S(1)} %get-tuple-element.36.low_ref, f32[384,128]{1,0:T(8,128)S(1)} %collective-permute-done.4.b_ref), custom_call_target="tpu_custom_call" | custom-call | flops 226492 | tf_op jit(solution)/shard_map/pallas_call | solution.py:200
  14.6 0.0 collective-permute-done.6.b_ref
  14.6 0.4 %shard_map.61 = (f32[384,128]{1,0:T(8,128)S(1)}, f32[8,128]{1,0:T(8,128)S(1)}) custom-call(f32[10,128]{1,0:T(8,128)S(1)} %get-tuple-element.26.mask_ref, f32[384,128]{1,0:T(8,128)S(1)} %shard_map.60.running_ref, bf16[768,384]{1,0:T(8,128)(2,1)S(1)} %get-tuple-element.37.high_ref, bf16[768,384]{1,0:T(8,128)(2,1)S(1)} %get-tuple-element.38.low_ref, ...), custom_call_target="tpu_custom_call" | custom-call | flops 113246 | tf_op jit(solution)/shard_map/pallas_call | solution.py:200
  15.0 2.8 %collective-permute-done.5.b_ref = f32[384,128]{1,0:T(8,128)S(1)} collective-permute-done((f32[384,128]{1,0:T(8,128)S(1)}, f32[384,128]{1,0:T(8,128)S(1)}, u32[]{:S(2)}, u32[]{:S(2)}) %collective-permute-start.5) | collective-permute-done | bytes 196640 | tf_op jit(solution)/shard_map/ppermute | solution.py:223
  17.8 0.6 %shard_map.62 = (f32[384,128]{1,0:T(8,128)S(1)}, f32[384,128]{1,0:T(8,128)S(1)}, f32[1,128]{1,0:T(1,128)S(1)}) custom-call(f32[10,128]{1,0:T(8,128)S(1)} %get-tuple-element.26.mask_ref, f32[768,128]{1,0:T(8,128)S(1)} %shard_map.59.running_ref, bf16[768,384]{1,0:T(8,128)(2,1)S(1)} %get-tuple-element.37.high_ref, ...), custom_call_target="tpu_custom_call" | custom-call | flops 226492 | tf_op jit(solution)/shard_map/pallas_call | solution.py:200
  18.4 0.4 %collective-permute-start.11 = (f32[384,128]{1,0:T(8,128)S(1)}, f32[384,128]{1,0:T(8,128)S(1)}, u32[]{:S(2)}, u32[]{:S(2)}) collective-permute-start(f32[384,128]{1,0:T(8,128)S(1)} %get-tuple-element.45), channel_id=1, source_target_pairs={{0,4},{4,0},{8,12},{12,8},{1,5},{5,1},{9,13},{13,9},{2,6},{6,2},{1... | collective-permute-start | bytes 589832 | tf_op jit(solution)/shard_map/ppermute | solution.py:223
  18.9 0.1 collective-permute-start.7
  19.0 1.0 %collective-permute-done.7 = f32[1,128]{1,0:T(1,128)S(1)} collective-permute-done((f32[1,128]{1,0:T(1,128)S(1)}, f32[1,128]{1,0:T(1,128)S(1)}, u32[]{:S(2)}, u32[]{:S(2)}) %collective-permute-start.7) | collective-permute-done | bytes 544 | tf_op jit(solution)/shard_map/ppermute | solution.py:316
  20.0 1.5 %collective-permute-start.8 = (f32[1,128]{1,0:T(1,128)S(1)}, f32[1,128]{1,0:T(1,128)S(1)}, u32[]{:S(2)}, u32[]{:S(2)}) collective-permute-start(f32[1,128]{1,0:T(1,128)S(1)} %add.9), channel_id=1, source_target_pairs={{0,12},{1,13},{2,14},{3,15},{4,8},{5,9},{6,10},{7,11},{8,4},{9,5},... | collective-permute-start | bytes 1544 | tf_op jit(solution)/shard_map/ppermute | solution.py:316
  21.5 1.5 %collective-permute-done.8 = f32[1,128]{1,0:T(1,128)S(1)} collective-permute-done((f32[1,128]{1,0:T(1,128)S(1)}, f32[1,128]{1,0:T(1,128)S(1)}, u32[]{:S(2)}, u32[]{:S(2)}) %collective-permute-start.8) | collective-permute-done | bytes 544 | tf_op jit(solution)/shard_map/ppermute | solution.py:316
  23.0 1.6 %collective-permute-start.9 = (f32[1,128]{1,0:T(1,128)S(1)}, f32[1,128]{1,0:T(1,128)S(1)}, u32[]{:S(2)}, u32[]{:S(2)}) collective-permute-start(f32[1,128]{1,0:T(1,128)S(1)} %add.10), channel_id=1, source_target_pairs={{0,5},{1,4},{2,7},{3,6},{4,1},{5,0},{6,3},{7,2},{8,13},{9,12},{10,... | collective-permute-start | bytes 1544 | tf_op jit(solution)/shard_map/ppermute | solution.py:316
  24.5 1.4 %collective-permute-done.9 = f32[1,128]{1,0:T(1,128)S(1)} collective-permute-done((f32[1,128]{1,0:T(1,128)S(1)}, f32[1,128]{1,0:T(1,128)S(1)}, u32[]{:S(2)}, u32[]{:S(2)}) %collective-permute-start.9) | collective-permute-done | bytes 544 | tf_op jit(solution)/shard_map/ppermute | solution.py:316
  25.9 2.6 %collective-permute-start.10 = (f32[1,128]{1,0:T(1,128)S(1)}, f32[1,128]{1,0:T(1,128)S(1)}, u32[]{:S(2)}, u32[]{:S(2)}) collective-permute-start(f32[1,128]{1,0:T(1,128)S(1)} %add.11.one_ref), channel_id=1, source_target_pairs={{0,6},{1,7},{2,4},{3,5},{4,2},{5,3},{6,0},{7,1},{8,14},{9,15},{10,... | collective-permute-start | bytes 1544 | tf_op jit(solution)/shard_map/ppermute | solution.py:316
  28.5 1.3 %collective-permute-done.10.two_ref = f32[1,128]{1,0:T(1,128)S(1)} collective-permute-done((f32[1,128]{1,0:T(1,128)S(1)}, f32[1,128]{1,0:T(1,128)S(1)}, u32[]{:S(2)}, u32[]{:S(2)}) %collective-permute-start.10) | collective-permute-done | bytes 544 | tf_op jit(solution)/shard_map/ppermute | solution.py:316
  29.8 1.0 %shard_map.63 = f32[384,384]{1,0:T(8,128)} custom-call(f32[10,128]{1,0:T(8,128)S(1)} %get-tuple-element.26.mask_ref, f32[1,128]{1,0:T(1,128)S(1)} %add.11.one_ref, f32[1,128]{1,0:T(1,128)S(1)} %collective-permute-done.10.two_ref, f32[384,128]{1,0:T(8,128)S(1)} %get-tuple-element.44.keep_ref, f32[384,128]{1,0:T(8,128)S(1)} %collective-permute-done.11.take_ref, ...), custom_call_target="tpu_custom_call" | custom-call | tf_op jit(solution)/shard_map/pallas_call | solution.py:200
  (4 shorter events, 0.0 us)
Async XLA Ops:
  0.0 6.7 %collective-permute-start.1 = (f32[4,6,128,128]{3,2,1,0:T(8,128)}, f32[4,6,128,128]{3,2,1,0:T(8,128)S(1)}, u32[]{:S(2)}, u32[]{:S(2)}) collective-permute-start(f32[4,6,128,128]{3,2,1,0:T(8,128)} %bitcast.4), channel_id=1, source_target_pairs={{0,4},{4,0},{8,12},{12,8},{1,5},{5,1},{9,13},{13,9},{2,6},{6,2},{1... | collective-permute-start | bytes 4718600 | tf_op jit(solution)/shard_map/ppermute | solution.py:223
  0.5 8.9 %collective-permute-start.3 = (f32[384,384]{1,0:T(8,128)}, f32[384,384]{1,0:T(8,128)S(1)}, u32[]{:S(2)}, u32[]{:S(2)}) collective-permute-start(f32[384,384]{1,0:T(8,128)} %b_ref.1), channel_id=1, source_target_pairs={{0,4},{4,0},{8,12},{12,8},{1,5},{5,1},{9,13},{13,9},{2,6},{6,2},{1... | collective-permute-start | bytes 1769480 | tf_op jit(solution)/shard_map/ppermute | solution.py:223
  1.7 9.3 %collective-permute-start.2 = (f32[384,128]{1,0:T(8,128)S(1)}, f32[384,128]{1,0:T(8,128)S(1)}, u32[]{:S(2)}, u32[]{:S(2)}) collective-permute-start(f32[384,128]{1,0:T(8,128)S(1)} %get-tuple-element.27.refs_1_), channel_id=1, source_target_pairs={{0,8},{4,12},{8,0},{12,4},{1,9},{5,13},{9,1},{13,5},{2,10},{6,14},... | collective-permute-start | bytes 589832 | tf_op jit(solution)/shard_map/ppermute | solution.py:223
  5.5 1.2 %collective-permute-start = (f32[8,128]{1,0:T(8,128)S(1)}, f32[8,128]{1,0:T(8,128)S(1)}, u32[]{:S(2)}, u32[]{:S(2)}) collective-permute-start(f32[8,128]{1,0:T(8,128)S(1)} %shard_map.55), channel_id=1, source_target_pairs={{0,4},{4,0},{8,12},{12,8},{1,5},{5,1},{9,13},{13,9},{2,6},{6,2},{1... | collective-permute-start | bytes 12296 | tf_op jit(solution)/shard_map/ppermute | solution.py:223
  5.5 8.4 %collective-permute-start.4 = (f32[384,128]{1,0:T(8,128)S(1)}, f32[384,128]{1,0:T(8,128)S(1)}, u32[]{:S(2)}, u32[]{:S(2)}) collective-permute-start(f32[384,128]{1,0:T(8,128)S(1)} %get-tuple-element.32.refs_0_), channel_id=1, source_target_pairs={{0,8},{4,12},{8,0},{12,4},{1,9},{5,13},{9,1},{13,5},{2,10},{6,14},... | collective-permute-start | bytes 589832 | tf_op jit(solution)/shard_map/ppermute | solution.py:223
  11.0 3.6 %collective-permute-start.6 = (f32[384,128]{1,0:T(8,128)S(1)}, f32[384,128]{1,0:T(8,128)S(1)}, u32[]{:S(2)}, u32[]{:S(2)}) collective-permute-start(f32[384,128]{1,0:T(8,128)S(1)} %collective-permute-done.2.b_ref), channel_id=1, source_target_pairs={{0,4},{4,0},{8,12},{12,8},{1,5},{5,1},{9,13},{13,9},{2,6},{6,2},{1... | collective-permute-start | bytes 589832 | tf_op jit(solution)/shard_map/ppermute | solution.py:223
  11.1 6.6 %collective-permute-start.5 = (f32[384,128]{1,0:T(8,128)S(1)}, f32[384,128]{1,0:T(8,128)S(1)}, u32[]{:S(2)}, u32[]{:S(2)}) collective-permute-start(f32[384,128]{1,0:T(8,128)S(1)} %get-tuple-element.39), channel_id=1, source_target_pairs={{0,12},{4,8},{8,4},{12,0},{1,13},{5,9},{9,5},{13,1},{2,14},{6,10},... | collective-permute-start | bytes 589832 | tf_op jit(solution)/shard_map/ppermute | solution.py:223
  18.4 11.4 %collective-permute-start.11 = (f32[384,128]{1,0:T(8,128)S(1)}, f32[384,128]{1,0:T(8,128)S(1)}, u32[]{:S(2)}, u32[]{:S(2)}) collective-permute-start(f32[384,128]{1,0:T(8,128)S(1)} %get-tuple-element.45), channel_id=1, source_target_pairs={{0,4},{4,0},{8,12},{12,8},{1,5},{5,1},{9,13},{13,9},{2,6},{6,2},{1... | collective-permute-start | bytes 589832 | tf_op jit(solution)/shard_map/ppermute | solution.py:223
  18.9 1.1 %collective-permute-start.7 = (f32[1,128]{1,0:T(1,128)S(1)}, f32[1,128]{1,0:T(1,128)S(1)}, u32[]{:S(2)}, u32[]{:S(2)}) collective-permute-start(f32[1,128]{1,0:T(1,128)S(1)} %get-tuple-element.43), channel_id=1, source_target_pairs={{0,4},{1,5},{2,6},{3,7},{4,0},{5,1},{6,2},{7,3},{8,12},{9,13},{10,... | collective-permute-start | bytes 1544 | tf_op jit(solution)/shard_map/ppermute | solution.py:316
  20.0 3.0 %collective-permute-start.8 = (f32[1,128]{1,0:T(1,128)S(1)}, f32[1,128]{1,0:T(1,128)S(1)}, u32[]{:S(2)}, u32[]{:S(2)}) collective-permute-start(f32[1,128]{1,0:T(1,128)S(1)} %add.9), channel_id=1, source_target_pairs={{0,12},{1,13},{2,14},{3,15},{4,8},{5,9},{6,10},{7,11},{8,4},{9,5},... | collective-permute-start | bytes 1544 | tf_op jit(solution)/shard_map/ppermute | solution.py:316
  23.0 3.0 %collective-permute-start.9 = (f32[1,128]{1,0:T(1,128)S(1)}, f32[1,128]{1,0:T(1,128)S(1)}, u32[]{:S(2)}, u32[]{:S(2)}) collective-permute-start(f32[1,128]{1,0:T(1,128)S(1)} %add.10), channel_id=1, source_target_pairs={{0,5},{1,4},{2,7},{3,6},{4,1},{5,0},{6,3},{7,2},{8,13},{9,12},{10,... | collective-permute-start | bytes 1544 | tf_op jit(solution)/shard_map/ppermute | solution.py:316
  25.9 3.9 %collective-permute-start.10 = (f32[1,128]{1,0:T(1,128)S(1)}, f32[1,128]{1,0:T(1,128)S(1)}, u32[]{:S(2)}, u32[]{:S(2)}) collective-permute-start(f32[1,128]{1,0:T(1,128)S(1)} %add.11.one_ref), channel_id=1, source_target_pairs={{0,6},{1,7},{2,4},{3,5},{4,2},{5,3},{6,0},{7,1},{8,14},{9,15},{10,... | collective-permute-start | bytes 1544 | tf_op jit(solution)/shard_map/ppermute | solution.py:316

commit v4 on v3

--- a/solution.py
+++ b/solution.py
@@ -47,10 +47,13 @@
     outs, sems = refs[:-1], refs[-1]
     size = b_ref.shape[1] // col_blocks
     core = lax.rem(me_ref[0], 2)
-    where = [columns(core, 0, col_blocks, size), columns(core, 1, col_blocks, size)]
-    if len(outs) > 2:
-        where.append(middle_of(col_blocks, size))
-    copies = [pltpu.make_async_copy(b_ref.at[:, w], out, sems.at[i]) for i, (w, out) in enumerate(zip(where, outs))]
+    every, early = pl.ds(0, b_ref.shape[0]), outs[1].shape[0]
+    late = pl.ds(early, b_ref.shape[0] - early)
+    mine, others = columns(core, 0, col_blocks, size), columns(core, 1, col_blocks, size)
+    where = [(every, mine), (pl.ds(0, early), others), (late, others)]
+    if len(outs) > 3:
+        where.append((every, middle_of(col_blocks, size)))
+    copies = [pltpu.make_async_copy(b_ref.at[w], out, sems.at[i]) for i, (w, out) in enumerate(zip(where, outs))]
     for copy in copies:
         copy.start()
     for copy in copies:
@@ -144,9 +147,10 @@
         )
 
 
-def add_sum(running_ref, high_ref, low_ref, b_ref, out_ref):
-    rows = running_ref.shape[0]
-    out_ref[...] = running_ref[...] + product(high_ref[:rows], low_ref[:rows], b_ref[...])
+def add_sum(first, running_ref, high_ref, low_ref, b_ref, out_ref):
+    rows, depth = running_ref.shape[0], b_ref.shape[0]
+    high, low = high_ref[:rows, first : first + depth], low_ref[:rows, first : first + depth]
+    out_ref[...] = running_ref[...] + product(high, low, b_ref[...])
 
 
 def masked(value, mask_ref, first, out_ref, squares):
@@ -172,7 +176,8 @@
     *before, keep_ref, give_ref, squares_ref = refs
     height, size = keep_ref.shape[0], mask_ref.shape[1]
     count = keep_ref.shape[0] // size * (keep_ref.shape[1] // size)
-    total = running_ref[...] + product(high_ref[...], low_ref[...], b_ref[...])
+    first = high_ref.shape[1] - b_ref.shape[0]
+    total = running_ref[...] + product(high_ref[:, first:], low_ref[:, first:], b_ref[...])
     squares = before[0][...] if before else jnp.zeros((8, size), jnp.float32)
     squares = masked(total[:height], mask_ref, 0, keep_ref, squares)
     squares = masked(total[height:], mask_ref, count, give_ref, squares)
@@ -224,22 +229,26 @@
 
     piece = shape(height, half * size)
     middle = shape(height, size)
-    side, other, *mids = call(
+    early = (row_blocks - row_blocks // 3) * size
+    mids = [b_panel[:, half * size : (half + 1) * size]] * odd
+    side, other, rest = call(
         functools.partial(cut, col_blocks),
         0,
-        [piece, piece] + [middle] * odd,
+        [piece, shape(early, half * size), shape(height - early, half * size)],
         "sh",
         me,
         b_panel,
-        scratch=[pltpu.SemaphoreType.DMA((2 + odd,))],
+        scratch=[pltpu.SemaphoreType.DMA((3,))],
     )
     steps = range(1, chips)
     far_mids = [[move(mid, step, 0) for mid in mids] for step in steps]
     far_sides = [move(side, step, 0) for step in steps]
     far_others = [move(other, step, 1) for step in steps]
+    far_rests = [move(rest, step, 1) for step in steps]
 
     rows, cols = a_rows[0], a_cols[0]
-    near_blocks = move(blocks, 0, 1)
+    sent_blocks, _ = lax.optimization_barrier((blocks, mids))
+    near_blocks = move(sent_blocks, 0, 1)
     near_b = move(b_panel, 0, 1)
     packed = call(functools.partial(pack, size), 0, shape(8, size), "sss", rows, cols, pattern)
     near_ids = move(packed, 0, 1)
@@ -275,11 +284,11 @@
     for at, step in enumerate(steps):
         same, cross = dense[4 * step : 4 * step + 2], dense[4 * step + 2 : 4 * step + 4]
         for far_mid in far_mids[at]:
-            far_mid, running = lax.optimization_barrier((far_mid, running))
+            far_mid, mask = lax.optimization_barrier((far_mid, mask))
             forward = move(far_mid, 0, 1)
-            mid_running = [call(add_sum, flops, middle, "vvvv", *mid_running, *same, far_mid)]
+            mid_running = [call(functools.partial(add_sum, 0), flops, middle, "vvvv", *mid_running, *same, far_mid)]
             if step < chips - 1:
-                mid_running = [call(add_sum, flops, middle, "vvvv", *mid_running, *cross, forward)]
+                mid_running = [call(functools.partial(add_sum, 0), flops, middle, "vvvv", *mid_running, *cross, forward)]
             else:
                 *mid_running, squares = call(
                     finish_middle,
@@ -292,9 +301,11 @@
                     forward,
                 )
                 before = [squares]
-        running = call(add_sum, 2 * flops * half, wide, "vvvv", running, *same, far_sides[at])
+        running = call(functools.partial(add_sum, 0), 2 * flops * half, wide, "vvvv", running, *same, far_sides[at])
+        far_other, before = lax.optimization_barrier((far_others[at], before))
+        running = call(functools.partial(add_sum, 0), 2 * flops * half, wide, "vvvv", running, *cross, far_other)
         if step < chips - 1:
-            running = call(add_sum, 2 * flops * half, wide, "vvvv", running, *cross, far_others[at])
+            running = call(functools.partial(add_sum, early), 2 * flops * half, wide, "vvvv", running, *cross, far_rests[at])
     keep, give, squares = call(
         finish,
         2 * flops * half,
@@ -303,7 +314,7 @@
         mask,
         running,
         *cross,
-        far_others[-1],
+        far_rests[-1],
         *before,
     )
     take = move(give, 0, 1)

time: 31.1 us -> 30.7 us (0.987)
  waiting for transfers between devices: 9.94 us -> 7.81 us
  local copies, waits for them, and re-layouts: 0 us -> 0.94 us
  starting transfers between devices: 11.5 us -> 12.4 us
    ppermute x8 -> x9, waiting for transfers between devices: 4.83 us -> 2.54 us  [move(): return lax.ppermute(value, 'blk', pairs)]
    slice x0 -> x1, local copies, waits for them, and re-layouts: none -> 0.94 us  [body(): mids = [b_panel[:, half * size:(half + 1) * size]] * odd]
    ppermute x8 -> x9, starting transfers between devices: 5.7 us -> 6.52 us  [move(): return lax.ppermute(value, 'blk', pairs)]
    pallas_call x9 -> x10, Pallas kernels: 9.22 us -> 9.26 us  [call(): pl.pallas_call(kernel, out_shape=outs, in_specs=specs, out_specs=jax.tree...]
  transfers between devices with their start and end apart: 12 -> 13, of which waited for: 7 -> 7; matrix products, arithmetic and copies ran while one was open for 0% -> 0% of each run, Pallas kernels for 25% -> 26%
where the time goes in v4:
time: 30.7 us; the launch traced here: 30.5 us
  starting transfers between devices  12.4 us (40%)
  Pallas kernels  9.26 us (30%)
  waiting for transfers between devices  7.81 us (25%)
  local copies, waits for them, and re-layouts  0.94 us (3%)
    pallas_call x10, Pallas kernels, call(): pl.pallas_call(kernel, out_shape=outs, in_specs=specs, out_specs=jax.tree...  9.26 us
    ppermute x9, starting transfers between devices, move(): return lax.ppermute(value, 'blk', pairs)  6.52 us
    ppermute x4, starting transfers between devices, swap(): return lax.ppermute(value, ('blk', 'col'), pairs)  5.85 us
    ppermute x4, waiting for transfers between devices, swap(): return lax.ppermute(value, ('blk', 'col'), pairs)  5.27 us
    ppermute x9, waiting for transfers between devices, move(): return lax.ppermute(value, 'blk', pairs)  2.54 us
    slice x1, local copies, waits for them, and re-layouts, body(): mids = [b_panel[:, half * size:(half + 1) * size]] * odd  0.94 us
  transfers between devices with their start and end apart: 13, of which 7 were waited for; matrix products, arithmetic and copies ran while one was open for 0% of the time, Pallas kernels for 26%

profile of v4, /device:TPU:0, one launch (start us, length us, event | category | flops | bytes accessed | tf_op | source)
XLA Modules:
  0.0 30.5 jit_solution(9835194301004099533)
XLA Ops:
  0.0 0.9 %slice.3.refs_1_ = f32[384,128]{1,0:T(8,128)S(1)} slice(f32[384,384]{1,0:T(8,128)} %b_ref.1), slice={[0:384], [128:256]} | slice | bytes 393216 | tf_op jit(solution)/shard_map/slice | solution.py:233
  0.9 0.5 %collective-permute-start.2 = (f32[4,6,128,128]{3,2,1,0:T(8,128)}, f32[4,6,128,128]{3,2,1,0:T(8,128)S(1)}, u32[]{:S(2)}, u32[]{:S(2)}) collective-permute-start(f32[4,6,128,128]{3,2,1,0:T(8,128)} %bitcast.4), channel_id=1, source_target_pairs={{0,4},{4,0},{8,12},{12,8},{1,5},{5,1},{9,13},{13,9},{2,6},{6,2},{1... | collective-permute-start | bytes 4718600 | tf_op jit(solution)/shard_map/ppermute | solution.py:228
  1.5 0.1 collective-permute-start.3
  1.5 2.9 %collective-permute-start = (f32[384,128]{1,0:T(8,128)S(1)}, f32[384,128]{1,0:T(8,128)S(1)}, u32[]{:S(2)}, u32[]{:S(2)}) collective-permute-start(f32[384,128]{1,0:T(8,128)S(1)} %slice.3.refs_1_), channel_id=1, source_target_pairs={{0,8},{4,12},{8,0},{12,4},{1,9},{5,13},{9,1},{13,5},{2,10},{6,14},... | collective-permute-start | bytes 589832 | tf_op jit(solution)/shard_map/ppermute | solution.py:228
  4.5 0.8 %shard_map.55 = f32[8,128]{1,0:T(8,128)S(1)} custom-call(s32[4,6]{1,0:T(4,128)} %bitcast.6, s32[4,6]{1,0:T(4,128)} %bitcast.8, s32[3,3]{1,0:T(4,128)} %pattern_ref.3), custom_call_target="tpu_custom_call" | custom-call | tf_op jit(solution)/shard_map/pallas_call | solution.py:205
  5.3 0.1 collective-permute-start.1
  5.3 1.0 %shard_map.57 = (f32[384,128]{1,0:T(8,128)S(1)}, f32[256,128]{1,0:T(8,128)S(1)}, f32[128,128]{1,0:T(8,128)S(1)}) custom-call(s32[1]{0:T(128)} %bitcast.me_ref, f32[384,384]{1,0:T(8,128)} %b_ref.1), custom_call_target="tpu_custom_call" | custom-call | tf_op jit(solution)/shard_map/pallas_call | solution.py:205
  6.4 0.1 collective-permute-start.4
  6.5 0.0 collective-permute-done.1.near_ids
  6.5 0.0 collective-permute-done.2.near_ref
  6.5 2.6 %shard_map.56 = (f32[10,128]{1,0:T(8,128)S(1)}, bf16[768,384]{1,0:T(8,128)(2,1)S(1)}, bf16[768,384]{1,0:T(8,128)(2,1)S(1)}, bf16[768,384]{1,0:T(8,128)(2,1)S(1)}...) custom-call(s32[1]{0:T(128)} %bitcast.me_ref, ...), custom_call_target="tpu_custom_call" | custom-call | tf_op jit(solution)/shard_map/pallas_call | solution.py:205
  9.1 0.6 %collective-permute-done.b_ref = f32[384,128]{1,0:T(8,128)S(1)} collective-permute-done((f32[384,128]{1,0:T(8,128)S(1)}, f32[384,128]{1,0:T(8,128)S(1)}, u32[]{:S(2)}, u32[]{:S(2)}) %collective-permute-start) | collective-permute-done | bytes 196640 | tf_op jit(solution)/shard_map/ppermute | solution.py:228
  9.7 2.6 %collective-permute-start.5 = (f32[256,128]{1,0:T(8,128)S(1)}, f32[256,128]{1,0:T(8,128)S(1)}, u32[]{:S(2)}, u32[]{:S(2)}) collective-permute-start(f32[256,128]{1,0:T(8,128)S(1)} %get-tuple-element.42), channel_id=1, source_target_pairs={{0,12},{4,8},{8,4},{12,0},{1,13},{5,9},{9,5},{13,1},{2,14},{6,10},... | collective-permute-start | bytes 393224 | tf_op jit(solution)/shard_map/ppermute | solution.py:228
  12.3 0.0 collective-permute-start.7
  12.4 1.6 %shard_map.58 = (f32[768,128]{1,0:T(8,128)S(1)}, f32[384,128]{1,0:T(8,128)S(1)}) custom-call(f32[10,128]{1,0:T(8,128)S(1)} %get-tuple-element.31.mask_ref, bf16[768,384]{1,0:T(8,128)(2,1)S(1)} %get-tuple-element.32.own_high, bf16[768,384]{1,0:T(8,128)(2,1)S(1)} %get-tuple-element.33.own_low, bf16[768,384]{1,0:T(8,128)(2,1)S(1)} %get-tuple-element.34.near_high, ...), custom_call_target="tpu_custom_call" | custom-call | flops 679477 | tf_op jit(solution)/shard_map/pallas_call | solution.py:205
  14.0 0.4 %shard_map.60.running_ref = f32[384,128]{1,0:T(8,128)S(1)} custom-call(f32[384,128]{1,0:T(8,128)S(1)} %get-tuple-element.43.running_ref, bf16[768,384]{1,0:T(8,128)(2,1)S(1)} %get-tuple-element.38.high_ref, bf16[768,384]{1,0:T(8,128)(2,1)S(1)} %get-tuple-element.39.low_ref, f32[384,128]{1,0:T(8,128)S(1)} %collective-permute-done.b_ref), custom_call_target="tpu_custom_call" | custom-call | flops 113246 | tf_op jit(solution)/shard_map/pallas_call | solution.py:205
  14.4 0.6 %shard_map.59.running_ref = f32[768,128]{1,0:T(8,128)S(1)} custom-call(f32[768,128]{1,0:T(8,128)S(1)} %get-tuple-element.37.running_ref, bf16[768,384]{1,0:T(8,128)(2,1)S(1)} %get-tuple-element.38.high_ref, bf16[768,384]{1,0:T(8,128)(2,1)S(1)} %get-tuple-element.39.low_ref, f32[384,128]{1,0:T(8,128)S(1)} %collective-permute-done.4.b_ref), custom_call_target="tpu_custom_call" | custom-call | flops 226492 | tf_op jit(solution)/shard_map/pallas_call | solution.py:205
  15.1 0.4 %shard_map.61 = (f32[384,128]{1,0:T(8,128)S(1)}, f32[8,128]{1,0:T(8,128)S(1)}) custom-call(f32[10,128]{1,0:T(8,128)S(1)} %get-tuple-element.31.mask_ref, f32[384,128]{1,0:T(8,128)S(1)} %shard_map.60.running_ref, bf16[768,384]{1,0:T(8,128)(2,1)S(1)} %get-tuple-element.40.high_ref, bf16[768,384]{1,0:T(8,128)(2,1)S(1)} %get-tuple-element.41.low_ref, ...), custom_call_target="tpu_custom_call" | custom-call | flops 113246 | tf_op jit(solution)/shard_map/pallas_call | solution.py:205
  15.5 1.0 %collective-permute-done.5.b_ref = f32[256,128]{1,0:T(8,128)S(1)} collective-permute-done((f32[256,128]{1,0:T(8,128)S(1)}, f32[256,128]{1,0:T(8,128)S(1)}, u32[]{:S(2)}, u32[]{:S(2)}) %collective-permute-start.5) | collective-permute-done | bytes 131104 | tf_op jit(solution)/shard_map/ppermute | solution.py:228
  16.4 0.5 %shard_map.62.running_ref = f32[768,128]{1,0:T(8,128)S(1)} custom-call(f32[768,128]{1,0:T(8,128)S(1)} %shard_map.59.running_ref, bf16[768,384]{1,0:T(8,128)(2,1)S(1)} %get-tuple-element.40.high_ref, bf16[768,384]{1,0:T(8,128)(2,1)S(1)} %get-tuple-element.41.low_ref, f32[256,128]{1,0:T(8,128)S(1)} %collective-permute-done.5.b_ref), custom_call_target="tpu_custom_call" | custom-call | flops 226492 | tf_op jit(solution)/shard_map/pallas_call | solution.py:205
  16.9 0.9 %collective-permute-done.7.b_ref = f32[128,128]{1,0:T(8,128)S(1)} collective-permute-done((f32[128,128]{1,0:T(8,128)S(1)}, f32[128,128]{1,0:T(8,128)S(1)}, u32[]{:S(2)}, u32[]{:S(2)}) %collective-permute-start.7) | collective-permute-done | bytes 65568 | tf_op jit(solution)/shard_map/ppermute | solution.py:228
  17.9 0.3 %shard_map.63 = (f32[384,128]{1,0:T(8,128)S(1)}, f32[384,128]{1,0:T(8,128)S(1)}, f32[1,128]{1,0:T(1,128)S(1)}) custom-call(f32[10,128]{1,0:T(8,128)S(1)} %get-tuple-element.31.mask_ref, f32[768,128]{1,0:T(8,128)S(1)} %shard_map.62.running_ref, bf16[768,384]{1,0:T(8,128)(2,1)S(1)} %get-tuple-element.40.high_ref, ...), custom_call_target="tpu_custom_call" | custom-call | flops 226492 | tf_op jit(solution)/shard_map/pallas_call | solution.py:205
  18.2 0.2 collective-permute-start.12
  18.4 0.4 %collective-permute-start.8 = (f32[1,128]{1,0:T(1,128)S(1)}, f32[1,128]{1,0:T(1,128)S(1)}, u32[]{:S(2)}, u32[]{:S(2)}) collective-permute-start(f32[1,128]{1,0:T(1,128)S(1)} %get-tuple-element.49), channel_id=1, source_target_pairs={{0,4},{1,5},{2,6},{3,7},{4,0},{5,1},{6,2},{7,3},{8,12},{9,13},{10,... | collective-permute-start | bytes 1544 | tf_op jit(solution)/shard_map/ppermute | solution.py:327
  18.8 0.9 %collective-permute-done.8 = f32[1,128]{1,0:T(1,128)S(1)} collective-permute-done((f32[1,128]{1,0:T(1,128)S(1)}, f32[1,128]{1,0:T(1,128)S(1)}, u32[]{:S(2)}, u32[]{:S(2)}) %collective-permute-start.8) | collective-permute-done | bytes 544 | tf_op jit(solution)/shard_map/ppermute | solution.py:327
  19.7 1.4 %collective-permute-start.9 = (f32[1,128]{1,0:T(1,128)S(1)}, f32[1,128]{1,0:T(1,128)S(1)}, u32[]{:S(2)}, u32[]{:S(2)}) collective-permute-start(f32[1,128]{1,0:T(1,128)S(1)} %add.9), channel_id=1, source_target_pairs={{0,12},{1,13},{2,14},{3,15},{4,8},{5,9},{6,10},{7,11},{8,4},{9,5},... | collective-permute-start | bytes 1544 | tf_op jit(solution)/shard_map/ppermute | solution.py:327
  21.1 1.6 %collective-permute-done.9 = f32[1,128]{1,0:T(1,128)S(1)} collective-permute-done((f32[1,128]{1,0:T(1,128)S(1)}, f32[1,128]{1,0:T(1,128)S(1)}, u32[]{:S(2)}, u32[]{:S(2)}) %collective-permute-start.9) | collective-permute-done | bytes 544 | tf_op jit(solution)/shard_map/ppermute | solution.py:327
  22.7 1.5 %collective-permute-start.10 = (f32[1,128]{1,0:T(1,128)S(1)}, f32[1,128]{1,0:T(1,128)S(1)}, u32[]{:S(2)}, u32[]{:S(2)}) collective-permute-start(f32[1,128]{1,0:T(1,128)S(1)} %add.10), channel_id=1, source_target_pairs={{0,5},{1,4},{2,7},{3,6},{4,1},{5,0},{6,3},{7,2},{8,13},{9,12},{10,... | collective-permute-start | bytes 1544 | tf_op jit(solution)/shard_map/ppermute | solution.py:327
  24.2 1.4 %collective-permute-done.10 = f32[1,128]{1,0:T(1,128)S(1)} collective-permute-done((f32[1,128]{1,0:T(1,128)S(1)}, f32[1,128]{1,0:T(1,128)S(1)}, u32[]{:S(2)}, u32[]{:S(2)}) %collective-permute-start.10) | collective-permute-done | bytes 544 | tf_op jit(solution)/shard_map/ppermute | solution.py:327
  25.6 2.5 %collective-permute-start.11 = (f32[1,128]{1,0:T(1,128)S(1)}, f32[1,128]{1,0:T(1,128)S(1)}, u32[]{:S(2)}, u32[]{:S(2)}) collective-permute-start(f32[1,128]{1,0:T(1,128)S(1)} %add.11.one_ref), channel_id=1, source_target_pairs={{0,6},{1,7},{2,4},{3,5},{4,2},{5,3},{6,0},{7,1},{8,14},{9,15},{10,... | collective-permute-start | bytes 1544 | tf_op jit(solution)/shard_map/ppermute | solution.py:327
  28.2 1.3 %collective-permute-done.11.two_ref = f32[1,128]{1,0:T(1,128)S(1)} collective-permute-done((f32[1,128]{1,0:T(1,128)S(1)}, f32[1,128]{1,0:T(1,128)S(1)}, u32[]{:S(2)}, u32[]{:S(2)}) %collective-permute-start.11) | collective-permute-done | bytes 544 | tf_op jit(solution)/shard_map/ppermute | solution.py:327
  29.5 1.0 %shard_map.64 = f32[384,384]{1,0:T(8,128)} custom-call(f32[10,128]{1,0:T(8,128)S(1)} %get-tuple-element.31.mask_ref, f32[1,128]{1,0:T(1,128)S(1)} %add.11.one_ref, f32[1,128]{1,0:T(1,128)S(1)} %collective-permute-done.11.two_ref, f32[384,128]{1,0:T(8,128)S(1)} %get-tuple-element.50.keep_ref, f32[384,128]{1,0:T(8,128)S(1)} %collective-permute-done.12.take_ref, ...), custom_call_target="tpu_custom_call" | custom-call | tf_op jit(solution)/shard_map/pallas_call | solution.py:205
  (8 shorter events, 0.0 us)
Async XLA Ops:
  0.9 5.6 %collective-permute-start.2 = (f32[4,6,128,128]{3,2,1,0:T(8,128)}, f32[4,6,128,128]{3,2,1,0:T(8,128)S(1)}, u32[]{:S(2)}, u32[]{:S(2)}) collective-permute-start(f32[4,6,128,128]{3,2,1,0:T(8,128)} %bitcast.4), channel_id=1, source_target_pairs={{0,4},{4,0},{8,12},{12,8},{1,5},{5,1},{9,13},{13,9},{2,6},{6,2},{1... | collective-permute-start | bytes 4718600 | tf_op jit(solution)/shard_map/ppermute | solution.py:228
  1.5 10.9 %collective-permute-start.3 = (f32[384,384]{1,0:T(8,128)}, f32[384,384]{1,0:T(8,128)S(1)}, u32[]{:S(2)}, u32[]{:S(2)}) collective-permute-start(f32[384,384]{1,0:T(8,128)} %b_ref.1), channel_id=1, source_target_pairs={{0,4},{4,0},{8,12},{12,8},{1,5},{5,1},{9,13},{13,9},{2,6},{6,2},{1... | collective-permute-start | bytes 1769480 | tf_op jit(solution)/shard_map/ppermute | solution.py:228
  1.5 8.2 %collective-permute-start = (f32[384,128]{1,0:T(8,128)S(1)}, f32[384,128]{1,0:T(8,128)S(1)}, u32[]{:S(2)}, u32[]{:S(2)}) collective-permute-start(f32[384,128]{1,0:T(8,128)S(1)} %slice.3.refs_1_), channel_id=1, source_target_pairs={{0,8},{4,12},{8,0},{12,4},{1,9},{5,13},{9,1},{13,5},{2,10},{6,14},... | collective-permute-start | bytes 589832 | tf_op jit(solution)/shard_map/ppermute | solution.py:228
  5.3 1.3 %collective-permute-start.1 = (f32[8,128]{1,0:T(8,128)S(1)}, f32[8,128]{1,0:T(8,128)S(1)}, u32[]{:S(2)}, u32[]{:S(2)}) collective-permute-start(f32[8,128]{1,0:T(8,128)S(1)} %shard_map.55), channel_id=1, source_target_pairs={{0,4},{4,0},{8,12},{12,8},{1,5},{5,1},{9,13},{13,9},{2,6},{6,2},{1... | collective-permute-start | bytes 12296 | tf_op jit(solution)/shard_map/ppermute | solution.py:228
  6.4 8.0 %collective-permute-start.4 = (f32[384,128]{1,0:T(8,128)S(1)}, f32[384,128]{1,0:T(8,128)S(1)}, u32[]{:S(2)}, u32[]{:S(2)}) collective-permute-start(f32[384,128]{1,0:T(8,128)S(1)} %get-tuple-element.36.refs_0_), channel_id=1, source_target_pairs={{0,8},{4,12},{8,0},{12,4},{1,9},{5,13},{9,1},{13,5},{2,10},{6,14},... | collective-permute-start | bytes 589832 | tf_op jit(solution)/shard_map/ppermute | solution.py:228
  9.7 5.3 %collective-permute-start.6 = (f32[384,128]{1,0:T(8,128)S(1)}, f32[384,128]{1,0:T(8,128)S(1)}, u32[]{:S(2)}, u32[]{:S(2)}) collective-permute-start(f32[384,128]{1,0:T(8,128)S(1)} %collective-permute-done.b_ref), channel_id=1, source_target_pairs={{0,4},{4,0},{8,12},{12,8},{1,5},{5,1},{9,13},{13,9},{2,6},{6,2},{1... | collective-permute-start | bytes 589832 | tf_op jit(solution)/shard_map/ppermute | solution.py:228
  9.7 6.7 %collective-permute-start.5 = (f32[256,128]{1,0:T(8,128)S(1)}, f32[256,128]{1,0:T(8,128)S(1)}, u32[]{:S(2)}, u32[]{:S(2)}) collective-permute-start(f32[256,128]{1,0:T(8,128)S(1)} %get-tuple-element.42), channel_id=1, source_target_pairs={{0,12},{4,8},{8,4},{12,0},{1,13},{5,9},{9,5},{13,1},{2,14},{6,10},... | collective-permute-start | bytes 393224 | tf_op jit(solution)/shard_map/ppermute | solution.py:228
  12.3 5.5 %collective-permute-start.7 = (f32[128,128]{1,0:T(8,128)S(1)}, f32[128,128]{1,0:T(8,128)S(1)}, u32[]{:S(2)}, u32[]{:S(2)}) collective-permute-start(f32[128,128]{1,0:T(8,128)S(1)} %get-tuple-element.47), channel_id=1, source_target_pairs={{0,12},{4,8},{8,4},{12,0},{1,13},{5,9},{9,5},{13,1},{2,14},{6,10},... | collective-permute-start | bytes 196616 | tf_op jit(solution)/shard_map/ppermute | solution.py:228
  18.2 11.3 %collective-permute-start.12 = (f32[384,128]{1,0:T(8,128)S(1)}, f32[384,128]{1,0:T(8,128)S(1)}, u32[]{:S(2)}, u32[]{:S(2)}) collective-permute-start(f32[384,128]{1,0:T(8,128)S(1)} %get-tuple-element.51), channel_id=1, source_target_pairs={{0,4},{4,0},{8,12},{12,8},{1,5},{5,1},{9,13},{13,9},{2,6},{6,2},{1... | collective-permute-start | bytes 589832 | tf_op jit(solution)/shard_map/ppermute | solution.py:228
  18.4 1.3 %collective-permute-start.8 = (f32[1,128]{1,0:T(1,128)S(1)}, f32[1,128]{1,0:T(1,128)S(1)}, u32[]{:S(2)}, u32[]{:S(2)}) collective-permute-start(f32[1,128]{1,0:T(1,128)S(1)} %get-tuple-element.49), channel_id=1, source_target_pairs={{0,4},{1,5},{2,6},{3,7},{4,0},{5,1},{6,2},{7,3},{8,12},{9,13},{10,... | collective-permute-start | bytes 1544 | tf_op jit(solution)/shard_map/ppermute | solution.py:327
  19.7 3.0 %collective-permute-start.9 = (f32[1,128]{1,0:T(1,128)S(1)}, f32[1,128]{1,0:T(1,128)S(1)}, u32[]{:S(2)}, u32[]{:S(2)}) collective-permute-start(f32[1,128]{1,0:T(1,128)S(1)} %add.9), channel_id=1, source_target_pairs={{0,12},{1,13},{2,14},{3,15},{4,8},{5,9},{6,10},{7,11},{8,4},{9,5},... | collective-permute-start | bytes 1544 | tf_op jit(solution)/shard_map/ppermute | solution.py:327
  22.7 3.0 %collective-permute-start.10 = (f32[1,128]{1,0:T(1,128)S(1)}, f32[1,128]{1,0:T(1,128)S(1)}, u32[]{:S(2)}, u32[]{:S(2)}) collective-permute-start(f32[1,128]{1,0:T(1,128)S(1)} %add.10), channel_id=1, source_target_pairs={{0,5},{1,4},{2,7},{3,6},{4,1},{5,0},{6,3},{7,2},{8,13},{9,12},{10,... | collective-permute-start | bytes 1544 | tf_op jit(solution)/shard_map/ppermute | solution.py:327
  25.6 3.9 %collective-permute-start.11 = (f32[1,128]{1,0:T(1,128)S(1)}, f32[1,128]{1,0:T(1,128)S(1)}, u32[]{:S(2)}, u32[]{:S(2)}) collective-permute-start(f32[1,128]{1,0:T(1,128)S(1)} %add.11.one_ref), channel_id=1, source_target_pairs={{0,6},{1,7},{2,4},{3,5},{4,2},{5,3},{6,0},{7,1},{8,14},{9,15},{10,... | collective-permute-start | bytes 1544 | tf_op jit(solution)/shard_map/ppermute | solution.py:327

commit v5 on v4

--- a/solution.py
+++ b/solution.py
@@ -27,6 +27,13 @@
 
 def product(high_a, low_a, b):
     high_b, low_b = split(b)
+    width = b.shape[1]
+    if width <= 128:
+        left = jnp.concatenate([high_a, low_a], axis=1)
+        both = jnp.concatenate([high_b, low_b], axis=1)
+        right = jnp.concatenate([both, both], axis=0)
+        result = jnp.dot(left, right, preferred_element_type=jnp.float32)
+        return result[:, :width] + result[:, width:]
     left = jnp.concatenate([high_a, high_a, low_a], axis=1)
     right = jnp.concatenate([high_b, low_b, high_b], axis=0)
     return jnp.dot(left, right, preferred_element_type=jnp.float32)
@@ -188,7 +195,7 @@
     *mid_refs, out_ref = refs
     width = keep_ref.shape[1]
     squares = jnp.sum(one_ref[...] + two_ref[...], axis=1, keepdims=True)
-    factor = -jnp.minimum(1.0, limit / jnp.sqrt(squares + 1e-06))
+    factor = -jnp.minimum(1.0, limit * lax.rsqrt(squares + 1e-06))
     core = mask_ref[mask_ref.shape[0] - 1, 0:1].reshape(1, 1)
     keep, take = keep_ref[...] * factor, take_ref[...] * factor
     out_ref[:, :width] = jnp.where(core == 0.0, keep, take)

time: 30.7 us -> 30.7 us (level)
  Pallas kernels: 9.26 us -> 8.33 us
  waiting for transfers between devices: 7.81 us -> 8.69 us
    pallas_call x10, Pallas kernels: 9.26 us -> 8.33 us  [call(): pl.pallas_call(kernel, out_shape=outs, in_specs=specs, out_specs=jax.tree...]
    ppermute x9, waiting for transfers between devices: 2.54 us -> 3.41 us  [move(): return lax.ppermute(value, 'blk', pairs)]
  transfers between devices with their start and end apart: 13 -> 13, of which waited for: 7 -> 8; matrix products, arithmetic and copies ran while one was open for 0% -> 0% of each run, Pallas kernels for 26% -> 23%
where the time goes in v5:
time: 30.7 us; the launch traced here: 30.4 us
  starting transfers between devices  12.4 us (40%)
  waiting for transfers between devices  8.69 us (28%)
  Pallas kernels  8.33 us (27%)
  local copies, waits for them, and re-layouts  0.94 us (3%)
    pallas_call x10, Pallas kernels, call(): pl.pallas_call(kernel, out_shape=outs, in_specs=specs, out_specs=jax.tree...  8.33 us
    ppermute x9, starting transfers between devices, move(): return lax.ppermute(value, 'blk', pairs)  6.51 us
    ppermute x4, starting transfers between devices, swap(): return lax.ppermute(value, ('blk', 'col'), pairs)  5.85 us
    ppermute x4, waiting for transfers between devices, swap(): return lax.ppermute(value, ('blk', 'col'), pairs)  5.27 us
    ppermute x9, waiting for transfers between devices, move(): return lax.ppermute(value, 'blk', pairs)  3.41 us
    slice x1, local copies, waits for them, and re-layouts, body(): mids = [b_panel[:, half * size:(half + 1) * size]] * odd  0.94 us
  transfers between devices with their start and end apart: 13, of which 8 were waited for; matrix products, arithmetic and copies ran while one was open for 0% of the time, Pallas kernels for 23%

profile of v5, /device:TPU:0, one launch (start us, length us, event | category | flops | bytes accessed | tf_op | source)
XLA Modules:
  0.0 30.4 jit_solution(10524031401346410956)
XLA Ops:
  0.0 0.9 %slice.3.refs_1_ = f32[384,128]{1,0:T(8,128)S(1)} slice(f32[384,384]{1,0:T(8,128)} %b_ref.1), slice={[0:384], [128:256]} | slice | bytes 393216 | tf_op jit(solution)/shard_map/slice | solution.py:240
  0.9 0.5 %collective-permute-start.2 = (f32[4,6,128,128]{3,2,1,0:T(8,128)}, f32[4,6,128,128]{3,2,1,0:T(8,128)S(1)}, u32[]{:S(2)}, u32[]{:S(2)}) collective-permute-start(f32[4,6,128,128]{3,2,1,0:T(8,128)} %bitcast.4), channel_id=1, source_target_pairs={{0,4},{4,0},{8,12},{12,8},{1,5},{5,1},{9,13},{13,9},{2,6},{6,2},{1... | collective-permute-start | bytes 4718600 | tf_op jit(solution)/shard_map/ppermute | solution.py:235
  1.5 0.1 collective-permute-start.3
  1.5 2.9 %collective-permute-start = (f32[384,128]{1,0:T(8,128)S(1)}, f32[384,128]{1,0:T(8,128)S(1)}, u32[]{:S(2)}, u32[]{:S(2)}) collective-permute-start(f32[384,128]{1,0:T(8,128)S(1)} %slice.3.refs_1_), channel_id=1, source_target_pairs={{0,8},{4,12},{8,0},{12,4},{1,9},{5,13},{9,1},{13,5},{2,10},{6,14},... | collective-permute-start | bytes 589832 | tf_op jit(solution)/shard_map/ppermute | solution.py:235
  4.5 0.8 %shard_map.55 = f32[8,128]{1,0:T(8,128)S(1)} custom-call(s32[4,6]{1,0:T(4,128)} %bitcast.6, s32[4,6]{1,0:T(4,128)} %bitcast.8, s32[3,3]{1,0:T(4,128)} %pattern_ref.3), custom_call_target="tpu_custom_call" | custom-call | tf_op jit(solution)/shard_map/pallas_call | solution.py:212
  5.3 0.1 collective-permute-start.1
  5.3 1.0 %shard_map.57 = (f32[384,128]{1,0:T(8,128)S(1)}, f32[256,128]{1,0:T(8,128)S(1)}, f32[128,128]{1,0:T(8,128)S(1)}) custom-call(s32[1]{0:T(128)} %bitcast.me_ref, f32[384,384]{1,0:T(8,128)} %b_ref.1), custom_call_target="tpu_custom_call" | custom-call | tf_op jit(solution)/shard_map/pallas_call | solution.py:212
  6.4 0.1 collective-permute-start.4
  6.5 0.0 collective-permute-done.2.near_ref
  6.5 2.6 %shard_map.56 = (f32[10,128]{1,0:T(8,128)S(1)}, bf16[768,384]{1,0:T(8,128)(2,1)S(1)}, bf16[768,384]{1,0:T(8,128)(2,1)S(1)}, bf16[768,384]{1,0:T(8,128)(2,1)S(1)}...) custom-call(s32[1]{0:T(128)} %bitcast.me_ref, ...), custom_call_target="tpu_custom_call" | custom-call | tf_op jit(solution)/shard_map/pallas_call | solution.py:212
  9.2 0.6 %collective-permute-done.b_ref = f32[384,128]{1,0:T(8,128)S(1)} collective-permute-done((f32[384,128]{1,0:T(8,128)S(1)}, f32[384,128]{1,0:T(8,128)S(1)}, u32[]{:S(2)}, u32[]{:S(2)}) %collective-permute-start) | collective-permute-done | bytes 196640 | tf_op jit(solution)/shard_map/ppermute | solution.py:235
  9.7 2.6 %collective-permute-start.5 = (f32[256,128]{1,0:T(8,128)S(1)}, f32[256,128]{1,0:T(8,128)S(1)}, u32[]{:S(2)}, u32[]{:S(2)}) collective-permute-start(f32[256,128]{1,0:T(8,128)S(1)} %get-tuple-element.42), channel_id=1, source_target_pairs={{0,12},{4,8},{8,4},{12,0},{1,13},{5,9},{9,5},{13,1},{2,14},{6,10},... | collective-permute-start | bytes 393224 | tf_op jit(solution)/shard_map/ppermute | solution.py:235
  12.3 0.0 collective-permute-start.7
  12.4 1.1 %shard_map.58 = (f32[768,128]{1,0:T(8,128)S(1)}, f32[384,128]{1,0:T(8,128)S(1)}) custom-call(f32[10,128]{1,0:T(8,128)S(1)} %get-tuple-element.31.mask_ref, bf16[768,384]{1,0:T(8,128)(2,1)S(1)} %get-tuple-element.32.own_high, bf16[768,384]{1,0:T(8,128)(2,1)S(1)} %get-tuple-element.33.own_low, bf16[768,384]{1,0:T(8,128)(2,1)S(1)} %get-tuple-element.34.near_high, ...), custom_call_target="tpu_custom_call" | custom-call | flops 679477 | tf_op jit(solution)/shard_map/pallas_call | solution.py:212
  13.5 0.3 %shard_map.60.running_ref = f32[384,128]{1,0:T(8,128)S(1)} custom-call(f32[384,128]{1,0:T(8,128)S(1)} %get-tuple-element.43.running_ref, bf16[768,384]{1,0:T(8,128)(2,1)S(1)} %get-tuple-element.38.high_ref, bf16[768,384]{1,0:T(8,128)(2,1)S(1)} %get-tuple-element.39.low_ref, f32[384,128]{1,0:T(8,128)S(1)} %collective-permute-done.b_ref), custom_call_target="tpu_custom_call" | custom-call | flops 113246 | tf_op jit(solution)/shard_map/pallas_call | solution.py:212
  13.8 0.2 collective-permute-done.4.b_ref
  14.0 0.5 %shard_map.59.running_ref = f32[768,128]{1,0:T(8,128)S(1)} custom-call(f32[768,128]{1,0:T(8,128)S(1)} %get-tuple-element.37.running_ref, bf16[768,384]{1,0:T(8,128)(2,1)S(1)} %get-tuple-element.38.high_ref, bf16[768,384]{1,0:T(8,128)(2,1)S(1)} %get-tuple-element.39.low_ref, f32[384,128]{1,0:T(8,128)S(1)} %collective-permute-done.4.b_ref), custom_call_target="tpu_custom_call" | custom-call | flops 226492 | tf_op jit(solution)/shard_map/pallas_call | solution.py:212
  14.5 0.3 %shard_map.61 = (f32[384,128]{1,0:T(8,128)S(1)}, f32[8,128]{1,0:T(8,128)S(1)}) custom-call(f32[10,128]{1,0:T(8,128)S(1)} %get-tuple-element.31.mask_ref, f32[384,128]{1,0:T(8,128)S(1)} %shard_map.60.running_ref, bf16[768,384]{1,0:T(8,128)(2,1)S(1)} %get-tuple-element.40.high_ref, bf16[768,384]{1,0:T(8,128)(2,1)S(1)} %get-tuple-element.41.low_ref, ...), custom_call_target="tpu_custom_call" | custom-call | flops 113246 | tf_op jit(solution)/shard_map/pallas_call | solution.py:212
  14.8 1.6 %collective-permute-done.5.b_ref = f32[256,128]{1,0:T(8,128)S(1)} collective-permute-done((f32[256,128]{1,0:T(8,128)S(1)}, f32[256,128]{1,0:T(8,128)S(1)}, u32[]{:S(2)}, u32[]{:S(2)}) %collective-permute-start.5) | collective-permute-done | bytes 131104 | tf_op jit(solution)/shard_map/ppermute | solution.py:235
  16.4 0.4 %shard_map.62.running_ref = f32[768,128]{1,0:T(8,128)S(1)} custom-call(f32[768,128]{1,0:T(8,128)S(1)} %shard_map.59.running_ref, bf16[768,384]{1,0:T(8,128)(2,1)S(1)} %get-tuple-element.40.high_ref, bf16[768,384]{1,0:T(8,128)(2,1)S(1)} %get-tuple-element.41.low_ref, f32[256,128]{1,0:T(8,128)S(1)} %collective-permute-done.5.b_ref), custom_call_target="tpu_custom_call" | custom-call | flops 226492 | tf_op jit(solution)/shard_map/pallas_call | solution.py:212
  16.8 1.0 %collective-permute-done.7.b_ref = f32[128,128]{1,0:T(8,128)S(1)} collective-permute-done((f32[128,128]{1,0:T(8,128)S(1)}, f32[128,128]{1,0:T(8,128)S(1)}, u32[]{:S(2)}, u32[]{:S(2)}) %collective-permute-start.7) | collective-permute-done | bytes 65568 | tf_op jit(solution)/shard_map/ppermute | solution.py:235
  17.9 0.3 shard_map.63
  18.1 0.2 collective-permute-start.12
  18.3 0.4 %collective-permute-start.8 = (f32[1,128]{1,0:T(1,128)S(1)}, f32[1,128]{1,0:T(1,128)S(1)}, u32[]{:S(2)}, u32[]{:S(2)}) collective-permute-start(f32[1,128]{1,0:T(1,128)S(1)} %get-tuple-element.49), channel_id=1, source_target_pairs={{0,4},{1,5},{2,6},{3,7},{4,0},{5,1},{6,2},{7,3},{8,12},{9,13},{10,... | collective-permute-start | bytes 1544 | tf_op jit(solution)/shard_map/ppermute | solution.py:334
  18.7 0.9 %collective-permute-done.8 = f32[1,128]{1,0:T(1,128)S(1)} collective-permute-done((f32[1,128]{1,0:T(1,128)S(1)}, f32[1,128]{1,0:T(1,128)S(1)}, u32[]{:S(2)}, u32[]{:S(2)}) %collective-permute-start.8) | collective-permute-done | bytes 544 | tf_op jit(solution)/shard_map/ppermute | solution.py:334
  19.6 1.4 %collective-permute-start.9 = (f32[1,128]{1,0:T(1,128)S(1)}, f32[1,128]{1,0:T(1,128)S(1)}, u32[]{:S(2)}, u32[]{:S(2)}) collective-permute-start(f32[1,128]{1,0:T(1,128)S(1)} %add.9), channel_id=1, source_target_pairs={{0,12},{1,13},{2,14},{3,15},{4,8},{5,9},{6,10},{7,11},{8,4},{9,5},... | collective-permute-start | bytes 1544 | tf_op jit(solution)/shard_map/ppermute | solution.py:334
  21.0 1.6 %collective-permute-done.9 = f32[1,128]{1,0:T(1,128)S(1)} collective-permute-done((f32[1,128]{1,0:T(1,128)S(1)}, f32[1,128]{1,0:T(1,128)S(1)}, u32[]{:S(2)}, u32[]{:S(2)}) %collective-permute-start.9) | collective-permute-done | bytes 544 | tf_op jit(solution)/shard_map/ppermute | solution.py:334
  22.6 1.5 %collective-permute-start.10 = (f32[1,128]{1,0:T(1,128)S(1)}, f32[1,128]{1,0:T(1,128)S(1)}, u32[]{:S(2)}, u32[]{:S(2)}) collective-permute-start(f32[1,128]{1,0:T(1,128)S(1)} %add.10), channel_id=1, source_target_pairs={{0,5},{1,4},{2,7},{3,6},{4,1},{5,0},{6,3},{7,2},{8,13},{9,12},{10,... | collective-permute-start | bytes 1544 | tf_op jit(solution)/shard_map/ppermute | solution.py:334
  24.1 1.4 %collective-permute-done.10 = f32[1,128]{1,0:T(1,128)S(1)} collective-permute-done((f32[1,128]{1,0:T(1,128)S(1)}, f32[1,128]{1,0:T(1,128)S(1)}, u32[]{:S(2)}, u32[]{:S(2)}) %collective-permute-start.10) | collective-permute-done | bytes 544 | tf_op jit(solution)/shard_map/ppermute | solution.py:334
  25.6 2.5 %collective-permute-start.11 = (f32[1,128]{1,0:T(1,128)S(1)}, f32[1,128]{1,0:T(1,128)S(1)}, u32[]{:S(2)}, u32[]{:S(2)}) collective-permute-start(f32[1,128]{1,0:T(1,128)S(1)} %add.11.one_ref), channel_id=1, source_target_pairs={{0,6},{1,7},{2,4},{3,5},{4,2},{5,3},{6,0},{7,1},{8,14},{9,15},{10,... | collective-permute-start | bytes 1544 | tf_op jit(solution)/shard_map/ppermute | solution.py:334
  28.1 1.3 %collective-permute-done.11.two_ref = f32[1,128]{1,0:T(1,128)S(1)} collective-permute-done((f32[1,128]{1,0:T(1,128)S(1)}, f32[1,128]{1,0:T(1,128)S(1)}, u32[]{:S(2)}, u32[]{:S(2)}) %collective-permute-start.11) | collective-permute-done | bytes 544 | tf_op jit(solution)/shard_map/ppermute | solution.py:334
  29.5 1.0 %shard_map.64 = f32[384,384]{1,0:T(8,128)} custom-call(f32[10,128]{1,0:T(8,128)S(1)} %get-tuple-element.31.mask_ref, f32[1,128]{1,0:T(1,128)S(1)} %add.11.one_ref, f32[1,128]{1,0:T(1,128)S(1)} %collective-permute-done.11.two_ref, f32[384,128]{1,0:T(8,128)S(1)} %get-tuple-element.50.keep_ref, f32[384,128]{1,0:T(8,128)S(1)} %collective-permute-done.12.take_ref, ...), custom_call_target="tpu_custom_call" | custom-call | tf_op jit(solution)/shard_map/pallas_call | solution.py:212
  (8 shorter events, 0.0 us)
Async XLA Ops:
  0.9 5.6 %collective-permute-start.2 = (f32[4,6,128,128]{3,2,1,0:T(8,128)}, f32[4,6,128,128]{3,2,1,0:T(8,128)S(1)}, u32[]{:S(2)}, u32[]{:S(2)}) collective-permute-start(f32[4,6,128,128]{3,2,1,0:T(8,128)} %bitcast.4), channel_id=1, source_target_pairs={{0,4},{4,0},{8,12},{12,8},{1,5},{5,1},{9,13},{13,9},{2,6},{6,2},{1... | collective-permute-start | bytes 4718600 | tf_op jit(solution)/shard_map/ppermute | solution.py:235
  1.5 10.9 %collective-permute-start.3 = (f32[384,384]{1,0:T(8,128)}, f32[384,384]{1,0:T(8,128)S(1)}, u32[]{:S(2)}, u32[]{:S(2)}) collective-permute-start(f32[384,384]{1,0:T(8,128)} %b_ref.1), channel_id=1, source_target_pairs={{0,4},{4,0},{8,12},{12,8},{1,5},{5,1},{9,13},{13,9},{2,6},{6,2},{1... | collective-permute-start | bytes 1769480 | tf_op jit(solution)/shard_map/ppermute | solution.py:235
  1.5 8.2 %collective-permute-start = (f32[384,128]{1,0:T(8,128)S(1)}, f32[384,128]{1,0:T(8,128)S(1)}, u32[]{:S(2)}, u32[]{:S(2)}) collective-permute-start(f32[384,128]{1,0:T(8,128)S(1)} %slice.3.refs_1_), channel_id=1, source_target_pairs={{0,8},{4,12},{8,0},{12,4},{1,9},{5,13},{9,1},{13,5},{2,10},{6,14},... | collective-permute-start | bytes 589832 | tf_op jit(solution)/shard_map/ppermute | solution.py:235
  5.3 1.3 %collective-permute-start.1 = (f32[8,128]{1,0:T(8,128)S(1)}, f32[8,128]{1,0:T(8,128)S(1)}, u32[]{:S(2)}, u32[]{:S(2)}) collective-permute-start(f32[8,128]{1,0:T(8,128)S(1)} %shard_map.55), channel_id=1, source_target_pairs={{0,4},{4,0},{8,12},{12,8},{1,5},{5,1},{9,13},{13,9},{2,6},{6,2},{1... | collective-permute-start | bytes 12296 | tf_op jit(solution)/shard_map/ppermute | solution.py:235
  6.4 7.6 %collective-permute-start.4 = (f32[384,128]{1,0:T(8,128)S(1)}, f32[384,128]{1,0:T(8,128)S(1)}, u32[]{:S(2)}, u32[]{:S(2)}) collective-permute-start(f32[384,128]{1,0:T(8,128)S(1)} %get-tuple-element.36.refs_0_), channel_id=1, source_target_pairs={{0,8},{4,12},{8,0},{12,4},{1,9},{5,13},{9,1},{13,5},{2,10},{6,14},... | collective-permute-start | bytes 589832 | tf_op jit(solution)/shard_map/ppermute | solution.py:235
  9.7 4.7 %collective-permute-start.6 = (f32[384,128]{1,0:T(8,128)S(1)}, f32[384,128]{1,0:T(8,128)S(1)}, u32[]{:S(2)}, u32[]{:S(2)}) collective-permute-start(f32[384,128]{1,0:T(8,128)S(1)} %collective-permute-done.b_ref), channel_id=1, source_target_pairs={{0,4},{4,0},{8,12},{12,8},{1,5},{5,1},{9,13},{13,9},{2,6},{6,2},{1... | collective-permute-start | bytes 589832 | tf_op jit(solution)/shard_map/ppermute | solution.py:235
  9.7 6.7 %collective-permute-start.5 = (f32[256,128]{1,0:T(8,128)S(1)}, f32[256,128]{1,0:T(8,128)S(1)}, u32[]{:S(2)}, u32[]{:S(2)}) collective-permute-start(f32[256,128]{1,0:T(8,128)S(1)} %get-tuple-element.42), channel_id=1, source_target_pairs={{0,12},{4,8},{8,4},{12,0},{1,13},{5,9},{9,5},{13,1},{2,14},{6,10},... | collective-permute-start | bytes 393224 | tf_op jit(solution)/shard_map/ppermute | solution.py:235
  12.3 5.5 %collective-permute-start.7 = (f32[128,128]{1,0:T(8,128)S(1)}, f32[128,128]{1,0:T(8,128)S(1)}, u32[]{:S(2)}, u32[]{:S(2)}) collective-permute-start(f32[128,128]{1,0:T(8,128)S(1)} %get-tuple-element.47), channel_id=1, source_target_pairs={{0,12},{4,8},{8,4},{12,0},{1,13},{5,9},{9,5},{13,1},{2,14},{6,10},... | collective-permute-start | bytes 196616 | tf_op jit(solution)/shard_map/ppermute | solution.py:235
  18.1 11.3 %collective-permute-start.12 = (f32[384,128]{1,0:T(8,128)S(1)}, f32[384,128]{1,0:T(8,128)S(1)}, u32[]{:S(2)}, u32[]{:S(2)}) collective-permute-start(f32[384,128]{1,0:T(8,128)S(1)} %get-tuple-element.51), channel_id=1, source_target_pairs={{0,4},{4,0},{8,12},{12,8},{1,5},{5,1},{9,13},{13,9},{2,6},{6,2},{1... | collective-permute-start | bytes 589832 | tf_op jit(solution)/shard_map/ppermute | solution.py:235
  18.3 1.3 %collective-permute-start.8 = (f32[1,128]{1,0:T(1,128)S(1)}, f32[1,128]{1,0:T(1,128)S(1)}, u32[]{:S(2)}, u32[]{:S(2)}) collective-permute-start(f32[1,128]{1,0:T(1,128)S(1)} %get-tuple-element.49), channel_id=1, source_target_pairs={{0,4},{1,5},{2,6},{3,7},{4,0},{5,1},{6,2},{7,3},{8,12},{9,13},{10,... | collective-permute-start | bytes 1544 | tf_op jit(solution)/shard_map/ppermute | solution.py:334
  19.6 3.0 %collective-permute-start.9 = (f32[1,128]{1,0:T(1,128)S(1)}, f32[1,128]{1,0:T(1,128)S(1)}, u32[]{:S(2)}, u32[]{:S(2)}) collective-permute-start(f32[1,128]{1,0:T(1,128)S(1)} %add.9), channel_id=1, source_target_pairs={{0,12},{1,13},{2,14},{3,15},{4,8},{5,9},{6,10},{7,11},{8,4},{9,5},... | collective-permute-start | bytes 1544 | tf_op jit(solution)/shard_map/ppermute | solution.py:334
  22.6 3.0 %collective-permute-start.10 = (f32[1,128]{1,0:T(1,128)S(1)}, f32[1,128]{1,0:T(1,128)S(1)}, u32[]{:S(2)}, u32[]{:S(2)}) collective-permute-start(f32[1,128]{1,0:T(1,128)S(1)} %add.10), channel_id=1, source_target_pairs={{0,5},{1,4},{2,7},{3,6},{4,1},{5,0},{6,3},{7,2},{8,13},{9,12},{10,... | collective-permute-start | bytes 1544 | tf_op jit(solution)/shard_map/ppermute | solution.py:334
  25.6 3.9 %collective-permute-start.11 = (f32[1,128]{1,0:T(1,128)S(1)}, f32[1,128]{1,0:T(1,128)S(1)}, u32[]{:S(2)}, u32[]{:S(2)}) collective-permute-start(f32[1,128]{1,0:T(1,128)S(1)} %add.11.one_ref), channel_id=1, source_target_pairs={{0,6},{1,7},{2,4},{3,5},{4,2},{5,3},{6,0},{7,1},{8,14},{9,15},{10,... | collective-permute-start | bytes 1544 | tf_op jit(solution)/shard_map/ppermute | solution.py:334

commit v6 on v5

--- a/solution.py
+++ b/solution.py
@@ -141,7 +141,21 @@
     write(at, core.astype(jnp.float32))
 
 
-def start_sum(mask_ref, own_high, own_low, near_high, near_low, near_b, *refs):
+def halves(b_ref, high_ref, low_ref):
+    high_ref[...], low_ref[...] = split(b_ref[...])
+
+
+def only_product(high_ref, low_ref, high_b_ref, low_b_ref, out_ref):
+    rows, width = out_ref.shape
+    left = jnp.concatenate([high_ref[:rows], low_ref[:rows]], axis=1)
+    both = jnp.concatenate([high_b_ref[...], low_b_ref[...]], axis=1)
+    right = jnp.concatenate([both, both], axis=0)
+    result = jnp.dot(left, right, preferred_element_type=jnp.float32)
+    out_ref[...] = result[:, :width] + result[:, width:]
+
+
+def start_sum(odd, mask_ref, own_high, own_low, near_high, near_low, near_b, *refs):
+    before, refs = refs[:odd], refs[odd:]
     pieces, outs = refs[: len(refs) // 2], refs[len(refs) // 2 :]
     height, width = pieces[0].shape
     core = mask_ref[mask_ref.shape[0] - 1, 0:1].reshape(1, 1)
@@ -152,6 +166,8 @@
         out_ref[...] = product(own_high[:rows], own_low[:rows], own_b[...]) + product(
             near_high[:rows], near_low[:rows], piece
         )
+    for first_ref in before:
+        outs[1][...] += first_ref[...]
 
 
 def add_sum(first, running_ref, high_ref, low_ref, b_ref, out_ref):
@@ -259,6 +275,11 @@
     near_b = move(b_panel, 0, 1)
     packed = call(functools.partial(pack, size), 0, shape(8, size), "sss", rows, cols, pattern)
     near_ids = move(packed, 0, 1)
+    forwards, parts = [], []
+    for far_mid in far_mids[0]:
+        forwards = [move(far_mid, 0, 1)]
+        parts = call(halves, 9200000000000, [shape(height, size, dtype=jnp.bfloat16)] * 2, "v", far_mid)
+        near_ids, near_blocks, parts = lax.optimization_barrier((near_ids, near_blocks, parts))
     mask, *dense = call(
         functools.partial(prepare, (half, odd)),
         0,
@@ -276,14 +297,18 @@
     )
     flops = 6 * height * height * size
     wide = shape(2 * height, half * size)
+    firsts = [call(only_product, 0, middle, "vvvv", *dense[4:6], *parts)]  if odd else []
+    if odd:
+        near_b, firsts = lax.optimization_barrier((near_b, firsts))
     running, *mid_running = call(
-        start_sum,
+        functools.partial(start_sum, odd),
         4 * flops * half + 2 * flops * odd,
         [wide] + [middle] * odd,
-        "vvvvvvv" + "v" * odd,
+        "vvvvvvv" + "v" * (2 * odd),
         mask,
         *dense[0:4],
         near_b,
+        *firsts,
         side,
         *mids,
     )
@@ -291,9 +316,12 @@
     for at, step in enumerate(steps):
         same, cross = dense[4 * step : 4 * step + 2], dense[4 * step + 2 : 4 * step + 4]
         for far_mid in far_mids[at]:
-            far_mid, mask = lax.optimization_barrier((far_mid, mask))
-            forward = move(far_mid, 0, 1)
-            mid_running = [call(functools.partial(add_sum, 0), flops, middle, "vvvv", *mid_running, *same, far_mid)]
+            if step == 1:
+                forward = forwards[0]
+            else:
+                far_mid, mask = lax.optimization_barrier((far_mid, mask))
+                forward = move(far_mid, 0, 1)
+                mid_running = [call(functools.partial(add_sum, 0), flops, middle, "vvvv", *mid_running, *same, far_mid)]
             if step < chips - 1:
                 mid_running = [call(functools.partial(add_sum, 0), flops, middle, "vvvv", *mid_running, *cross, forward)]
             else:
@@ -308,7 +336,8 @@
                     forward,
                 )
                 before = [squares]
-        running = call(functools.partial(add_sum, 0), 2 * flops * half, wide, "vvvv", running, *same, far_sides[at])
+        far_side, before = lax.optimization_barrier((far_sides[at], before))
+        running = call(functools.partial(add_sum, 0), 2 * flops * half, wide, "vvvv", running, *same, far_side)
         far_other, before = lax.optimization_barrier((far_others[at], before))
         running = call(functools.partial(add_sum, 0), 2 * flops * half, wide, "vvvv", running, *cross, far_other)
         if step < chips - 1:

time: 30.7 us -> 30.5 us (level)
  waiting for transfers between devices: 8.69 us -> 6.66 us
  starting transfers between devices: 12.4 us -> 14.1 us
    ppermute x9, waiting for transfers between devices: 3.41 us -> 1.83 us  [move(): return lax.ppermute(value, 'blk', pairs)]
    ppermute x9, starting transfers between devices: 6.51 us -> 7.77 us  [move(): return lax.ppermute(value, 'blk', pairs)]
    ppermute x4, starting transfers between devices: 5.85 us -> 6.3 us  [swap(): return lax.ppermute(value, ('blk', 'col'), pairs)]
    ppermute x4, waiting for transfers between devices: 5.27 us -> 4.83 us  [swap(): return lax.ppermute(value, ('blk', 'col'), pairs)]
    pallas_call x10 -> x11, Pallas kernels: 8.33 us -> 8.44 us  [call(): pl.pallas_call(kernel, out_shape=outs, in_specs=specs, out_specs=jax.tree...]
  transfers between devices with their start and end apart: 13 -> 13, of which waited for: 8 -> 6; matrix products, arithmetic and copies ran while one was open for 0% -> 0% of each run, Pallas kernels for 23% -> 24%
where the time goes in v6:
time: 30.5 us; the launch traced here: 30.2 us
  starting transfers between devices  14.1 us (46%)
  Pallas kernels  8.44 us (28%)
  waiting for transfers between devices  6.66 us (22%)
  local copies, waits for them, and re-layouts  0.94 us (3%)
    pallas_call x11, Pallas kernels, call(): pl.pallas_call(kernel, out_shape=outs, in_specs=specs, out_specs=jax.tree...  8.44 us
    ppermute x9, starting transfers between devices, move(): return lax.ppermute(value, 'blk', pairs)  7.77 us
    ppermute x4, starting transfers between devices, swap(): return lax.ppermute(value, ('blk', 'col'), pairs)  6.3 us
    ppermute x4, waiting for transfers between devices, swap(): return lax.ppermute(value, ('blk', 'col'), pairs)  4.83 us
    ppermute x9, waiting for transfers between devices, move(): return lax.ppermute(value, 'blk', pairs)  1.83 us
    slice x1, local copies, waits for them, and re-layouts, body(): mids = [b_panel[:, half * size:(half + 1) * size]] * odd  0.94 us
  transfers between devices with their start and end apart: 13, of which 6 were waited for; matrix products, arithmetic and copies ran while one was open for 0% of the time, Pallas kernels for 24%

profile of v6, /device:TPU:0, one launch (start us, length us, event | category | flops | bytes accessed | tf_op | source)
XLA Modules:
  0.0 30.2 jit_solution(16264867152075625744)
XLA Ops:
  0.0 0.9 %slice.3.refs_2_ = f32[384,128]{1,0:T(8,128)S(1)} slice(f32[384,384]{1,0:T(8,128)} %b_ref.1), slice={[0:384], [128:256]} | slice | bytes 393216 | tf_op jit(solution)/shard_map/slice | solution.py:256
  0.9 0.5 %collective-permute-start.1 = (f32[4,6,128,128]{3,2,1,0:T(8,128)}, f32[4,6,128,128]{3,2,1,0:T(8,128)S(1)}, u32[]{:S(2)}, u32[]{:S(2)}) collective-permute-start(f32[4,6,128,128]{3,2,1,0:T(8,128)} %bitcast.4), channel_id=1, source_target_pairs={{0,4},{4,0},{8,12},{12,8},{1,5},{5,1},{9,13},{13,9},{2,6},{6,2},{1... | collective-permute-start | bytes 4718600 | tf_op jit(solution)/shard_map/ppermute | solution.py:251
  1.5 2.6 %collective-permute-start.2 = (f32[384,128]{1,0:T(8,128)S(1)}, f32[384,128]{1,0:T(8,128)S(1)}, u32[]{:S(2)}, u32[]{:S(2)}) collective-permute-start(f32[384,128]{1,0:T(8,128)S(1)} %slice.3.refs_2_), channel_id=1, source_target_pairs={{0,8},{4,12},{8,0},{12,4},{1,9},{5,13},{9,1},{13,5},{2,10},{6,14},... | collective-permute-start | bytes 589832 | tf_op jit(solution)/shard_map/ppermute | solution.py:251
  4.0 0.8 %shard_map.55 = f32[8,128]{1,0:T(8,128)S(1)} custom-call(s32[4,6]{1,0:T(4,128)} %bitcast.6, s32[4,6]{1,0:T(4,128)} %bitcast.8, s32[3,3]{1,0:T(4,128)} %pattern_ref.3), custom_call_target="tpu_custom_call" | custom-call | tf_op jit(solution)/shard_map/pallas_call | solution.py:228
  4.8 0.2 collective-permute-start
  5.1 0.3 %collective-permute-start.3 = (f32[384,384]{1,0:T(8,128)}, f32[384,384]{1,0:T(8,128)S(1)}, u32[]{:S(2)}, u32[]{:S(2)}) collective-permute-start(f32[384,384]{1,0:T(8,128)} %b_ref.1), channel_id=1, source_target_pairs={{0,4},{4,0},{8,12},{12,8},{1,5},{5,1},{9,13},{13,9},{2,6},{6,2},{1... | collective-permute-start | bytes 1769480 | tf_op jit(solution)/shard_map/ppermute | solution.py:251
  5.4 1.0 %shard_map.59 = (f32[384,128]{1,0:T(8,128)S(1)}, f32[256,128]{1,0:T(8,128)S(1)}, f32[128,128]{1,0:T(8,128)S(1)}) custom-call(s32[1]{0:T(128)} %bitcast.me_ref, f32[384,384]{1,0:T(8,128)} %b_ref.1), custom_call_target="tpu_custom_call" | custom-call | tf_op jit(solution)/shard_map/pallas_call | solution.py:228
  6.4 0.1 collective-permute-start.4
  6.5 0.0 collective-permute-done.near_ids
  6.5 1.5 %collective-permute-start.6 = (f32[256,128]{1,0:T(8,128)S(1)}, f32[256,128]{1,0:T(8,128)S(1)}, u32[]{:S(2)}, u32[]{:S(2)}) collective-permute-start(f32[256,128]{1,0:T(8,128)S(1)} %get-tuple-element.60), channel_id=1, source_target_pairs={{0,12},{4,8},{8,4},{12,0},{1,13},{5,9},{9,5},{13,1},{2,14},{6,10},... | collective-permute-start | bytes 393224 | tf_op jit(solution)/shard_map/ppermute | solution.py:251
  8.0 1.7 %collective-permute-done.2.b_ref = f32[384,128]{1,0:T(8,128)S(1)} collective-permute-done((f32[384,128]{1,0:T(8,128)S(1)}, f32[384,128]{1,0:T(8,128)S(1)}, u32[]{:S(2)}, u32[]{:S(2)}) %collective-permute-start.2) | collective-permute-done | bytes 196640 | tf_op jit(solution)/shard_map/ppermute | solution.py:251
  9.7 0.8 %collective-permute-start.7 = (f32[128,128]{1,0:T(8,128)S(1)}, f32[128,128]{1,0:T(8,128)S(1)}, u32[]{:S(2)}, u32[]{:S(2)}) collective-permute-start(f32[128,128]{1,0:T(8,128)S(1)} %get-tuple-element.63), channel_id=1, source_target_pairs={{0,12},{4,8},{8,4},{12,0},{1,13},{5,9},{9,5},{13,1},{2,14},{6,10},... | collective-permute-start | bytes 196616 | tf_op jit(solution)/shard_map/ppermute | solution.py:251
  10.5 0.0 collective-permute-done.1.near_ref
  10.5 1.3 %collective-permute-start.5 = (f32[384,128]{1,0:T(8,128)S(1)}, f32[384,128]{1,0:T(8,128)S(1)}, u32[]{:S(2)}, u32[]{:S(2)}) collective-permute-start(f32[384,128]{1,0:T(8,128)S(1)} %collective-permute-done.2.b_ref), channel_id=1, source_target_pairs={{0,4},{4,0},{8,12},{12,8},{1,5},{5,1},{9,13},{13,9},{2,6},{6,2},{1... | collective-permute-start | bytes 589832 | tf_op jit(solution)/shard_map/ppermute | solution.py:251
  11.9 2.7 %shard_map.57 = (f32[10,128]{1,0:T(8,128)S(1)}, bf16[768,384]{1,0:T(8,128)(2,1)S(1)}, bf16[768,384]{1,0:T(8,128)(2,1)S(1)}, bf16[768,384]{1,0:T(8,128)(2,1)S(1)}...) custom-call(s32[1]{0:T(128)} %bitcast.me_ref, ...), custom_call_target="tpu_custom_call" | custom-call | tf_op jit(solution)/shard_map/pallas_call | solution.py:228
  14.6 0.3 %shard_map.58.refs_0_ = f32[384,128]{1,0:T(8,128)S(1)} custom-call(bf16[768,384]{1,0:T(8,128)(2,1)S(1)} %get-tuple-element.47.high_ref, bf16[768,384]{1,0:T(8,128)(2,1)S(1)} %get-tuple-element.48.low_ref, bf16[384,128]{1,0:T(8,128)(2,1)S(1)} %get-tuple-element.49.high_b_ref, bf16[384,128]{1,0:T(8,128)(2,1)S(1)} %get-tuple-element.50.low_b_ref), custom_call_target="tpu_custom_call" | custom-call | tf_op jit(solution)/shard_map/pallas_call | solution.py:228
  14.9 1.1 %shard_map.60 = (f32[768,128]{1,0:T(8,128)S(1)}, f32[384,128]{1,0:T(8,128)S(1)}) custom-call(f32[10,128]{1,0:T(8,128)S(1)} %get-tuple-element.42.mask_ref, bf16[768,384]{1,0:T(8,128)(2,1)S(1)} %get-tuple-element.43.own_high, bf16[768,384]{1,0:T(8,128)(2,1)S(1)} %get-tuple-element.44.own_low, bf16[768,384]{1,0:T(8,128)(2,1)S(1)} %get-tuple-element.45.near_high, ...), custom_call_target="tpu_custom_call" | custom-call | flops 679477 | tf_op jit(solution)/shard_map/pallas_call | solution.py:228
  16.1 0.3 %shard_map.61 = (f32[384,128]{1,0:T(8,128)S(1)}, f32[8,128]{1,0:T(8,128)S(1)}) custom-call(f32[10,128]{1,0:T(8,128)S(1)} %get-tuple-element.42.mask_ref, f32[384,128]{1,0:T(8,128)S(1)} %get-tuple-element.55.running_ref, bf16[768,384]{1,0:T(8,128)(2,1)S(1)} %get-tuple-element.56.high_ref, bf16[768,384]{1,0:T(8,128)(2,1)S(1)} %get-tuple-element.57.low_ref, ...), custom_call_target="tpu_custom_call" | custom-call | flops 113246 | tf_op jit(solution)/shard_map/pallas_call | solution.py:228
  16.4 0.5 %shard_map.62.running_ref = f32[768,128]{1,0:T(8,128)S(1)} custom-call(f32[768,128]{1,0:T(8,128)S(1)} %get-tuple-element.54.running_ref, bf16[768,384]{1,0:T(8,128)(2,1)S(1)} %get-tuple-element.47.high_ref, bf16[768,384]{1,0:T(8,128)(2,1)S(1)} %get-tuple-element.48.low_ref, f32[384,128]{1,0:T(8,128)S(1)} %collective-permute-done.4.b_ref), custom_call_target="tpu_custom_call" | custom-call | flops 226492 | tf_op jit(solution)/shard_map/pallas_call | solution.py:228
  16.9 0.4 %shard_map.63.running_ref = f32[768,128]{1,0:T(8,128)S(1)} custom-call(f32[768,128]{1,0:T(8,128)S(1)} %shard_map.62.running_ref, bf16[768,384]{1,0:T(8,128)(2,1)S(1)} %get-tuple-element.56.high_ref, bf16[768,384]{1,0:T(8,128)(2,1)S(1)} %get-tuple-element.57.low_ref, f32[256,128]{1,0:T(8,128)S(1)} %collective-permute-done.6.b_ref), custom_call_target="tpu_custom_call" | custom-call | flops 226492 | tf_op jit(solution)/shard_map/pallas_call | solution.py:228
  17.3 0.1 collective-permute-done.7.b_ref
  17.4 0.3 shard_map.64
  17.7 0.4 %collective-permute-start.12 = (f32[384,128]{1,0:T(8,128)S(1)}, f32[384,128]{1,0:T(8,128)S(1)}, u32[]{:S(2)}, u32[]{:S(2)}) collective-permute-start(f32[384,128]{1,0:T(8,128)S(1)} %get-tuple-element.67), channel_id=1, source_target_pairs={{0,4},{4,0},{8,12},{12,8},{1,5},{5,1},{9,13},{13,9},{2,6},{6,2},{1... | collective-permute-start | bytes 589832 | tf_op jit(solution)/shard_map/ppermute | solution.py:251
  18.1 0.2 collective-permute-start.8
  18.3 0.9 %collective-permute-done.8 = f32[1,128]{1,0:T(1,128)S(1)} collective-permute-done((f32[1,128]{1,0:T(1,128)S(1)}, f32[1,128]{1,0:T(1,128)S(1)}, u32[]{:S(2)}, u32[]{:S(2)}) %collective-permute-start.8) | collective-permute-done | bytes 544 | tf_op jit(solution)/shard_map/ppermute | solution.py:363
  19.2 1.7 %collective-permute-start.9 = (f32[1,128]{1,0:T(1,128)S(1)}, f32[1,128]{1,0:T(1,128)S(1)}, u32[]{:S(2)}, u32[]{:S(2)}) collective-permute-start(f32[1,128]{1,0:T(1,128)S(1)} %add.9), channel_id=1, source_target_pairs={{0,12},{1,13},{2,14},{3,15},{4,8},{5,9},{6,10},{7,11},{8,4},{9,5},... | collective-permute-start | bytes 1544 | tf_op jit(solution)/shard_map/ppermute | solution.py:363
  20.9 1.3 %collective-permute-done.9 = f32[1,128]{1,0:T(1,128)S(1)} collective-permute-done((f32[1,128]{1,0:T(1,128)S(1)}, f32[1,128]{1,0:T(1,128)S(1)}, u32[]{:S(2)}, u32[]{:S(2)}) %collective-permute-start.9) | collective-permute-done | bytes 544 | tf_op jit(solution)/shard_map/ppermute | solution.py:363
  22.2 1.8 %collective-permute-start.10 = (f32[1,128]{1,0:T(1,128)S(1)}, f32[1,128]{1,0:T(1,128)S(1)}, u32[]{:S(2)}, u32[]{:S(2)}) collective-permute-start(f32[1,128]{1,0:T(1,128)S(1)} %add.10), channel_id=1, source_target_pairs={{0,5},{1,4},{2,7},{3,6},{4,1},{5,0},{6,3},{7,2},{8,13},{9,12},{10,... | collective-permute-start | bytes 1544 | tf_op jit(solution)/shard_map/ppermute | solution.py:363
  24.0 1.3 %collective-permute-done.10 = f32[1,128]{1,0:T(1,128)S(1)} collective-permute-done((f32[1,128]{1,0:T(1,128)S(1)}, f32[1,128]{1,0:T(1,128)S(1)}, u32[]{:S(2)}, u32[]{:S(2)}) %collective-permute-start.10) | collective-permute-done | bytes 544 | tf_op jit(solution)/shard_map/ppermute | solution.py:363
  25.3 2.7 %collective-permute-start.11 = (f32[1,128]{1,0:T(1,128)S(1)}, f32[1,128]{1,0:T(1,128)S(1)}, u32[]{:S(2)}, u32[]{:S(2)}) collective-permute-start(f32[1,128]{1,0:T(1,128)S(1)} %add.11.one_ref), channel_id=1, source_target_pairs={{0,6},{1,7},{2,4},{3,5},{4,2},{5,3},{6,0},{7,1},{8,14},{9,15},{10,... | collective-permute-start | bytes 1544 | tf_op jit(solution)/shard_map/ppermute | solution.py:363
  28.0 1.3 %collective-permute-done.11.two_ref = f32[1,128]{1,0:T(1,128)S(1)} collective-permute-done((f32[1,128]{1,0:T(1,128)S(1)}, f32[1,128]{1,0:T(1,128)S(1)}, u32[]{:S(2)}, u32[]{:S(2)}) %collective-permute-start.11) | collective-permute-done | bytes 544 | tf_op jit(solution)/shard_map/ppermute | solution.py:363
  29.3 1.0 %shard_map.65 = f32[384,384]{1,0:T(8,128)} custom-call(f32[10,128]{1,0:T(8,128)S(1)} %get-tuple-element.42.mask_ref, f32[1,128]{1,0:T(1,128)S(1)} %add.11.one_ref, f32[1,128]{1,0:T(1,128)S(1)} %collective-permute-done.11.two_ref, f32[384,128]{1,0:T(8,128)S(1)} %get-tuple-element.66.keep_ref, f32[384,128]{1,0:T(8,128)S(1)} %collective-permute-done.12.take_ref, ...), custom_call_target="tpu_custom_call" | custom-call | tf_op jit(solution)/shard_map/pallas_call | solution.py:228
  (9 shorter events, 0.0 us)
Async XLA Ops:
  0.9 9.6 %collective-permute-start.1 = (f32[4,6,128,128]{3,2,1,0:T(8,128)}, f32[4,6,128,128]{3,2,1,0:T(8,128)S(1)}, u32[]{:S(2)}, u32[]{:S(2)}) collective-permute-start(f32[4,6,128,128]{3,2,1,0:T(8,128)} %bitcast.4), channel_id=1, source_target_pairs={{0,4},{4,0},{8,12},{12,8},{1,5},{5,1},{9,13},{13,9},{2,6},{6,2},{1... | collective-permute-start | bytes 4718600 | tf_op jit(solution)/shard_map/ppermute | solution.py:251
  1.5 8.2 %collective-permute-start.2 = (f32[384,128]{1,0:T(8,128)S(1)}, f32[384,128]{1,0:T(8,128)S(1)}, u32[]{:S(2)}, u32[]{:S(2)}) collective-permute-start(f32[384,128]{1,0:T(8,128)S(1)} %slice.3.refs_2_), channel_id=1, source_target_pairs={{0,8},{4,12},{8,0},{12,4},{1,9},{5,13},{9,1},{13,5},{2,10},{6,14},... | collective-permute-start | bytes 589832 | tf_op jit(solution)/shard_map/ppermute | solution.py:251
  4.8 1.7 %collective-permute-start = (f32[8,128]{1,0:T(8,128)S(1)}, f32[8,128]{1,0:T(8,128)S(1)}, u32[]{:S(2)}, u32[]{:S(2)}) collective-permute-start(f32[8,128]{1,0:T(8,128)S(1)} %shard_map.55), channel_id=1, source_target_pairs={{0,4},{4,0},{8,12},{12,8},{1,5},{5,1},{9,13},{13,9},{2,6},{6,2},{1... | collective-permute-start | bytes 12296 | tf_op jit(solution)/shard_map/ppermute | solution.py:251
  5.1 9.9 %collective-permute-start.3 = (f32[384,384]{1,0:T(8,128)}, f32[384,384]{1,0:T(8,128)S(1)}, u32[]{:S(2)}, u32[]{:S(2)}) collective-permute-start(f32[384,384]{1,0:T(8,128)} %b_ref.1), channel_id=1, source_target_pairs={{0,4},{4,0},{8,12},{12,8},{1,5},{5,1},{9,13},{13,9},{2,6},{6,2},{1... | collective-permute-start | bytes 1769480 | tf_op jit(solution)/shard_map/ppermute | solution.py:251
  6.4 10.0 %collective-permute-start.4 = (f32[384,128]{1,0:T(8,128)S(1)}, f32[384,128]{1,0:T(8,128)S(1)}, u32[]{:S(2)}, u32[]{:S(2)}) collective-permute-start(f32[384,128]{1,0:T(8,128)S(1)} %get-tuple-element.53.refs_1_), channel_id=1, source_target_pairs={{0,8},{4,12},{8,0},{12,4},{1,9},{5,13},{9,1},{13,5},{2,10},{6,14},... | collective-permute-start | bytes 589832 | tf_op jit(solution)/shard_map/ppermute | solution.py:251
  6.5 10.4 %collective-permute-start.6 = (f32[256,128]{1,0:T(8,128)S(1)}, f32[256,128]{1,0:T(8,128)S(1)}, u32[]{:S(2)}, u32[]{:S(2)}) collective-permute-start(f32[256,128]{1,0:T(8,128)S(1)} %get-tuple-element.60), channel_id=1, source_target_pairs={{0,12},{4,8},{8,4},{12,0},{1,13},{5,9},{9,5},{13,1},{2,14},{6,10},... | collective-permute-start | bytes 393224 | tf_op jit(solution)/shard_map/ppermute | solution.py:251
  9.7 7.7 %collective-permute-start.7 = (f32[128,128]{1,0:T(8,128)S(1)}, f32[128,128]{1,0:T(8,128)S(1)}, u32[]{:S(2)}, u32[]{:S(2)}) collective-permute-start(f32[128,128]{1,0:T(8,128)S(1)} %get-tuple-element.63), channel_id=1, source_target_pairs={{0,12},{4,8},{8,4},{12,0},{1,13},{5,9},{9,5},{13,1},{2,14},{6,10},... | collective-permute-start | bytes 196616 | tf_op jit(solution)/shard_map/ppermute | solution.py:251
  10.5 5.5 %collective-permute-start.5 = (f32[384,128]{1,0:T(8,128)S(1)}, f32[384,128]{1,0:T(8,128)S(1)}, u32[]{:S(2)}, u32[]{:S(2)}) collective-permute-start(f32[384,128]{1,0:T(8,128)S(1)} %collective-permute-done.2.b_ref), channel_id=1, source_target_pairs={{0,4},{4,0},{8,12},{12,8},{1,5},{5,1},{9,13},{13,9},{2,6},{6,2},{1... | collective-permute-start | bytes 589832 | tf_op jit(solution)/shard_map/ppermute | solution.py:251
  17.7 11.6 %collective-permute-start.12 = (f32[384,128]{1,0:T(8,128)S(1)}, f32[384,128]{1,0:T(8,128)S(1)}, u32[]{:S(2)}, u32[]{:S(2)}) collective-permute-start(f32[384,128]{1,0:T(8,128)S(1)} %get-tuple-element.67), channel_id=1, source_target_pairs={{0,4},{4,0},{8,12},{12,8},{1,5},{5,1},{9,13},{13,9},{2,6},{6,2},{1... | collective-permute-start | bytes 589832 | tf_op jit(solution)/shard_map/ppermute | solution.py:251
  18.1 1.1 %collective-permute-start.8 = (f32[1,128]{1,0:T(1,128)S(1)}, f32[1,128]{1,0:T(1,128)S(1)}, u32[]{:S(2)}, u32[]{:S(2)}) collective-permute-start(f32[1,128]{1,0:T(1,128)S(1)} %get-tuple-element.65), channel_id=1, source_target_pairs={{0,4},{1,5},{2,6},{3,7},{4,0},{5,1},{6,2},{7,3},{8,12},{9,13},{10,... | collective-permute-start | bytes 1544 | tf_op jit(solution)/shard_map/ppermute | solution.py:363
  19.2 3.0 %collective-permute-start.9 = (f32[1,128]{1,0:T(1,128)S(1)}, f32[1,128]{1,0:T(1,128)S(1)}, u32[]{:S(2)}, u32[]{:S(2)}) collective-permute-start(f32[1,128]{1,0:T(1,128)S(1)} %add.9), channel_id=1, source_target_pairs={{0,12},{1,13},{2,14},{3,15},{4,8},{5,9},{6,10},{7,11},{8,4},{9,5},... | collective-permute-start | bytes 1544 | tf_op jit(solution)/shard_map/ppermute | solution.py:363
  22.2 3.1 %collective-permute-start.10 = (f32[1,128]{1,0:T(1,128)S(1)}, f32[1,128]{1,0:T(1,128)S(1)}, u32[]{:S(2)}, u32[]{:S(2)}) collective-permute-start(f32[1,128]{1,0:T(1,128)S(1)} %add.10), channel_id=1, source_target_pairs={{0,5},{1,4},{2,7},{3,6},{4,1},{5,0},{6,3},{7,2},{8,13},{9,12},{10,... | collective-permute-start | bytes 1544 | tf_op jit(solution)/shard_map/ppermute | solution.py:363
  25.3 4.0 %collective-permute-start.11 = (f32[1,128]{1,0:T(1,128)S(1)}, f32[1,128]{1,0:T(1,128)S(1)}, u32[]{:S(2)}, u32[]{:S(2)}) collective-permute-start(f32[1,128]{1,0:T(1,128)S(1)} %add.11.one_ref), channel_id=1, source_target_pairs={{0,6},{1,7},{2,4},{3,5},{4,2},{5,3},{6,0},{7,1},{8,14},{9,15},{10,... | collective-permute-start | bytes 1544 | tf_op jit(solution)/shard_map/ppermute | solution.py:363
